TPU v7x, 32 devices: a whole 2x2x4 slice. The times are simulated.
32 devices in a mesh: rep: 2 (over x), dp: 4 (over z), mp: 4 (over y, core).
Axes of the slice: x: 2, y: 2, z: 4, core: 2. Of those that a mesh axis runs over, the one named last changes fastest.
Arguments:
- tokens: bfloat16 [3072, 2048], P(('rep', 'dp', 'mp')), may hold values from -6 to 6
- request_ids: int32 [8, 384], P(('rep', 'dp')), may hold values from 0 to 7, never falling along the last dimension, each value on 1 to 192 neighbouring positions
- cache_entries: bfloat16 [4096, 4096], P(('rep', 'dp', 'mp')), may hold values from -250 to 250, as said below
- cached_lengths: int32 [8, 8], replicated, may hold values from 1 to 256, 512 in all within a row
- traded: int32 [4], P('dp'), may hold values from 0 to 1, as said below
- query_weight: bfloat16 [2048, 2048], P(None, 'mp'), may hold values from -0.125 to 0.125
- key_weight: bfloat16 [2048, 2048], P(None, 'mp'), may hold values from -0.125 to 0.125
- value_weight: bfloat16 [2048, 2048], P(None, 'mp'), may hold values from -0.125 to 0.125
- output_weight: bfloat16 [2048, 2048], P('mp'), may hold values from -0.125 to 0.125
- gate_weight: bfloat16 [2048, 8192], P('dp', 'mp'), may hold values from -0.125 to 0.125
- up_weight: bfloat16 [2048, 8192], P('dp', 'mp'), may hold values from -0.125 to 0.125
- down_weight: bfloat16 [2048, 8192], P('dp', 'mp'), may hold values from -0.0625 to 0.0625
Outputs:
- layer_output: bfloat16 [3072, 2048], P(('rep', 'dp', 'mp'))
Inputs may be any that keep to these rules, and one draw needn't show every extreme that they name: `request_ids`: each group's row never falls; every request 0 to 7 has 1 to 192 new tokens in each group, some request exactly 192. `cached_lengths`: each row sums to 512; its largest entry is 256. `traded`: exactly 2 entries are 1. `cache_entries`: keys are stored already rotated to their positions; rows of cache group g are g * 512 to (g + 1) * 512 - 1, the requests' prefixes in request order.
All inputs are finite; a program needn't handle non-finite values.
Results may differ from a plain program's by a relative error of at most 0.013.
The roundings to bfloat16 on the way count: a program that leaves them out, or rounds other values in their place, can miss the bound.
Values may be sent and summed in bfloat16 or wider, within the bound.
No kernel may reach another device: no remote copies, remote signals or barrier semaphores. Data moves between devices by JAX's collectives and lax.ppermute only.
A program may use at most 128 MiB of HBM per device.

v0:
```python
import math

import jax
import jax.numpy as jnp
from jax import lax
from jax.sharding import PartitionSpec as P

D = 2048
HEADS = 16
HEAD_DIM = 128
TOK_GROUP = 384
CACHE = 512


EPSILON = 1e-05
ROPE_BASE = 10000.0


def swapped(value, axis, apart):
    mask = 2**apart
    pairs = [(source, source ^ mask) for source in range(lax.axis_size(axis))]
    return lax.ppermute(value, axis, pairs)


def layer_norm(rows):
    center = rows - jnp.mean(rows, axis=-1, keepdims=True)
    spread = jnp.mean(center * center, axis=-1, keepdims=True)
    return center * lax.rsqrt(spread + EPSILON)


def request_layout(request_row, length_row, cache_size):
    number = length_row.shape[0]
    labels = jnp.arange(number, dtype=jnp.int32)
    onehot = (request_row[:, None] == labels[None, :]).astype(jnp.int32)
    counts = jnp.sum(onehot, axis=0)
    starts = jnp.cumsum(counts) - counts
    token_place = jnp.arange(request_row.shape[0], dtype=jnp.int32)
    positions = jnp.sum(onehot * (length_row - starts)[None, :], axis=1) + token_place
    bounds = jnp.cumsum(length_row)
    cache_place = jnp.arange(cache_size, dtype=jnp.int32)
    owner = jnp.sum((cache_place[:, None] >= bounds[None, :]).astype(jnp.int32), axis=1)
    return (positions, owner)


def rotate(vectors, positions):
    half = vectors.shape[-1] // 2
    freq = ROPE_BASE ** (-jnp.arange(half, dtype=jnp.float32) / half)
    angle = positions.astype(jnp.float32)[:, None] * freq[None, :]
    cosine = jnp.cos(angle)[:, None, :]
    sine = jnp.sin(angle)[:, None, :]
    first = vectors[..., :half]
    second = vectors[..., half:]
    return jnp.concatenate(
        [first * cosine - second * sine, second * cosine + first * sine], axis=-1
    )


def attend(query, keys_new, values_new, keys_cache, values_cache, request_row, owner):
    scale = 1.0 / math.sqrt(query.shape[-1])
    keys = jnp.concatenate([keys_cache, keys_new], axis=0)
    values = jnp.concatenate([values_cache, values_new], axis=0)
    scores = jnp.einsum("thd,khd->htk", query, keys, preferred_element_type=jnp.float32) * scale
    count = request_row.shape[0]
    place = jnp.arange(count, dtype=jnp.int32)
    same_cache = owner[None, :] == request_row[:, None]
    same_new = (request_row[None, :] == request_row[:, None]) & (place[None, :] <= place[:, None])
    allowed = jnp.concatenate([same_cache, same_new], axis=1)
    scores = jnp.where(allowed[None], scores, -1e30)
    top = jnp.max(scores, axis=-1, keepdims=True)
    raised = jnp.exp(scores - top)
    total = jnp.sum(raised, axis=-1, keepdims=True)
    weights = (raised / total).astype(jnp.bfloat16)
    mixed = jnp.einsum("htk,khd->thd", weights, values, preferred_element_type=jnp.float32)
    return mixed.astype(jnp.bfloat16)


def local(
    tokens,
    request_ids,
    cache_entries,
    cached_lengths,
    traded,
    query_weight,
    key_weight,
    value_weight,
    output_weight,
    gate_weight,
    up_weight,
    down_weight,
):
    tensor_size = lax.axis_size("mp")
    local_heads = HEADS // tensor_size
    replica = lax.axis_index("rep")
    within = lax.axis_index("dp")
    pairs = lax.axis_size("dp")
    group = replica * pairs + within
    moved_here = traded[0] == 1
    source = jnp.where(moved_here, (1 - replica) * pairs + within, group)
    length_row = lax.dynamic_slice_in_dim(cached_lengths, source, 1, 0)[0]
    request_row = request_ids[0]
    partner = swapped(cache_entries, "rep", 0)
    stored = jnp.where(moved_here, partner, cache_entries)
    by_heads = lax.all_to_all(
        stored.reshape(stored.shape[0], 2, D), "mp", split_axis=2, concat_axis=0, tiled=True
    )
    keys_cache = by_heads[:, 0].reshape(CACHE, local_heads, HEAD_DIM)
    values_cache = by_heads[:, 1].reshape(CACHE, local_heads, HEAD_DIM)
    rows_full = lax.all_gather(tokens, "mp", axis=0, tiled=True)
    positions, owner = request_layout(request_row, length_row, CACHE)
    normed = layer_norm(rows_full.astype(jnp.float32)).astype(jnp.bfloat16)
    query = jnp.dot(normed, query_weight, preferred_element_type=jnp.float32).reshape(
        TOK_GROUP, local_heads, HEAD_DIM
    )
    query = rotate(query, positions).astype(jnp.bfloat16)
    keys_new = jnp.dot(normed, key_weight, preferred_element_type=jnp.float32).reshape(
        TOK_GROUP, local_heads, HEAD_DIM
    )
    keys_new = rotate(keys_new, positions).astype(jnp.bfloat16)
    values_new = (
        jnp.dot(normed, value_weight, preferred_element_type=jnp.float32)
        .astype(jnp.bfloat16)
        .reshape(TOK_GROUP, local_heads, HEAD_DIM)
    )
    mixed = attend(query, keys_new, values_new, keys_cache, values_cache, request_row, owner)
    mixed = mixed.reshape(TOK_GROUP, local_heads * HEAD_DIM)
    own_sum = lax.psum_scatter(
        jnp.dot(mixed, output_weight, preferred_element_type=jnp.float32),
        "mp",
        scatter_dimension=0,
        tiled=True,
    )
    state_own = (tokens.astype(jnp.float32) + own_sum).astype(jnp.bfloat16)
    normed_own = layer_norm(state_own.astype(jnp.float32)).astype(jnp.bfloat16)
    normed_two = lax.all_gather(normed_own, "mp", axis=0, tiled=True)

    def add_rows(piece):
        return jnp.dot(normed_two, piece, preferred_element_type=jnp.float32)

    gate = add_rows(lax.all_gather(gate_weight, "dp", axis=0, tiled=True))
    upward = add_rows(lax.all_gather(up_weight, "dp", axis=0, tiled=True))
    activated = (jax.nn.silu(gate) * upward).astype(jnp.bfloat16)
    terms = lax.dot_general(
        activated,
        lax.all_gather(down_weight, "dp", axis=0, tiled=True),
        (((1,), (1,)), ((), ())),
        preferred_element_type=jnp.float32,
    )
    hidden_own = lax.psum_scatter(terms, "mp", scatter_dimension=0, tiled=True)
    return (state_own.astype(jnp.float32) + hidden_own).astype(jnp.bfloat16)


def solution(mesh):
    in_specs = (
        P(("rep", "dp", "mp"), None),
        P(("rep", "dp"), None),
        P(("rep", "dp", "mp"), None),
        P(),
        P("dp"),
        P(None, "mp"),
        P(None, "mp"),
        P(None, "mp"),
        P("mp", None),
        P("dp", "mp"),
        P("dp", "mp"),
        P("dp", "mp"),
    )
    out_specs = P(("rep", "dp", "mp"), None)
    return jax.shard_map(local, mesh=mesh, in_specs=in_specs, out_specs=out_specs, check_vma=False)
```

profile of v0, /device:TPU:0, one launch (start us, length us, event | category | flops | bytes accessed | tf_op | source)
XLA Modules:
  0.0 673.7 jit_solution(5296299036820021018)
XLA Ops:
  8.3 3.0 collective-permute-start
  14.3 20.3 %collective-permute-done = bf16[128,4096]{0,1:T(8,128)(2,1)} collective-permute-done((bf16[128,4096]{0,1:T(8,128)(2,1)S(1)}, bf16[128,4096]{0,1:T(8,128)(2,1)}, u32[]{:S(2)}, u32[]{:S(2)}) %collective-permute-start) | collective-permute-done | bytes 1048608 | tf_op jit(solution)/shard_map/ppermute | solution.py:22
  34.7 9.5 %copy.67 = bf16[128,2,2048]{0,1,2:T(2,128)(2,1)} copy(bf16[128,2,2048]{0,2,1:T(8,128)(2,1)S(1)} %bitcast.29) | data formatting | bytes 2097152 | tf_op jit(solution)/shard_map/reshape | solution.py:104
  44.2 3.5 all-to-all-start
  50.2 12.0 %all-to-all-done = bf16[128,2,2048]{0,1,2:T(2,128)(2,1)S(1)} async-done(((bf16[128,2,2048]{0,1,2:T(2,128)(2,1)}), bf16[128,2,2048]{0,1,2:T(2,128)(2,1)S(1)}, u32[]{:S(2)}, u32[]{:S(2)}) %all-to-all-start) | async-done | bytes 1048608 | tf_op jit(solution)/shard_map/all_to_all | solution.py:103
  67.3 2.0 copy.70
  71.1 2.0 fusion.4
  73.1 3.6 fusion.36
  78.1 4.0 fusion.38
  82.1 2.3 reshape.151
  84.3 3.9 convolution_convert_fusion
  88.2 1.9 copy.78
  90.1 2.3 fusion.42
  93.9 2.7 fusion.44
  97.7 2.7 fusion.45
  100.7 39.6 %reduce-scatter.3.cloned.1.call-done = f32[96,2048]{1,0:T(8,128)} async-done(((f32[384,2048]{1,0:T(8,128)}), f32[96,2048]{1,0:T(8,128)}) %reduce-scatter.3.cloned.1.call-update) | async-done | bytes 786448 | tf_op jit(solution)/shard_map/reduce_scatter | solution.py:126
  144.7 18.0 %all-gather.8.cloned.1.call-done = bf16[384,2048]{1,0:T(8,128)(2,1)} async-done(((bf16[96,2048]{1,0:T(8,128)(2,1)}), bf16[384,2048]{1,0:T(8,128)(2,1)}) %all-gather.8.cloned.1.call-update) | async-done | bytes 1572880 | tf_op jit(solution)/shard_map/all_gather | solution.py:134
  162.7 151.2 %all-gather.10.cloned.1.call-done = bf16[2048,2048]{1,0:T(8,128)(2,1)} async-done(((bf16[512,2048]{1,0:T(8,128)(2,1)}), bf16[2048,2048]{1,0:T(8,128)(2,1)}) %all-gather.10.cloned.1.call-update) | async-done | bytes 8388624 | tf_op jit(solution)/shard_map/all_gather | solution.py:139
  313.8 9.0 %fusion.46 = f32[384,2048]{1,0:T(8,128)} fusion(bf16[384,2048]{1,0:T(8,128)(2,1)} %all-gather.8.cloned.1.call-done, bf16[2048,2048]{1,0:T(8,128)(2,1)} %all-gather.10.cloned.1.call-done), kind=kOutput, calls=%fused_computation.77 | convolution fusion | flops 3221225472 | bytes 13107200 | tf_op jit(solution)/shard_map/dot_general | solution.py:137
  322.9 140.4 %all-gather.12.cloned.1.call-done = bf16[2048,2048]{1,0:T(8,128)(2,1)} async-done(((bf16[512,2048]{1,0:T(8,128)(2,1)}), bf16[2048,2048]{1,0:T(8,128)(2,1)}) %all-gather.12.cloned.1.call-update) | async-done | bytes 8388624 | tf_op jit(solution)/shard_map/all_gather | solution.py:140
  463.2 149.4 %all-gather.14.cloned.1.call-done = bf16[2048,2048]{1,0:T(8,128)(2,1)} async-done(((bf16[512,2048]{1,0:T(8,128)(2,1)}), bf16[2048,2048]{1,0:T(8,128)(2,1)}) %all-gather.14.cloned.1.call-update) | async-done | bytes 8388624 | tf_op jit(solution)/shard_map/all_gather | solution.py:144
  612.6 15.9 %fusion.25 = f32[384,2048]{1,0:T(8,128)} fusion(bf16[2048,2048]{1,0:T(8,128)(2,1)} %all-gather.14.cloned.1.call-done, f32[384,2048]{1,0:T(8,128)} %fusion.46, bf16[384,2048]{1,0:T(8,128)(2,1)} %all-gather.8.cloned.1.call-done, bf16[2048,2048]{1,0:T(8,128)(2,1)} %all-gather.12.cloned.1.call-done), kind=kOutput, calls=%fused_computation.42 | convolution fusion | flops 6447169536 | bytes 24641536 | tf_op jit(solution)/shard_map/dot_general | solution.py:142
  628.5 36.3 %reduce-scatter.5.cloned.1.call-done = f32[96,2048]{1,0:T(8,128)} async-done(((f32[384,2048]{1,0:T(8,128)}), f32[96,2048]{1,0:T(8,128)}) %reduce-scatter.5.cloned.1.call-update) | async-done | bytes 786448 | tf_op jit(solution)/shard_map/reduce_scatter | solution.py:148
  664.9 2.0 fusion.24
  (65 shorter events, 22.0 us)
Async XLA Ops:
  6.5 91.1 %copy-start = (bf16[512,2048]{1,0:T(8,128)(2,1)S(1)}, bf16[512,2048]{1,0:T(8,128)(2,1)}, u32[]{:S(2)}) copy-start(bf16[512,2048]{1,0:T(8,128)(2,1)} %param.20) | copy-start | bytes 6291460
  6.5 62.8 %all-gather.6.cloned.1.call-start = ((), (), s32[]{:S(2)}) async-start(), calls=%async_computation.3 | async-start | bytes 1966080 | tf_op jit(solution)/shard_map/all_gather | solution.py:108
  8.3 26.3 %collective-permute-start = (bf16[128,4096]{0,1:T(8,128)(2,1)S(1)}, bf16[128,4096]{0,1:T(8,128)(2,1)}, u32[]{:S(2)}, u32[]{:S(2)}) collective-permute-start(bf16[128,4096]{0,1:T(8,128)(2,1)S(1)} %copy.65), channel_id=1, source_target_pairs={{0,16},{16,0},{1,17},{17,1},{2,18},{18,2},{3,19},{19,3},{4,20},{20... | collective-permute-start | bytes 3145736 | tf_op jit(solution)/shard_map/ppermute | solution.py:22
  44.2 18.0 %all-to-all-start = ((bf16[128,2,2048]{0,1,2:T(2,128)(2,1)}), bf16[128,2,2048]{0,1,2:T(2,128)(2,1)S(1)}, u32[]{:S(2)}, u32[]{:S(2)}) async-start(bf16[128,2,2048]{0,1,2:T(2,128)(2,1)} %copy.67), calls=%async_computation | async-start | bytes 2097152 | tf_op jit(solution)/shard_map/all_to_all | solution.py:103
  47.7 92.6 %reduce-scatter.3.cloned.1.call-start = ((), (), s32[]{:S(2)}) async-start(), calls=%async_computation.4 | async-start | bytes 3932160 | tf_op jit(solution)/shard_map/reduce_scatter | solution.py:126
  69.3 3.8 copy-start.2
  90.1 2.3 copy-start.4
  90.1 2.3 copy-start.5
  92.9 1.0 copy-start.8
  93.9 2.7 copy-start.6
  93.9 2.7 copy-start.7
  97.7 42.6 %copy-start.3 = (bf16[96,2048]{1,0:T(8,128)(2,1)S(1)}, bf16[96,2048]{1,0:T(8,128)(2,1)}, u32[]{:S(2)}) copy-start(bf16[96,2048]{1,0:T(8,128)(2,1)} %param.12) | copy-start | bytes 1179652
  100.4 62.3 %all-gather.8.cloned.1.call-start = ((), (), s32[]{:S(2)}) async-start(), calls=%async_computation.5 | async-start | bytes 1966080 | tf_op jit(solution)/shard_map/all_gather | solution.py:134
  142.9 171.0 %all-gather.10.cloned.1.call-start = ((), (), s32[]{:S(2)}) async-start(), calls=%async_computation.6 | async-start | bytes 10485760 | tf_op jit(solution)/shard_map/all_gather | solution.py:139
  143.4 319.8 %all-gather.12.cloned.1.call-start = ((), (), s32[]{:S(2)}) async-start(), calls=%async_computation.7 | async-start | bytes 10485760 | tf_op jit(solution)/shard_map/all_gather | solution.py:140
  144.0 468.6 %all-gather.14.cloned.1.call-start = ((), (), s32[]{:S(2)}) async-start(), calls=%async_computation.8 | async-start | bytes 10485760 | tf_op jit(solution)/shard_map/all_gather | solution.py:144
  144.6 520.2 %reduce-scatter.5.cloned.1.call-start = ((), (), s32[]{:S(2)}) async-start(), calls=%async_computation.9 | async-start | bytes 3932160 | tf_op jit(solution)/shard_map/reduce_scatter | solution.py:148
  612.6 54.2 %copy-start.1 = (bf16[512,2048]{1,0:T(8,128)(2,1)S(1)}, bf16[512,2048]{1,0:T(8,128)(2,1)}, u32[]{:S(2)}) copy-start(bf16[512,2048]{1,0:T(8,128)(2,1)} %param.20) | copy-start | bytes 6291460
Sparse Core Ops, SparseCore 0:
  11.5 19.9 all-gather.5
  100.5 39.6 reduce-scatter.2
  143.0 19.6 all-gather.7
  164.2 149.6 all-gather.9
  315.3 147.8 all-gather.11
  464.7 147.8 all-gather.13
  628.7 36.1 reduce-scatter.4
where the time goes:
time: 674 us
  waiting for transfers between devices  569 us (84%)
  matrix products  41 us (6%)
  local copies, waits for them, and re-layouts  26.4 us (4%)
  other arithmetic  16.2 us (2%)
  between operations  14.3 us (2%)
  starting transfers between devices  6.98 us (1%)
    all_gather x1, waiting for transfers between devices, local(): gate = add_rows(lax.all_gather(gate_weight, 'dp', axis=0, tiled=True))  151 us
    all_gather x1, waiting for transfers between devices, local(): lax.all_gather(down_weight, 'dp', axis=0, tiled=True)  149 us
    all_gather x1, waiting for transfers between devices, local(): upward = add_rows(lax.all_gather(up_weight, 'dp', axis=0, tiled=True))  140 us
    reduce_scatter x1, waiting for transfers between devices, local(): lax.psum_scatter(jnp.dot(mixed, output_weight, preferred_element_type=jnp...  39.6 us
    reduce_scatter x1, waiting for transfers between devices, local(): hidden_own = lax.psum_scatter(terms, 'mp', scatter_dimension=0, tiled=True)  36.3 us
    ppermute x1, waiting for transfers between devices, swapped(): return lax.ppermute(value, axis, pairs)  20.3 us
    all_gather x1, waiting for transfers between devices, local(): normed_two = lax.all_gather(normed_own, 'mp', axis=0, tiled=True)  18 us
    dot_general x1, matrix products, local(): lax.dot_general(activated, lax.all_gather(down_weight, 'dp', axis=0, tile...  15.9 us
  transfers between devices with their start and end apart: 9, of which 8 were waited for; matrix products, arithmetic and copies ran while one was open for 5% of the time, Pallas kernels for 0%

commit v1 on v0

v1 whole, which is shorter than its diff:
```python
import math

import jax
import jax.numpy as jnp
from jax import lax
from jax.experimental import pallas as pl
from jax.experimental.pallas import tpu as pltpu
from jax.sharding import PartitionSpec as P

HEAD_DIM = 128
EPSILON = 1e-05
ROPE_BASE = 10000.0
VMEM_LIMIT = 48 * 1024 * 1024
TILE = 256
MASKED = -1e30


def swap(value, axis, mask):
    pairs = [(source, source ^ mask) for source in range(lax.axis_size(axis))]
    return lax.ppermute(value, axis, pairs)


def layer_norm(rows):
    center = rows - jnp.mean(rows, axis=-1, keepdims=True)
    spread = jnp.mean(center * center, axis=-1, keepdims=True)
    return center * lax.rsqrt(spread + EPSILON)


def vmem():
    return pl.BlockSpec(memory_space=pltpu.VMEM)


def smem():
    return pl.BlockSpec(memory_space=pltpu.SMEM)


def anywhere():
    return pl.BlockSpec(memory_space=pl.ANY)


def params():
    return pltpu.CompilerParams(vmem_limit_bytes=VMEM_LIMIT)


def cost(flops, moved, transcendentals=0):
    return pl.CostEstimate(
        flops=flops, bytes_accessed=moved, transcendentals=transcendentals
    )


def project_body(n0, n1, n2, n3, cosine, sine, wq, wk, wv, q_ref, k_ref, v_ref, rows):
    count = n0.shape[0]

    @pl.when(pl.program_id(0) == 0)
    def _():
        for at, part in enumerate((n0, n1, n2, n3)):
            rows[pl.ds(at * count, count), :] = part[...]

    x = rows[...]
    width = wq.shape[1]
    for weight, out, turned in ((wq, q_ref, True), (wk, k_ref, True), (wv, v_ref, False)):
        product = jnp.dot(x, weight[...], preferred_element_type=jnp.float32)
        if not turned:
            out[...] = product.astype(jnp.bfloat16)
            continue
        for at in range(0, width, HEAD_DIM):
            head = product[:, at : at + HEAD_DIM]
            other = pltpu.roll(head, HEAD_DIM // 2, 1)
            out[:, at : at + HEAD_DIM] = (head * cosine[...] + other * sine[...]).astype(
                jnp.bfloat16
            )


def project(parts, cosine, sine, wq, wk, wv):
    count, depth = parts[0].shape
    rows, width = 4 * count, wq.shape[1]
    whole = lambda shape: pl.BlockSpec(shape, lambda i: (0, 0))
    column = pl.BlockSpec((depth, TILE), lambda i: (0, i))
    out = pl.BlockSpec((rows, TILE), lambda i: (0, i))
    shape = jax.ShapeDtypeStruct((rows, width), jnp.bfloat16)
    return pl.pallas_call(
        project_body,
        grid=(width // TILE,),
        in_specs=[whole((count, depth))] * 4 + [whole((rows, HEAD_DIM))] * 2 + [column] * 3,
        out_specs=[out] * 3,
        out_shape=[shape] * 3,
        scratch_shapes=[pltpu.VMEM((rows, depth), jnp.bfloat16)],
        compiler_params=params(),
        cost_estimate=cost(6 * rows * depth * width, 6 * depth * width + 2 * rows * depth),
    )(*parts, cosine, sine, wq, wk, wv)


def attend_body(q, k, v, keep, came, of_row, of_column, wo, near, far, mixed):
    rows = q.shape[0]
    heads = q.shape[1] // HEAD_DIM
    width = q.shape[1]
    cached = of_column.shape[1]
    low, high = of_row[:, 0:1], of_row[:, 1:2]
    first, place = of_row[:, 2:3], of_row[:, 3:4]
    column = of_column[0:1, :]
    fresh = of_column[1:2, :rows]
    on_cached = (column >= low) & (column < high)
    on_fresh = (fresh >= first) & (fresh <= place)
    scale = 1.0 / math.sqrt(HEAD_DIM)
    contract_last = (((1,), (1,)), ((), ()))
    for head in range(heads):
        at = slice(head * HEAD_DIM, (head + 1) * HEAD_DIM)
        after = slice(width + head * HEAD_DIM, width + (head + 1) * HEAD_DIM)
        keys = jnp.concatenate([keep[0, :, at], keep[1, :, at], came[0, :, at], came[1, :, at]])
        values = jnp.concatenate(
            [keep[0, :, after], keep[1, :, after], came[0, :, after], came[1, :, after]]
        )
        query = q[:, at]
        old = lax.dot_general(query, keys, contract_last, preferred_element_type=jnp.float32)
        new = lax.dot_general(query, k[:, at], contract_last, preferred_element_type=jnp.float32)
        old = jnp.where(on_cached, old * scale, MASKED)
        new = jnp.where(on_fresh, new * scale, MASKED)
        top = jnp.maximum(
            jnp.max(old, axis=-1, keepdims=True), jnp.max(new, axis=-1, keepdims=True)
        )
        old = jnp.exp(old - top)
        new = jnp.exp(new - top)
        share = 1.0 / (jnp.sum(old, axis=-1, keepdims=True) + jnp.sum(new, axis=-1, keepdims=True))
        sums = jnp.dot(
            (old * share).astype(jnp.bfloat16), values, preferred_element_type=jnp.float32
        ) + jnp.dot(
            (new * share).astype(jnp.bfloat16), v[:, at], preferred_element_type=jnp.float32
        )
        mixed[:, at] = sums.astype(jnp.bfloat16)
    split_rows(mixed[...], wo, near, far, False)


def split_rows(left, weight, near, far, transposed):
    count = left.shape[0] // 4
    width = near.shape[1]
    for at in range(0, width, TILE):
        if transposed:
            part = sum(
                lax.dot_general(
                    left[:, half * weight.shape[2] : (half + 1) * weight.shape[2]],
                    weight[half, at : at + TILE, :],
                    (((1,), (1,)), ((), ())),
                    preferred_element_type=jnp.float32,
                )
                for half in range(2)
            )
        else:
            part = jnp.dot(left, weight[:, at : at + TILE], preferred_element_type=jnp.float32)
        near[:count, at : at + TILE] = part[:count]
        far[:count, at : at + TILE] = part[count : 2 * count]
        near[count:, at : at + TILE] = part[2 * count : 3 * count]
        far[count:, at : at + TILE] = part[3 * count :]


def attend(q, k, v, keep, came, of_row, of_column, wo):
    rows, width = q.shape
    depth = wo.shape[1]
    shape = jax.ShapeDtypeStruct((rows // 2, depth), jnp.float32)
    cached = of_column.shape[1]
    return pl.pallas_call(
        attend_body,
        in_specs=[vmem()] * 8,
        out_specs=[vmem()] * 2,
        out_shape=[shape] * 2,
        scratch_shapes=[pltpu.VMEM((rows, width), jnp.bfloat16)],
        compiler_params=params(),
        cost_estimate=cost(
            4 * rows * width * (cached + rows) + 2 * rows * width * depth,
            6 * rows * depth,
            rows * (cached + rows) * width // HEAD_DIM,
        ),
    )(q, k, v, keep, came, of_row, of_column, wo)


def gate_up(masks, info, parts, gate, up, mine, other):
    count, depth = parts[0].shape
    rows = 4 * count
    shard, quarter = mine[0].shape[1:]
    pieces = len(mine)

    def body(info_ref, *refs):
        blocks, refs = refs[:4], refs[4:]
        gate_ref, up_ref, refs = refs[0], refs[1], refs[2:]
        sets, refs = (refs[:pieces], refs[pieces : 2 * pieces]), refs[2 * pieces :]
        act_ref, x, held, sems = refs
        own = info_ref[0]
        copies = []
        for half in range(2):
            begin = pl.multiple_of(info_ref[1 + half] * quarter, quarter)
            there = pl.ds(pl.multiple_of(own * shard, shard), shard)
            for which, source in enumerate((gate_ref, up_ref)):
                copies.append(
                    pltpu.make_async_copy(
                        source.at[:, pl.ds(begin, quarter)],
                        held.at[half, which, there, :],
                        sems.at[half, 0, which],
                    )
                )
            for at, mask in enumerate(masks[1:]):
                there = pl.ds(pl.multiple_of((own ^ mask) * shard, shard), shard)
                copies.append(
                    pltpu.make_async_copy(
                        sets[half][at], held.at[half, :, there, :], sems.at[half, at + 1, 0]
                    )
                )
        for copy in copies:
            copy.start()
        for at, block in enumerate(blocks):
            x[pl.ds(at * count, count), :] = block[...]
        for half in range(2):
            for copy in copies[half * (pieces + 2) : (half + 1) * (pieces + 2)]:
                copy.wait()
            for at in range(0, quarter, TILE):
                g = jnp.dot(
                    x[...], held[half, 0, :, at : at + TILE], preferred_element_type=jnp.float32
                )
                u = jnp.dot(
                    x[...], held[half, 1, :, at : at + TILE], preferred_element_type=jnp.float32
                )
                act_ref[:, half * quarter + at : half * quarter + at + TILE] = (
                    g / (1.0 + jnp.exp(-g)) * u
                ).astype(jnp.bfloat16)

    return pl.pallas_call(
        body,
        in_specs=[smem()] + [vmem()] * 4 + [anywhere()] * (2 + 2 * pieces),
        out_specs=vmem(),
        out_shape=jax.ShapeDtypeStruct((rows, 2 * quarter), jnp.bfloat16),
        scratch_shapes=[
            pltpu.VMEM((rows, depth), jnp.bfloat16),
            pltpu.VMEM((2, 2, depth, quarter), jnp.bfloat16),
            pltpu.SemaphoreType.DMA((2, pieces + 1, 2)),
        ],
        compiler_params=params(),
        cost_estimate=cost(8 * rows * depth * quarter, 8 * depth * quarter, 2 * rows * quarter),
    )(info, *parts, gate, up, *mine, *other)


def down_rows(masks, info, act, down, mine, other):
    rows = act.shape[0]
    shard, quarter = mine[0].shape
    pieces = len(mine)
    depth = shard * len(masks)

    def body(info_ref, act_ref, down_ref, *refs):
        sets, refs = (refs[:pieces], refs[pieces : 2 * pieces]), refs[2 * pieces :]
        near, far, held, sems = refs
        own = info_ref[0]
        copies = []
        for half in range(2):
            begin = pl.multiple_of(info_ref[1 + half] * quarter, quarter)
            for at, mask in enumerate(masks):
                there = pl.ds(pl.multiple_of((own ^ mask) * shard, shard), shard)
                source = sets[half][at - 1] if at else down_ref.at[:, pl.ds(begin, quarter)]
                copies.append(
                    pltpu.make_async_copy(source, held.at[half, there, :], sems.at[half, at])
                )
        for copy in copies:
            copy.start()
        for copy in copies:
            copy.wait()
        split_rows(act_ref[...], held, near, far, True)

    shape = jax.ShapeDtypeStruct((rows // 2, depth), jnp.float32)
    return pl.pallas_call(
        body,
        in_specs=[smem(), vmem()] + [anywhere()] * (1 + 2 * pieces),
        out_specs=[vmem()] * 2,
        out_shape=[shape] * 2,
        scratch_shapes=[
            pltpu.VMEM((2, depth, quarter), jnp.bfloat16),
            pltpu.SemaphoreType.DMA((2, pieces + 1)),
        ],
        compiler_params=params(),
        cost_estimate=cost(4 * rows * depth * quarter, 4 * depth * quarter + 4 * rows * depth),
    )(info, act, down, *mine, *other)


def gather_rows(rows):
    across = swap(rows, "mp", 2)
    return [rows, swap(rows, "mp", 1), across, swap(across, "mp", 1)]


def reduce_rows(near, far):
    count = near.shape[0] // 2
    came = swap(far, "mp", 1)
    sent = (near[count:] + came[count:]).astype(jnp.bfloat16)
    return near[:count] + came[:count] + swap(sent, "mp", 2).astype(jnp.float32)


def spread_pieces(own, leaving, pair, bits):
    pieces = {0: own, pair: swap(leaving, "dp", pair)}
    for bit in bits:
        pieces.update({mask ^ bit: swap(piece, "dp", bit) for mask, piece in list(pieces.items())})
    return pieces


def row_facts(request_row, length_row, member, cache_size):
    count = request_row.shape[0]
    number = length_row.shape[0]
    labels = jnp.arange(number, dtype=jnp.int32)
    onehot = (request_row[:, None] == labels[None, :]).astype(jnp.int32)
    counts = jnp.sum(onehot, axis=0)
    below = labels[:, None] < labels[None, :]
    starts = jnp.sum(jnp.where(below, counts[:, None], 0), axis=0)
    begins = jnp.sum(jnp.where(below, length_row[:, None], 0), axis=0)

    def blocks(size, order):
        step = jnp.arange(size // 4, dtype=jnp.int32)
        return jnp.concatenate([(member ^ mask) * (size // 4) + step for mask in order])

    place = blocks(count, (0, 1, 2, 3))
    request = jnp.concatenate(
        [
            lax.dynamic_slice_in_dim(request_row, (member ^ mask) * (count // 4), count // 4, 0)
            for mask in range(4)
        ]
    )
    onehot = (request[:, None] == labels[None, :]).astype(jnp.int32)
    first = jnp.sum(onehot * starts[None, :], axis=1)
    length = jnp.sum(onehot * length_row[None, :], axis=1)
    low = jnp.sum(onehot * begins[None, :], axis=1)
    positions = length + place - first
    of_row = jnp.stack([low, low + length, first, place], axis=1)
    cached = blocks(cache_size, (0, 2, 1, 3))
    of_column = jnp.stack([cached, jnp.pad(place, (0, cache_size - count))])
    return positions, of_row, of_column


def local(
    tokens,
    request_ids,
    cache_entries,
    cached_lengths,
    traded,
    query_weight,
    key_weight,
    value_weight,
    output_weight,
    gate_weight,
    up_weight,
    down_weight,
):
    replica = lax.axis_index("rep")
    within = lax.axis_index("dp")
    member = lax.axis_index("mp")
    planes = lax.axis_size("dp")
    group = replica * planes + within
    moved_here = traded[0] == 1
    source = jnp.where(moved_here, (1 - replica) * planes + within, group)
    length_row = lax.dynamic_slice_in_dim(cached_lengths, source, 1, 0)[0]

    normed = layer_norm(tokens.astype(jnp.float32)).astype(jnp.bfloat16)
    parts = gather_rows(normed)

    held, width = cache_entries.shape
    chip, core = member // 2, member % 2
    entries = cache_entries.reshape(held, 2, 2, 2, width // 8)
    near = lax.dynamic_slice_in_dim(entries, chip, 1, 2)[:, :, 0]
    far = lax.dynamic_slice_in_dim(entries, 1 - chip, 1, 2)[:, :, 0]
    near_came = swap(near, "rep", 1)
    far = swap(far, "mp", 2)
    far_came = swap(far, "rep", 1)
    near = jnp.where(moved_here, near_came, near)
    far = jnp.where(moved_here, far_came, far)

    def of_core(which):
        return jnp.stack(
            [
                lax.dynamic_slice_in_dim(rows, which, 1, 2).reshape(held, width // 4)
                for rows in (near, far)
            ]
        )

    keep = of_core(core)
    came = swap(of_core(1 - core), "mp", 1)

    pair = planes // 2
    bits = [1 << at for at in range(planes.bit_length() - 1) if 1 << at != pair]
    half = (within // pair) % 2
    quarter = gate_weight.shape[1] // 4
    index_mine, index_other = 2 * half + replica, 2 * half + 1 - replica
    index_leaving = 2 * (1 - half) + replica

    def cut(weight, index):
        return lax.dynamic_slice_in_dim(weight, index * quarter, quarter, 1)

    def gate_and_up(index):
        return jnp.stack([cut(gate_weight, index), cut(up_weight, index)])

    wide = spread_pieces(gate_and_up(index_mine), gate_and_up(index_leaving), pair, bits)
    masks = list(wide)
    wide_mine = [wide[mask] for mask in masks[1:]]
    wide_other = [swap(piece, "rep", 1) for piece in wide_mine]
    back = spread_pieces(cut(down_weight, index_mine), cut(down_weight, index_leaving), pair, bits)
    back_mine = [back[mask] for mask in masks[1:]]
    back_other = [swap(piece, "rep", 1) for piece in back_mine]
    info = jnp.stack([within, index_mine, index_other]).astype(jnp.int32)

    positions, of_row, of_column = row_facts(request_ids[0], length_row, member, 4 * held)
    half_dim = HEAD_DIM // 2
    freq = ROPE_BASE ** (-jnp.arange(half_dim, dtype=jnp.float32) / half_dim)
    angle = positions.astype(jnp.float32)[:, None] * freq[None, :]
    cosine, sine = jnp.cos(angle), jnp.sin(angle)
    cosine = jnp.concatenate([cosine, cosine], axis=1)
    sine = jnp.concatenate([-sine, sine], axis=1)
    q, k, v = project(parts, cosine, sine, query_weight, key_weight, value_weight)
    own_sum = reduce_rows(*attend(q, k, v, keep, came, of_row, of_column, output_weight))
    state_own = (tokens.astype(jnp.float32) + own_sum).astype(jnp.bfloat16)
    normed_own = layer_norm(state_own.astype(jnp.float32)).astype(jnp.bfloat16)

    rows_pair = gather_rows(swap(normed_own, "dp", pair))
    rows_own = gather_rows(normed_own)
    act_own = gate_up(masks, info, rows_own, gate_weight, up_weight, wide_mine, wide_other)
    act_pair = gate_up(masks, info, rows_pair, gate_weight, up_weight, wide_mine, wide_other)
    pair_sum = reduce_rows(*down_rows(masks, info, act_pair, down_weight, back_mine, back_other))
    own_sum = reduce_rows(*down_rows(masks, info, act_own, down_weight, back_mine, back_other))
    came_sum = swap(pair_sum.astype(jnp.bfloat16), "dp", pair).astype(jnp.float32)
    return (state_own.astype(jnp.float32) + (own_sum + came_sum)).astype(jnp.bfloat16)


def solution(mesh):
    in_specs = (
        P(("rep", "dp", "mp"), None),
        P(("rep", "dp"), None),
        P(("rep", "dp", "mp"), None),
        P(),
        P("dp"),
        P(None, "mp"),
        P(None, "mp"),
        P(None, "mp"),
        P("mp", None),
        P("dp", "mp"),
        P("dp", "mp"),
        P("dp", "mp"),
    )
    out_specs = P(("rep", "dp", "mp"), None)
    return jax.shard_map(local, mesh=mesh, in_specs=in_specs, out_specs=out_specs, check_vma=False)
```

time: 674 us -> 282 us (0.42)
  waiting for transfers between devices: 569 us -> 176 us
  matrix products: 41 us -> 0 us
  Pallas kernels: 0 us -> 35.9 us
  starting transfers between devices: 6.98 us -> 39.7 us
  between operations: 14.3 us -> 1.21 us
  local copies, waits for them, and re-layouts: 26.4 us -> 14.9 us
    all_gather x5 -> x0, waiting for transfers between devices: 459 us -> none  [the longest x1 151 us: local(): gate = add_rows(lax.all_gather(gate_weight, 'dp', axis=0, tiled=True))]
    ppermute x1 -> x33, waiting for transfers between devices: 20.3 us -> 176 us  [swap(): return lax.ppermute(value, axis, pairs)]
    reduce_scatter x2 -> x0, waiting for transfers between devices: 75.9 us -> none  [the longest x1 39.6 us: local(): lax.psum_scatter(jnp.dot(mixed, output_weight, preferred_element_type=jnp...]
    dot_general x8 -> x0, matrix products: 41 us -> none  [the longest x1 15.9 us: local(): lax.dot_general(activated, lax.all_gather(down_weight, 'dp', axis=0, tile...]
    ppermute x1 -> x33, starting transfers between devices: 3 us -> 39.7 us  [swap(): return lax.ppermute(value, axis, pairs)]
    pallas_call x0 -> x6, Pallas kernels: none -> 35.9 us  [the longest x2 11.9 us: gate_up(): pl.pallas_call(body, in_specs=[smem()] + [vmem()] * 4 + [anywhere()] * (2...]
    reshape x4 -> x1, local copies, waits for them, and re-layouts: 15 us -> 0.79 us  [local(): entries = cache_entries.reshape(held, 2, 2, 2, width // 8)]
    all_to_all x1 -> x0, waiting for transfers between devices: 12 us -> none  [local(): lax.all_to_all(stored.reshape(stored.shape[0], 2, D), 'mp', split_axis=2,...]
  transfers between devices with their start and end apart: 9 -> 33, of which waited for: 8 -> 16; matrix products, arithmetic and copies ran while one was open for 5% -> 7% of each run, Pallas kernels for 0% -> 10%
where the time goes in v1:
time: 282 us; the launch traced here: 281 us
  waiting for transfers between devices  176 us (62%)
  starting transfers between devices  39.7 us (14%)
  Pallas kernels  35.9 us (13%)
  local copies, waits for them, and re-layouts  14.9 us (5%)
  other arithmetic  13.5 us (5%)
    ppermute x33, waiting for transfers between devices, swap(): return lax.ppermute(value, axis, pairs)  176 us
    ppermute x33, starting transfers between devices, swap(): return lax.ppermute(value, axis, pairs)  39.7 us
    pallas_call x2, Pallas kernels, gate_up(): pl.pallas_call(body, in_specs=[smem()] + [vmem()] * 4 + [anywhere()] * (2...  11.9 us
    pallas_call x2, Pallas kernels, down_rows(): pl.pallas_call(body, in_specs=[smem(), vmem()] + [anywhere()] * (1 + 2 *...  11.5 us
    pallas_call x1, Pallas kernels, attend(): pl.pallas_call(attend_body, in_specs=[vmem()] * 8, out_specs=[vmem()] * 2...  7.13 us
  transfers between devices with their start and end apart: 33, of which 16 were waited for; matrix products, arithmetic and copies ran while one was open for 7% of the time, Pallas kernels for 10%

profile of v1, /device:TPU:0, one launch (start us, length us, event | category | flops | bytes accessed | tf_op | source)
XLA Modules:
  0.0 281.1 jit_solution(7199642798966520870)
XLA Ops:
  3.8 3.0 %collective-permute-start.1 = (bf16[96,2048]{1,0:T(8,128)(2,1)S(1)}, bf16[96,2048]{1,0:T(8,128)(2,1)}, u32[]{:S(2)}, u32[]{:S(2)}) collective-permute-start(bf16[96,2048]{1,0:T(8,128)(2,1)S(1)} %fusion.7.n0), channel_id=1, source_target_pairs={{0,2},{1,3},{2,0},{3,1},{4,6},{5,7},{6,4},{7,5},{8,10},{9,11},{10,... | collective-permute-start | bytes 1179656 | tf_op jit(solution)/shard_map/ppermute | solution.py:20
  14.2 13.0 %collective-permute-done.4 = bf16[128,2,2,512]{3,1,0,2:T(2,128)(2,1)S(1)} collective-permute-done((bf16[128,2,2,512]{3,1,0,2:T(2,128)(2,1)S(1)}, bf16[128,2,2,512]{3,1,0,2:T(2,128)(2,1)S(1)}, u32[]{:S(2)}, u32[]{:S(2)}) %collective-permute-start.4) | collective-permute-done | bytes 524320 | tf_op jit(solution)/shard_map/ppermute | solution.py:20
  29.9 10.4 %collective-permute-done.5 = bf16[128,2,2,512]{3,1,0,2:T(2,128)(2,1)S(1)} collective-permute-done((bf16[128,2,2,512]{3,1,0,2:T(2,128)(2,1)S(1)}, bf16[128,2,2,512]{3,1,0,2:T(2,128)(2,1)S(1)}, u32[]{:S(2)}, u32[]{:S(2)}) %collective-permute-start.5) | collective-permute-done | bytes 524320 | tf_op jit(solution)/shard_map/ppermute | solution.py:20
  46.5 5.3 %shard_map.118 = (bf16[384,512]{1,0:T(8,128)(2,1)S(1)}, bf16[384,512]{1,0:T(8,128)(2,1)S(1)}, bf16[384,512]{1,0:T(8,128)(2,1)S(1)}) custom-call(bf16[96,2048]{1,0:T(8,128)(2,1)S(1)} %fusion.7.n0, bf16[96,2048]{1,0:T(8,128)(2,1)} %collective-permute-done.n1, bf16[96,2048]{1,0:T(8,128)(2,1)} %collective-permute-done.1.n2, ...), custom_call_target="tpu_custom_call" | custom-call | flops 2415919104 | bytes 7864320 | tf_op jit(solution)/shard_map/pallas_call | solution.py:81
  56.5 7.1 %shard_map.119 = (f32[192,2048]{1,0:T(8,128)S(1)}, f32[192,2048]{1,0:T(8,128)}) custom-call(bf16[384,512]{1,0:T(8,128)(2,1)S(1)} %copy-done.7, bf16[384,512]{1,0:T(8,128)(2,1)S(1)} %copy-done.9, bf16[384,512]{1,0:T(8,128)(2,1)S(1)} %copy-done.11, bf16[2,128,1024]{2,1,0:T(8,128)(2,1)S(1)} %pad_maximum_fusion.2.keep, ...), custom_call_target="tpu_custom_call" | custom-call | flops 1509949440 | bytes 4718592 | tf_op jit(solution)/shard_map/pallas_call | solution.py:160
  67.1 2.6 collective-permute-start.12
  71.4 44.3 %collective-permute-done.12.refs_6_ = bf16[2,512,512]{2,1,0:T(8,128)(2,1)S(1)} collective-permute-done((bf16[2,512,512]{2,1,0:T(8,128)(2,1)S(1)}, bf16[2,512,512]{2,1,0:T(8,128)(2,1)S(1)}, u32[]{:S(2)}, u32[]{:S(2)}) %collective-permute-start.12) | collective-permute-done | bytes 1048608 | tf_op jit(solution)/shard_map/ppermute | solution.py:20
  120.7 2.0 collective-permute-start.18
  124.2 28.9 %collective-permute-done.14.refs_8_ = bf16[2,512,512]{2,1,0:T(8,128)(2,1)S(1)} collective-permute-done((bf16[2,512,512]{2,1,0:T(8,128)(2,1)S(1)}, bf16[2,512,512]{2,1,0:T(8,128)(2,1)S(1)}, u32[]{:S(2)}, u32[]{:S(2)}) %collective-permute-start.14) | collective-permute-done | bytes 1048608 | tf_op jit(solution)/shard_map/ppermute | solution.py:20
  157.0 5.4 %collective-permute-done.19.refs_1_ = bf16[512,512]{1,0:T(8,128)(2,1)} collective-permute-done((bf16[512,512]{1,0:T(8,128)(2,1)S(1)}, bf16[512,512]{1,0:T(8,128)(2,1)}, u32[]{:S(2)}, u32[]{:S(2)}) %collective-permute-start.19) | collective-permute-done | bytes 524320 | tf_op jit(solution)/shard_map/ppermute | solution.py:20
  162.5 2.2 collective-permute-start.26
  164.6 2.6 collective-permute-start.20
  167.2 14.7 %collective-permute-done.26.refs_0_ = bf16[96,2048]{1,0:T(8,128)(2,1)} collective-permute-done((bf16[96,2048]{1,0:T(8,128)(2,1)S(1)}, bf16[96,2048]{1,0:T(8,128)(2,1)}, u32[]{:S(2)}, u32[]{:S(2)}) %collective-permute-start.26) | collective-permute-done | bytes 393248 | tf_op jit(solution)/shard_map/ppermute | solution.py:20
  186.5 7.8 %collective-permute-done.28.refs_2_ = bf16[96,2048]{1,0:T(8,128)(2,1)} collective-permute-done((bf16[96,2048]{1,0:T(8,128)(2,1)}, bf16[96,2048]{1,0:T(8,128)(2,1)}, u32[]{:S(2)}, u32[]{:S(2)}) %collective-permute-start.28) | collective-permute-done | bytes 393248 | tf_op jit(solution)/shard_map/ppermute | solution.py:20
  202.4 6.3 %shard_map.122.act_ref = bf16[384,1024]{1,0:T(8,128)(2,1)S(1)} custom-call(s32[3]{0:T(128)S(1)} %pad_add_fusion.5.info_ref, bf16[96,2048]{1,0:T(8,128)(2,1)} %collective-permute-done.26.refs_0_, bf16[96,2048]{1,0:T(8,128)(2,1)} %collective-permute-done.27.refs_1_, bf16[96,2048]{1,0:T(8,128)(2,1)} %collective-permute-done.28.refs_2_, ...), custom_call_target="tpu_custom_call" | custom-call | flops 3221225472 | bytes 8388608 | tf_op jit(solution)/shard_map/pallas_call | solution.py:224
  208.8 11.8 %collective-permute-done.22.refs_4_ = bf16[512,512]{1,0:T(8,128)(2,1)} collective-permute-done((bf16[512,512]{1,0:T(8,128)(2,1)}, bf16[512,512]{1,0:T(8,128)(2,1)}, u32[]{:S(2)}, u32[]{:S(2)}) %collective-permute-start.22) | collective-permute-done | bytes 524320 | tf_op jit(solution)/shard_map/ppermute | solution.py:20
  220.6 10.8 %collective-permute-done.23.refs_5_ = bf16[512,512]{1,0:T(8,128)(2,1)} collective-permute-done((bf16[512,512]{1,0:T(8,128)(2,1)}, bf16[512,512]{1,0:T(8,128)(2,1)}, u32[]{:S(2)}, u32[]{:S(2)}) %collective-permute-start.23) | collective-permute-done | bytes 524320 | tf_op jit(solution)/shard_map/ppermute | solution.py:20
  231.4 5.8 %shard_map.123 = (f32[192,2048]{1,0:T(8,128)S(1)}, f32[192,2048]{1,0:T(8,128)}) custom-call(s32[3]{0:T(128)S(1)} %pad_add_fusion.5.info_ref, bf16[384,1024]{1,0:T(8,128)(2,1)S(1)} %shard_map.122.act_ref, bf16[512,2048]{1,0:T(8,128)(2,1)} %down_ref.3, bf16[512,512]{1,0:T(8,128)(2,1)} %collective-permute-done.18.refs_0_, ...), custom_call_target="tpu_custom_call" | custom-call | flops 1610612736 | bytes 7340032 | tf_op jit(solution)/shard_map/pallas_call | solution.py:265
  237.3 5.5 %shard_map.120.act_ref = bf16[384,1024]{1,0:T(8,128)(2,1)S(1)} custom-call(s32[3]{0:T(128)S(1)} %pad_add_fusion.5.info_ref, bf16[96,2048]{1,0:T(8,128)(2,1)S(1)} %fusion.5.refs_0_, bf16[96,2048]{1,0:T(8,128)(2,1)S(1)} %collective-permute-done.9.refs_1_, bf16[96,2048]{1,0:T(8,128)(2,1)S(1)} %copy-done.4, ...), custom_call_target="tpu_custom_call" | custom-call | flops 3221225472 | bytes 8388608 | tf_op jit(solution)/shard_map/pallas_call | solution.py:224
  242.8 5.7 %shard_map.121 = (f32[192,2048]{1,0:T(8,128)S(1)}, f32[192,2048]{1,0:T(8,128)}) custom-call(s32[3]{0:T(128)S(1)} %pad_add_fusion.5.info_ref, bf16[384,1024]{1,0:T(8,128)(2,1)S(1)} %shard_map.120.act_ref, bf16[512,2048]{1,0:T(8,128)(2,1)} %down_ref.3, bf16[512,512]{1,0:T(8,128)(2,1)} %collective-permute-done.18.refs_0_, ...), custom_call_target="tpu_custom_call" | custom-call | flops 1610612736 | bytes 7340032 | tf_op jit(solution)/shard_map/pallas_call | solution.py:265
  254.1 7.2 %collective-permute-done.31 = bf16[96,2048]{1,0:T(8,128)(2,1)S(1)} collective-permute-done((bf16[96,2048]{1,0:T(8,128)(2,1)S(1)}, bf16[96,2048]{1,0:T(8,128)(2,1)S(1)}, u32[]{:S(2)}, u32[]{:S(2)}) %collective-permute-start.31) | collective-permute-done | bytes 393248 | tf_op jit(solution)/shard_map/ppermute | solution.py:20
  261.4 2.6 collective-permute-start.32
  264.0 4.8 %collective-permute-done.25 = bf16[96,2048]{1,0:T(8,128)(2,1)S(1)} collective-permute-done((bf16[96,2048]{1,0:T(8,128)(2,1)S(1)}, bf16[96,2048]{1,0:T(8,128)(2,1)S(1)}, u32[]{:S(2)}, u32[]{:S(2)}) %collective-permute-start.25) | collective-permute-done | bytes 393248 | tf_op jit(solution)/shard_map/ppermute | solution.py:20
  268.8 11.3 %collective-permute-done.32 = bf16[96,2048]{1,0:T(8,128)(2,1)S(1)} collective-permute-done((bf16[96,2048]{1,0:T(8,128)(2,1)S(1)}, bf16[96,2048]{1,0:T(8,128)(2,1)S(1)}, u32[]{:S(2)}, u32[]{:S(2)}) %collective-permute-start.32) | collective-permute-done | bytes 393248 | tf_op jit(solution)/shard_map/ppermute | solution.py:20
  (148 shorter events, 58.8 us)
Async XLA Ops:
  3.8 25.3 %collective-permute-start.1 = (bf16[96,2048]{1,0:T(8,128)(2,1)S(1)}, bf16[96,2048]{1,0:T(8,128)(2,1)}, u32[]{:S(2)}, u32[]{:S(2)}) collective-permute-start(bf16[96,2048]{1,0:T(8,128)(2,1)S(1)} %fusion.7.n0), channel_id=1, source_target_pairs={{0,2},{1,3},{2,0},{3,1},{4,6},{5,7},{6,4},{7,5},{8,10},{9,11},{10,... | collective-permute-start | bytes 1179656 | tf_op jit(solution)/shard_map/ppermute | solution.py:20
  6.8 39.7 %collective-permute-start = (bf16[96,2048]{1,0:T(8,128)(2,1)S(1)}, bf16[96,2048]{1,0:T(8,128)(2,1)}, u32[]{:S(2)}, u32[]{:S(2)}) collective-permute-start(bf16[96,2048]{1,0:T(8,128)(2,1)S(1)} %fusion.7.n0), channel_id=1, source_target_pairs={{0,1},{1,0},{2,3},{3,2},{4,5},{5,4},{6,7},{7,6},{8,9},{9,8},{10,11... | collective-permute-start | bytes 1179656 | tf_op jit(solution)/shard_map/ppermute | solution.py:20
  8.8 20.4 %collective-permute-start.3 = (bf16[128,2,2,512]{3,1,0,2:T(2,128)(2,1)S(1)}, bf16[128,2,2,512]{3,1,0,2:T(2,128)(2,1)S(1)}, u32[]{:S(2)}, u32[]{:S(2)}) collective-permute-start(bf16[128,2,2,512]{3,1,0,2:T(2,128)(2,1)S(1)} %bitcast.44), channel_id=1, source_target_pairs={{0,16},{16,0},{1,17},{17,1},{2,18},{18,2},{3,19},{19,3},{4,20},{20... | collective-permute-start | bytes 1572872 | tf_op jit(solution)/shard_map/ppermute | solution.py:20
  10.8 16.4 %collective-permute-start.4 = (bf16[128,2,2,512]{3,1,0,2:T(2,128)(2,1)S(1)}, bf16[128,2,2,512]{3,1,0,2:T(2,128)(2,1)S(1)}, u32[]{:S(2)}, u32[]{:S(2)}) collective-permute-start(bf16[128,2,2,512]{3,1,0,2:T(2,128)(2,1)S(1)} %bitcast.46), channel_id=1, source_target_pairs={{0,2},{1,3},{2,0},{3,1},{4,6},{5,7},{6,4},{7,5},{8,10},{9,11},{10,... | collective-permute-start | bytes 1572872 | tf_op jit(solution)/shard_map/ppermute | solution.py:20
  29.1 17.4 %collective-permute-start.2 = (bf16[96,2048]{1,0:T(8,128)(2,1)}, bf16[96,2048]{1,0:T(8,128)(2,1)}, u32[]{:S(2)}, u32[]{:S(2)}) collective-permute-start(bf16[96,2048]{1,0:T(8,128)(2,1)} %collective-permute-done.1.n2), channel_id=1, source_target_pairs={{0,1},{1,0},{2,3},{3,2},{4,5},{5,4},{6,7},{7,6},{8,9},{9,8},{10,11... | collective-permute-start | bytes 1179656 | tf_op jit(solution)/shard_map/ppermute | solution.py:20
  64.8 51.4 %collective-permute-start.7 = (f32[192,2048]{1,0:T(8,128)}, f32[192,2048]{1,0:T(8,128)}, u32[]{:S(2)}, u32[]{:S(2)}) collective-permute-start(f32[192,2048]{1,0:T(8,128)} %get-tuple-element.18), channel_id=1, source_target_pairs={{0,1},{1,0},{2,3},{3,2},{4,5},{5,4},{6,7},{7,6},{8,9},{9,8},{10,11... | collective-permute-start | bytes 4718600 | tf_op jit(solution)/shard_map/ppermute | solution.py:20
  67.1 48.6 %collective-permute-start.12 = (bf16[2,512,512]{2,1,0:T(8,128)(2,1)S(1)}, bf16[2,512,512]{2,1,0:T(8,128)(2,1)S(1)}, u32[]{:S(2)}, u32[]{:S(2)}) collective-permute-start(bf16[2,512,512]{2,1,0:T(8,128)(2,1)S(1)} %pad_maximum_fusion), channel_id=1, source_target_pairs={{0,8},{4,12},{8,0},{12,4},{1,9},{5,13},{9,1},{13,5},{2,10},{6,14},... | collective-permute-start | bytes 3145736 | tf_op jit(solution)/shard_map/ppermute | solution.py:20
  69.8 52.9 %collective-permute-start.13 = (bf16[2,512,512]{2,1,0:T(8,128)(2,1)S(1)}, bf16[2,512,512]{2,1,0:T(8,128)(2,1)S(1)}, u32[]{:S(2)}, u32[]{:S(2)}) collective-permute-start(bf16[2,512,512]{2,1,0:T(8,128)(2,1)S(1)} %pad_maximum_fusion.1), channel_id=1, source_target_pairs={{0,4},{4,0},{8,12},{12,8},{1,5},{5,1},{9,13},{13,9},{2,6},{6,2},{1... | collective-permute-start | bytes 3145736 | tf_op jit(solution)/shard_map/ppermute | solution.py:20
  115.7 37.3 %collective-permute-start.14 = (bf16[2,512,512]{2,1,0:T(8,128)(2,1)S(1)}, bf16[2,512,512]{2,1,0:T(8,128)(2,1)S(1)}, u32[]{:S(2)}, u32[]{:S(2)}) collective-permute-start(bf16[2,512,512]{2,1,0:T(8,128)(2,1)S(1)} %collective-permute-done.12.refs_6_), channel_id=1, source_target_pairs={{0,4},{4,0},{8,12},{12,8},{1,5},{5,1},{9,13},{13,9},{2,6},{6,2},{1... | collective-permute-start | bytes 3145736 | tf_op jit(solution)/shard_map/ppermute | solution.py:20
  117.5 37.0 %collective-permute-start.8 = (bf16[96,2048]{1,0:T(8,128)(2,1)S(1)}, bf16[96,2048]{1,0:T(8,128)(2,1)S(1)}, u32[]{:S(2)}, u32[]{:S(2)}) collective-permute-start(bf16[96,2048]{1,0:T(8,128)(2,1)S(1)} %fusion.16), channel_id=1, source_target_pairs={{0,2},{1,3},{2,0},{3,1},{4,6},{5,7},{6,4},{7,5},{8,10},{9,11},{10,... | collective-permute-start | bytes 1179656 | tf_op jit(solution)/shard_map/ppermute | solution.py:20
  119.2 43.3 %collective-permute-start.19 = (bf16[512,512]{1,0:T(8,128)(2,1)S(1)}, bf16[512,512]{1,0:T(8,128)(2,1)}, u32[]{:S(2)}, u32[]{:S(2)}) collective-permute-start(bf16[512,512]{1,0:T(8,128)(2,1)S(1)} %get-tuple-element.28), channel_id=1, source_target_pairs={{0,4},{4,0},{8,12},{12,8},{1,5},{5,1},{9,13},{13,9},{2,6},{6,2},{1... | collective-permute-start | bytes 1572872 | tf_op jit(solution)/shard_map/ppermute | solution.py:20
  120.7 44.0 %collective-permute-start.18 = (bf16[512,512]{1,0:T(8,128)(2,1)S(1)}, bf16[512,512]{1,0:T(8,128)(2,1)}, u32[]{:S(2)}, u32[]{:S(2)}) collective-permute-start(bf16[512,512]{1,0:T(8,128)(2,1)S(1)} %get-tuple-element.29), channel_id=1, source_target_pairs={{0,8},{4,12},{8,0},{12,4},{1,9},{5,13},{9,1},{13,5},{2,10},{6,14},... | collective-permute-start | bytes 1572872 | tf_op jit(solution)/shard_map/ppermute | solution.py:20
  122.7 63.8 %collective-permute-start.15 = (bf16[2,512,512]{2,1,0:T(8,128)(2,1)S(1)}, bf16[2,512,512]{2,1,0:T(8,128)(2,1)S(1)}, u32[]{:S(2)}, u32[]{:S(2)}) collective-permute-start(bf16[2,512,512]{2,1,0:T(8,128)(2,1)S(1)} %collective-permute-done.12.refs_6_), channel_id=1, source_target_pairs={{0,16},{16,0},{1,17},{17,1},{2,18},{18,2},{3,19},{19,3},{4,20},{20... | collective-permute-start | bytes 3145736 | tf_op jit(solution)/shard_map/ppermute | solution.py:20
  153.1 41.2 %collective-permute-start.16 = (bf16[2,512,512]{2,1,0:T(8,128)(2,1)S(1)}, bf16[2,512,512]{2,1,0:T(8,128)(2,1)S(1)}, u32[]{:S(2)}, u32[]{:S(2)}) collective-permute-start(bf16[2,512,512]{2,1,0:T(8,128)(2,1)S(1)} %collective-permute-done.13.refs_7_), channel_id=1, source_target_pairs={{0,16},{16,0},{1,17},{17,1},{2,18},{18,2},{3,19},{19,3},{4,20},{20... | collective-permute-start | bytes 3145736 | tf_op jit(solution)/shard_map/ppermute | solution.py:20
  154.4 42.4 %collective-permute-start.17 = (bf16[2,512,512]{2,1,0:T(8,128)(2,1)S(1)}, bf16[2,512,512]{2,1,0:T(8,128)(2,1)S(1)}, u32[]{:S(2)}, u32[]{:S(2)}) collective-permute-start(bf16[2,512,512]{2,1,0:T(8,128)(2,1)S(1)} %collective-permute-done.14.refs_8_), channel_id=1, source_target_pairs={{0,16},{16,0},{1,17},{17,1},{2,18},{18,2},{3,19},{19,3},{4,20},{20... | collective-permute-start | bytes 3145736 | tf_op jit(solution)/shard_map/ppermute | solution.py:20
  162.5 19.4 %collective-permute-start.26 = (bf16[96,2048]{1,0:T(8,128)(2,1)S(1)}, bf16[96,2048]{1,0:T(8,128)(2,1)}, u32[]{:S(2)}, u32[]{:S(2)}) collective-permute-start(bf16[96,2048]{1,0:T(8,128)(2,1)S(1)} %fusion.5.refs_0_), channel_id=1, source_target_pairs={{0,8},{4,12},{8,0},{12,4},{1,9},{5,13},{9,1},{13,5},{2,10},{6,14},... | collective-permute-start | bytes 1179656 | tf_op jit(solution)/shard_map/ppermute | solution.py:20
  164.6 20.3 %collective-permute-start.20 = (bf16[512,512]{1,0:T(8,128)(2,1)}, bf16[512,512]{1,0:T(8,128)(2,1)}, u32[]{:S(2)}, u32[]{:S(2)}) collective-permute-start(bf16[512,512]{1,0:T(8,128)(2,1)} %collective-permute-done.18.refs_0_), channel_id=1, source_target_pairs={{0,4},{4,0},{8,12},{12,8},{1,5},{5,1},{9,13},{13,9},{2,6},{6,2},{1... | collective-permute-start | bytes 1572872 | tf_op jit(solution)/shard_map/ppermute | solution.py:20
  194.3 26.3 %collective-permute-start.21 = (bf16[512,512]{1,0:T(8,128)(2,1)}, bf16[512,512]{1,0:T(8,128)(2,1)}, u32[]{:S(2)}, u32[]{:S(2)}) collective-permute-start(bf16[512,512]{1,0:T(8,128)(2,1)} %collective-permute-done.18.refs_0_), channel_id=1, source_target_pairs={{0,16},{16,0},{1,17},{17,1},{2,18},{18,2},{3,19},{19,3},{4,20},{20... | collective-permute-start | bytes 1572872 | tf_op jit(solution)/shard_map/ppermute | solution.py:20
  196.9 23.7 %collective-permute-start.22 = (bf16[512,512]{1,0:T(8,128)(2,1)}, bf16[512,512]{1,0:T(8,128)(2,1)}, u32[]{:S(2)}, u32[]{:S(2)}) collective-permute-start(bf16[512,512]{1,0:T(8,128)(2,1)} %collective-permute-done.19.refs_1_), channel_id=1, source_target_pairs={{0,16},{16,0},{1,17},{17,1},{2,18},{18,2},{3,19},{19,3},{4,20},{20... | collective-permute-start | bytes 1572872 | tf_op jit(solution)/shard_map/ppermute | solution.py:20
  200.4 31.0 %collective-permute-start.23 = (bf16[512,512]{1,0:T(8,128)(2,1)}, bf16[512,512]{1,0:T(8,128)(2,1)}, u32[]{:S(2)}, u32[]{:S(2)}) collective-permute-start(bf16[512,512]{1,0:T(8,128)(2,1)} %collective-permute-done.20.refs_2_), channel_id=1, source_target_pairs={{0,16},{16,0},{1,17},{17,1},{2,18},{18,2},{3,19},{19,3},{4,20},{20... | collective-permute-start | bytes 1572872 | tf_op jit(solution)/shard_map/ppermute | solution.py:20
  201.9 35.3 %collective-permute-start.9 = (bf16[96,2048]{1,0:T(8,128)(2,1)S(1)}, bf16[96,2048]{1,0:T(8,128)(2,1)S(1)}, u32[]{:S(2)}, u32[]{:S(2)}) collective-permute-start(bf16[96,2048]{1,0:T(8,128)(2,1)S(1)} %fusion.5.refs_0_), channel_id=1, source_target_pairs={{0,1},{1,0},{2,3},{3,2},{4,5},{5,4},{6,7},{7,6},{8,9},{9,8},{10,11... | collective-permute-start | bytes 1179656 | tf_op jit(solution)/shard_map/ppermute | solution.py:20
  201.9 35.3 %collective-permute-start.11 = (bf16[96,2048]{1,0:T(8,128)(2,1)}, bf16[96,2048]{1,0:T(8,128)(2,1)S(1)}, u32[]{:S(2)}, u32[]{:S(2)}) collective-permute-start(bf16[96,2048]{1,0:T(8,128)(2,1)} %copy-done.3), channel_id=1, source_target_pairs={{0,1},{1,0},{2,3},{3,2},{4,5},{5,4},{6,7},{7,6},{8,9},{9,8},{10,11... | collective-permute-start | bytes 1179656 | tf_op jit(solution)/shard_map/ppermute | solution.py:20
  252.5 16.3 %collective-permute-start.25 = (bf16[96,2048]{1,0:T(8,128)(2,1)S(1)}, bf16[96,2048]{1,0:T(8,128)(2,1)S(1)}, u32[]{:S(2)}, u32[]{:S(2)}) collective-permute-start(bf16[96,2048]{1,0:T(8,128)(2,1)S(1)} %fusion.13), channel_id=1, source_target_pairs={{0,2},{1,3},{2,0},{3,1},{4,6},{5,7},{6,4},{7,5},{8,10},{9,11},{10,... | collective-permute-start | bytes 1179656 | tf_op jit(solution)/shard_map/ppermute | solution.py:20
  261.4 18.7 %collective-permute-start.32 = (bf16[96,2048]{1,0:T(8,128)(2,1)S(1)}, bf16[96,2048]{1,0:T(8,128)(2,1)S(1)}, u32[]{:S(2)}, u32[]{:S(2)}) collective-permute-start(bf16[96,2048]{1,0:T(8,128)(2,1)S(1)} %fusion.12), channel_id=1, source_target_pairs={{0,8},{4,12},{8,0},{12,4},{1,9},{5,13},{9,1},{13,5},{2,10},{6,14},... | collective-permute-start | bytes 1179656 | tf_op jit(solution)/shard_map/ppermute | solution.py:20
  (30 other events, 398.4 us)

commit v2 on v1

--- a/solution.py
+++ b/solution.py
@@ -13,6 +13,8 @@
 VMEM_LIMIT = 48 * 1024 * 1024
 TILE = 256
 MASKED = -1e30
+Z_APART = 2
+X_APART = 1
 
 
 def swap(value, axis, mask):
@@ -46,6 +48,87 @@
     return pl.CostEstimate(
         flops=flops, bytes_accessed=moved, transcendentals=transcendentals
     )
+
+
+def prepare_body(info, tokens, entries, normed, near, far):
+    normed[...] = layer_norm(tokens[...].astype(jnp.float32)).astype(jnp.bfloat16)
+    half = near.shape[1] // 2
+    for out, chip in ((near, info[0]), (far, 1 - info[0])):
+        begin = pl.multiple_of(chip * half, half)
+        out[:, :half] = entries[:, pl.ds(begin, half)]
+        out[:, half:] = entries[:, pl.ds(2 * half + begin, half)]
+
+
+def prepare(info, tokens, entries):
+    part = jax.ShapeDtypeStruct((entries.shape[0], entries.shape[1] // 2), jnp.bfloat16)
+    return pl.pallas_call(
+        prepare_body,
+        in_specs=[smem(), vmem(), vmem()],
+        out_specs=[vmem()] * 3,
+        out_shape=[jax.ShapeDtypeStruct(tokens.shape, jnp.bfloat16), part, part],
+        compiler_params=params(),
+        cost_estimate=cost(10 * tokens.size, 4 * tokens.size + 4 * entries.size),
+    )(info, tokens, entries)
+
+
+def cut_body(info, gate, up, down, *refs):
+    outs, sems = refs[:-1], refs[-1]
+    quarter = outs[0].shape[1]
+    copies = []
+    for at, out in enumerate(outs):
+        begin = pl.multiple_of(info[1 + at // 3] * quarter, quarter)
+        source = (gate, up, down)[at % 3].at[:, pl.ds(begin, quarter)]
+        copies.append(pltpu.make_async_copy(source, out, sems.at[at]))
+    for copy in copies:
+        copy.start()
+    for copy in copies:
+        copy.wait()
+
+
+def cut(info, *weights):
+    rows, columns = weights[0].shape
+    shape = jax.ShapeDtypeStruct((rows, columns // 4), jnp.bfloat16)
+    return pl.pallas_call(
+        cut_body,
+        in_specs=[smem()] + [anywhere()] * 3,
+        out_specs=[anywhere()] * 6,
+        out_shape=[shape] * 6,
+        scratch_shapes=[pltpu.SemaphoreType.DMA((6,))],
+        compiler_params=params(),
+        cost_estimate=cost(0, 6 * rows * columns),
+    )(info, *weights)
+
+
+def pick_body(info, near, near_came, far, far_came, keep, send):
+    quarter = keep.shape[2] // 2
+    moved = info[0] == 1
+
+    def fill(sources):
+        for at, source in enumerate(sources):
+            for out, core in ((keep, info[1]), (send, 1 - info[1])):
+                begin = pl.multiple_of(core * quarter, quarter)
+                out[at, :, :quarter] = source[:, pl.ds(begin, quarter)]
+                out[at, :, quarter:] = source[:, pl.ds(2 * quarter + begin, quarter)]
+
+    @pl.when(moved)
+    def _():
+        fill((near_came, far_came))
+
+    @pl.when(jnp.logical_not(moved))
+    def _():
+        fill((near, far))
+
+
+def pick(info, near, near_came, far, far_came):
+    shape = jax.ShapeDtypeStruct((2, near.shape[0], near.shape[1] // 2), jnp.bfloat16)
+    return pl.pallas_call(
+        pick_body,
+        in_specs=[smem()] + [vmem()] * 4,
+        out_specs=[vmem()] * 2,
+        out_shape=[shape] * 2,
+        compiler_params=params(),
+        cost_estimate=cost(0, 12 * near.size),
+    )(info, near, near_came, far, far_came)
 
 
 def project_body(n0, n1, n2, n3, cosine, sine, wq, wk, wv, q_ref, k_ref, v_ref, rows):
@@ -175,40 +258,36 @@
 def gate_up(masks, info, parts, gate, up, mine, other):
     count, depth = parts[0].shape
     rows = 4 * count
-    shard, quarter = mine[0].shape[1:]
-    pieces = len(mine)
+    shard, quarter = mine[0][0].shape
+    pieces = len(mine[0])
 
     def body(info_ref, *refs):
         blocks, refs = refs[:4], refs[4:]
-        gate_ref, up_ref, refs = refs[0], refs[1], refs[2:]
-        sets, refs = (refs[:pieces], refs[pieces : 2 * pieces]), refs[2 * pieces :]
+        wholes, refs = refs[:2], refs[2:]
+        sets, refs = refs[: 4 * pieces], refs[4 * pieces :]
         act_ref, x, held, sems = refs
         own = info_ref[0]
         copies = []
         for half in range(2):
             begin = pl.multiple_of(info_ref[1 + half] * quarter, quarter)
-            there = pl.ds(pl.multiple_of(own * shard, shard), shard)
-            for which, source in enumerate((gate_ref, up_ref)):
-                copies.append(
-                    pltpu.make_async_copy(
-                        source.at[:, pl.ds(begin, quarter)],
-                        held.at[half, which, there, :],
-                        sems.at[half, 0, which],
+            for which in range(2):
+                for at, mask in enumerate(masks):
+                    there = pl.ds(pl.multiple_of((own ^ mask) * shard, shard), shard)
+                    if at:
+                        source = sets[(2 * half + which) * pieces + at - 1]
+                    else:
+                        source = wholes[which].at[:, pl.ds(begin, quarter)]
+                    copies.append(
+                        pltpu.make_async_copy(
+                            source, held.at[half, which, there, :], sems.at[half, which, at]
+                        )
                     )
-                )
-            for at, mask in enumerate(masks[1:]):
-                there = pl.ds(pl.multiple_of((own ^ mask) * shard, shard), shard)
-                copies.append(
-                    pltpu.make_async_copy(
-                        sets[half][at], held.at[half, :, there, :], sems.at[half, at + 1, 0]
-                    )
-                )
         for copy in copies:
             copy.start()
         for at, block in enumerate(blocks):
             x[pl.ds(at * count, count), :] = block[...]
         for half in range(2):
-            for copy in copies[half * (pieces + 2) : (half + 1) * (pieces + 2)]:
+            for copy in copies[2 * half * (pieces + 1) : 2 * (half + 1) * (pieces + 1)]:
                 copy.wait()
             for at in range(0, quarter, TILE):
                 g = jnp.dot(
@@ -223,17 +302,17 @@
 
     return pl.pallas_call(
         body,
-        in_specs=[smem()] + [vmem()] * 4 + [anywhere()] * (2 + 2 * pieces),
+        in_specs=[smem()] + [vmem()] * 4 + [anywhere()] * (2 + 4 * pieces),
         out_specs=vmem(),
         out_shape=jax.ShapeDtypeStruct((rows, 2 * quarter), jnp.bfloat16),
         scratch_shapes=[
             pltpu.VMEM((rows, depth), jnp.bfloat16),
             pltpu.VMEM((2, 2, depth, quarter), jnp.bfloat16),
-            pltpu.SemaphoreType.DMA((2, pieces + 1, 2)),
+            pltpu.SemaphoreType.DMA((2, 2, pieces + 1)),
         ],
         compiler_params=params(),
         cost_estimate=cost(8 * rows * depth * quarter, 8 * depth * quarter, 2 * rows * quarter),
-    )(info, *parts, gate, up, *mine, *other)
+    )(info, *parts, gate, up, *mine[0], *mine[1], *other[0], *other[1])
 
 
 def down_rows(masks, info, act, down, mine, other):
@@ -288,11 +367,51 @@
     return near[:count] + came[:count] + swap(sent, "mp", 2).astype(jnp.float32)
 
 
-def spread_pieces(own, leaving, pair, bits):
-    pieces = {0: own, pair: swap(leaving, "dp", pair)}
-    for bit in bits:
-        pieces.update({mask ^ bit: swap(piece, "dp", bit) for mask, piece in list(pieces.items())})
-    return pieces
+def after(value, *earlier):
+    return lax.optimization_barrier((value,) + earlier)[0] if earlier else value
+
+
+def queue(transfers, apart):
+    done = []
+    for transfer in transfers:
+        done.append(transfer(*done[-apart:][:1]) if len(done) >= apart else transfer())
+    return done
+
+
+def spread_weights(mine, leaving, pair, bits, first):
+    steps = [[], [(0, pair)], []]
+    for start, step in ((0, steps[0]), (pair, steps[2])):
+        known = [start]
+        for bit in bits:
+            step += [(mask, bit) for mask in known]
+            known += [mask ^ bit for mask in known]
+    held = [{0: piece} for piece in mine]
+
+    def over_planes(weight, mask, bit):
+        def transfer(*earlier):
+            piece = leaving[weight] if bit == pair else held[weight][mask]
+            held[weight][mask ^ bit] = swap(after(piece, *earlier), "dp", bit)
+            return held[weight][mask ^ bit]
+
+        return transfer
+
+    order = [(0, 0), (0, 1), (1, 0), (1, 1), (0, 2), (2, 1), (1, 2), (2, 0), (2, 2)]
+    queue([over_planes(w, *step) for w, kind in order for step in steps[kind]], Z_APART)
+    other = [{} for _ in mine]
+
+    def over_replicas(weight, mask):
+        def transfer(*earlier):
+            other[weight][mask] = swap(after(held[weight][mask], *earlier), "rep", 1)
+            return other[weight][mask]
+
+        return transfer
+
+    order = [(0, 0), (0, 1), (1, 0), (1, 1), (0, 2), (1, 2), (2, 0), (2, 1), (2, 2)]
+    line = [lambda *_: first]
+    queue(line + [over_replicas(w, m ^ b) for w, kind in order for m, b in steps[kind]], X_APART)
+    masks = [0] + [mask ^ bit for step in steps for mask, bit in step]
+    pieces = lambda sets: [[part[mask] for mask in masks[1:]] for part in sets]
+    return masks, pieces(held), pieces(other)
 
 
 def row_facts(request_row, length_row, member, cache_size):
@@ -350,54 +469,26 @@
     source = jnp.where(moved_here, (1 - replica) * planes + within, group)
     length_row = lax.dynamic_slice_in_dim(cached_lengths, source, 1, 0)[0]
 
-    normed = layer_norm(tokens.astype(jnp.float32)).astype(jnp.bfloat16)
-    parts = gather_rows(normed)
-
-    held, width = cache_entries.shape
     chip, core = member // 2, member % 2
-    entries = cache_entries.reshape(held, 2, 2, 2, width // 8)
-    near = lax.dynamic_slice_in_dim(entries, chip, 1, 2)[:, :, 0]
-    far = lax.dynamic_slice_in_dim(entries, 1 - chip, 1, 2)[:, :, 0]
+    normed, near, far = prepare(chip[None].astype(jnp.int32), tokens, cache_entries)
     near_came = swap(near, "rep", 1)
     far = swap(far, "mp", 2)
+    parts = gather_rows(normed)
     far_came = swap(far, "rep", 1)
-    near = jnp.where(moved_here, near_came, near)
-    far = jnp.where(moved_here, far_came, far)
-
-    def of_core(which):
-        return jnp.stack(
-            [
-                lax.dynamic_slice_in_dim(rows, which, 1, 2).reshape(held, width // 4)
-                for rows in (near, far)
-            ]
-        )
-
-    keep = of_core(core)
-    came = swap(of_core(1 - core), "mp", 1)
+    choice = jnp.stack([traded[0], core]).astype(jnp.int32)
+    keep, came = pick(choice, near, near_came, far, far_came)
+    came = swap(came, "mp", 1)
 
     pair = planes // 2
     bits = [1 << at for at in range(planes.bit_length() - 1) if 1 << at != pair]
     half = (within // pair) % 2
-    quarter = gate_weight.shape[1] // 4
     index_mine, index_other = 2 * half + replica, 2 * half + 1 - replica
     index_leaving = 2 * (1 - half) + replica
-
-    def cut(weight, index):
-        return lax.dynamic_slice_in_dim(weight, index * quarter, quarter, 1)
-
-    def gate_and_up(index):
-        return jnp.stack([cut(gate_weight, index), cut(up_weight, index)])
-
-    wide = spread_pieces(gate_and_up(index_mine), gate_and_up(index_leaving), pair, bits)
-    masks = list(wide)
-    wide_mine = [wide[mask] for mask in masks[1:]]
-    wide_other = [swap(piece, "rep", 1) for piece in wide_mine]
-    back = spread_pieces(cut(down_weight, index_mine), cut(down_weight, index_leaving), pair, bits)
-    back_mine = [back[mask] for mask in masks[1:]]
-    back_other = [swap(piece, "rep", 1) for piece in back_mine]
-    info = jnp.stack([within, index_mine, index_other]).astype(jnp.int32)
-
-    positions, of_row, of_column = row_facts(request_ids[0], length_row, member, 4 * held)
+    info = jnp.stack([within, index_mine, index_other, index_leaving]).astype(jnp.int32)
+    cuts = cut(info[jnp.array([0, 1, 3])], gate_weight, up_weight, down_weight)
+    masks, mine, other = spread_weights(cuts[:3], cuts[3:], pair, bits, far_came)
+
+    positions, of_row, of_column = row_facts(request_ids[0], length_row, member, 4 * cache_entries.shape[0])
     half_dim = HEAD_DIM // 2
     freq = ROPE_BASE ** (-jnp.arange(half_dim, dtype=jnp.float32) / half_dim)
     angle = positions.astype(jnp.float32)[:, None] * freq[None, :]
@@ -411,10 +502,10 @@
 
     rows_pair = gather_rows(swap(normed_own, "dp", pair))
     rows_own = gather_rows(normed_own)
-    act_own = gate_up(masks, info, rows_own, gate_weight, up_weight, wide_mine, wide_other)
-    act_pair = gate_up(masks, info, rows_pair, gate_weight, up_weight, wide_mine, wide_other)
-    pair_sum = reduce_rows(*down_rows(masks, info, act_pair, down_weight, back_mine, back_other))
-    own_sum = reduce_rows(*down_rows(masks, info, act_own, down_weight, back_mine, back_other))
+    act_own = gate_up(masks, info, rows_own, gate_weight, up_weight, mine[:2], other[:2])
+    act_pair = gate_up(masks, info, rows_pair, gate_weight, up_weight, mine[:2], other[:2])
+    pair_sum = reduce_rows(*down_rows(masks, info, act_pair, down_weight, mine[2], other[2]))
+    own_sum = reduce_rows(*down_rows(masks, info, act_own, down_weight, mine[2], other[2]))
     came_sum = swap(pair_sum.astype(jnp.bfloat16), "dp", pair).astype(jnp.float32)
     return (state_own.astype(jnp.float32) + (own_sum + came_sum)).astype(jnp.bfloat16)
 

time: 282 us -> 225 us (0.80)
  waiting for transfers between devices: 176 us -> 131 us
  other arithmetic: 13.5 us -> 4.62 us
  local copies, waits for them, and re-layouts: 14.9 us -> 9.58 us
    ppermute x33 -> x39, waiting for transfers between devices: 176 us -> 131 us  [swap(): return lax.ppermute(value, axis, pairs)]
    another operation x5 -> x0, local copies, waits for them, and re-layouts: 6.37 us -> none  [the longest x4 4.71 us: of_core(): jnp.stack([lax.dynamic_slice_in_dim(rows, which, 1, 2).reshape(held, widt...]
    pallas_call x0 -> x3, Pallas kernels: none -> 4.75 us  [the longest x1 2.32 us: cut(): pl.pallas_call(cut_body, in_specs=[smem()] + [anywhere()] * 3, out_specs=...]
    unnamed x42 -> x50, local copies, waits for them, and re-layouts: 4.24 us -> 8.69 us
    dynamic_slice x5 -> x0, local copies, waits for them, and re-layouts: 3.24 us -> none  [the longest x1 1.6 us: of_core(): lax.dynamic_slice_in_dim(rows, which, 1, 2).reshape(held, width // 4)]
    ppermute x33 -> x39, starting transfers between devices: 39.7 us -> 40 us  [swap(): return lax.ppermute(value, axis, pairs)]
  transfers between devices with their start and end apart: 33 -> 39, of which waited for: 16 -> 23; matrix products, arithmetic and copies ran while one was open for 7% -> 2% of each run, Pallas kernels for 10% -> 17%
where the time goes in v2:
time: 225 us
  waiting for transfers between devices  131 us (58%)
  starting transfers between devices  40 us (18%)
  Pallas kernels  38.6 us (17%)
  local copies, waits for them, and re-layouts  9.58 us (4%)
  other arithmetic  4.62 us (2%)
    ppermute x39, waiting for transfers between devices, swap(): return lax.ppermute(value, axis, pairs)  131 us
    ppermute x39, starting transfers between devices, swap(): return lax.ppermute(value, axis, pairs)  40 us
    pallas_call x2, Pallas kernels, gate_up(): pl.pallas_call(body, in_specs=[smem()] + [vmem()] * 4 + [anywhere()] * (2...  12.9 us
    pallas_call x2, Pallas kernels, down_rows(): pl.pallas_call(body, in_specs=[smem(), vmem()] + [anywhere()] * (1 + 2 *...  9.67 us
    unnamed x50, local copies, waits for them, and re-layouts  8.69 us
    pallas_call x1, Pallas kernels, attend(): pl.pallas_call(attend_body, in_specs=[vmem()] * 8, out_specs=[vmem()] * 2...  6.11 us
    pallas_call x1, Pallas kernels, project(): pl.pallas_call(project_body, grid=(width // TILE,), in_specs=[whole((coun...  5.11 us
  transfers between devices with their start and end apart: 39, of which 23 were waited for; matrix products, arithmetic and copies ran while one was open for 2% of the time, Pallas kernels for 17%

profile of v2, /device:TPU:0, one launch (start us, length us, event | category | flops | bytes accessed | tf_op | source)
XLA Modules:
  0.0 224.9 jit_solution(2255416056235557316)
XLA Ops:
  3.5 3.0 %collective-permute-start.1 = (bf16[96,2048]{1,0:T(8,128)(2,1)S(1)}, bf16[96,2048]{1,0:T(8,128)(2,1)}, u32[]{:S(2)}, u32[]{:S(2)}) collective-permute-start(bf16[96,2048]{1,0:T(8,128)(2,1)S(1)} %get-tuple-element.41.n0), channel_id=1, source_target_pairs={{0,2},{1,3},{2,0},{3,1},{4,6},{5,7},{6,4},{7,5},{8,10},{9,11},{10,... | collective-permute-start | bytes 1179656 | tf_op jit(solution)/shard_map/ppermute | solution.py:22
  18.5 8.4 %collective-permute-done.4.far = bf16[128,2048]{1,0:T(8,128)(2,1)S(1)} collective-permute-done((bf16[128,2048]{1,0:T(8,128)(2,1)}, bf16[128,2048]{1,0:T(8,128)(2,1)S(1)}, u32[]{:S(2)}, u32[]{:S(2)}) %collective-permute-start.4) | collective-permute-done | bytes 524320 | tf_op jit(solution)/shard_map/ppermute | solution.py:22
  33.0 6.9 %collective-permute-done.5.far_came = bf16[128,2048]{1,0:T(8,128)(2,1)S(1)} collective-permute-done((bf16[128,2048]{1,0:T(8,128)(2,1)S(1)}, bf16[128,2048]{1,0:T(8,128)(2,1)S(1)}, u32[]{:S(2)}, u32[]{:S(2)}) %collective-permute-start.5) | collective-permute-done | bytes 524320 | tf_op jit(solution)/shard_map/ppermute | solution.py:22
  41.7 5.1 %shard_map.128 = (bf16[384,512]{1,0:T(8,128)(2,1)S(1)}, bf16[384,512]{1,0:T(8,128)(2,1)S(1)}, bf16[384,512]{1,0:T(8,128)(2,1)S(1)}) custom-call(bf16[96,2048]{1,0:T(8,128)(2,1)S(1)} %get-tuple-element.41.n0, bf16[96,2048]{1,0:T(8,128)(2,1)} %collective-permute-done.n1, bf16[96,2048]{1,0:T(8,128)(2,1)} %collective-permute-done.1.n2, ...), custom_call_target="tpu_custom_call" | custom-call | flops 2415919104 | bytes 7864320 | tf_op jit(solution)/shard_map/pallas_call | solution.py:164
  48.3 6.1 %shard_map.130 = (f32[192,2048]{1,0:T(8,128)S(1)}, f32[192,2048]{1,0:T(8,128)S(1)}) custom-call(bf16[384,512]{1,0:T(8,128)(2,1)S(1)} %get-tuple-element.42.q, bf16[384,512]{1,0:T(8,128)(2,1)S(1)} %get-tuple-element.43.k, bf16[384,512]{1,0:T(8,128)(2,1)S(1)} %get-tuple-element.44.v, bf16[2,128,1024]{2,1,0:T(8,128)(2,1)S(1)} %get-tuple-element.47.keep, ...), custom_call_target="tpu_custom_call" | custom-call | flops 1509949440 | bytes 4718592 | tf_op jit(solution)/shard_map/pallas_call | solution.py:243
  57.1 4.0 %collective-permute-done.18.refs_12_ = bf16[512,512]{1,0:T(8,128)(2,1)S(1)} collective-permute-done((bf16[512,512]{1,0:T(8,128)(2,1)S(1)}, bf16[512,512]{1,0:T(8,128)(2,1)S(1)}, u32[]{:S(2)}, u32[]{:S(2)}) %collective-permute-start.18) | collective-permute-done | bytes 524320 | tf_op jit(solution)/shard_map/ppermute | solution.py:22
  65.2 9.0 %collective-permute-done.14.refs_9_ = bf16[512,512]{1,0:T(8,128)(2,1)S(1)} collective-permute-done((bf16[512,512]{1,0:T(8,128)(2,1)S(1)}, bf16[512,512]{1,0:T(8,128)(2,1)S(1)}, u32[]{:S(2)}, u32[]{:S(2)}) %collective-permute-start.14) | collective-permute-done | bytes 524320 | tf_op jit(solution)/shard_map/ppermute | solution.py:22
  77.7 10.4 %collective-permute-done.16.refs_10_ = bf16[512,512]{1,0:T(8,128)(2,1)S(1)} collective-permute-done((bf16[512,512]{1,0:T(8,128)(2,1)S(1)}, bf16[512,512]{1,0:T(8,128)(2,1)S(1)}, u32[]{:S(2)}, u32[]{:S(2)}) %collective-permute-start.16) | collective-permute-done | bytes 524320 | tf_op jit(solution)/shard_map/ppermute | solution.py:22
  90.4 7.2 %collective-permute-done.15.refs_8_ = bf16[512,512]{1,0:T(8,128)(2,1)S(1)} collective-permute-done((bf16[512,512]{1,0:T(8,128)(2,1)S(1)}, bf16[512,512]{1,0:T(8,128)(2,1)S(1)}, u32[]{:S(2)}, u32[]{:S(2)}) %collective-permute-start.15) | collective-permute-done | bytes 524320 | tf_op jit(solution)/shard_map/ppermute | solution.py:22
  101.2 11.6 %collective-permute-done.24.refs_1_ = bf16[512,512]{1,0:T(8,128)(2,1)S(1)} collective-permute-done((bf16[512,512]{1,0:T(8,128)(2,1)S(1)}, bf16[512,512]{1,0:T(8,128)(2,1)S(1)}, u32[]{:S(2)}, u32[]{:S(2)}) %collective-permute-start.24) | collective-permute-done | bytes 524320 | tf_op jit(solution)/shard_map/ppermute | solution.py:22
  113.7 6.7 %collective-permute-done.17.refs_11_ = bf16[512,512]{1,0:T(8,128)(2,1)S(1)} collective-permute-done((bf16[512,512]{1,0:T(8,128)(2,1)S(1)}, bf16[512,512]{1,0:T(8,128)(2,1)S(1)}, u32[]{:S(2)}, u32[]{:S(2)}) %collective-permute-start.17) | collective-permute-done | bytes 524320 | tf_op jit(solution)/shard_map/ppermute | solution.py:22
  121.6 6.6 %collective-permute-done.25.refs_0_ = bf16[512,512]{1,0:T(8,128)(2,1)S(1)} collective-permute-done((bf16[512,512]{1,0:T(8,128)(2,1)S(1)}, bf16[512,512]{1,0:T(8,128)(2,1)S(1)}, u32[]{:S(2)}, u32[]{:S(2)}) %collective-permute-start.25) | collective-permute-done | bytes 524320 | tf_op jit(solution)/shard_map/ppermute | solution.py:22
  128.2 3.4 %collective-permute-done.23.refs_17_ = bf16[512,512]{1,0:T(8,128)(2,1)S(1)} collective-permute-done((bf16[512,512]{1,0:T(8,128)(2,1)S(1)}, bf16[512,512]{1,0:T(8,128)(2,1)S(1)}, u32[]{:S(2)}, u32[]{:S(2)}) %collective-permute-start.23) | collective-permute-done | bytes 524320 | tf_op jit(solution)/shard_map/ppermute | solution.py:22
  132.4 3.6 %collective-permute-start.32 = (bf16[96,2048]{1,0:T(8,128)(2,1)S(1)}, bf16[96,2048]{1,0:T(8,128)(2,1)S(1)}, u32[]{:S(2)}, u32[]{:S(2)}) collective-permute-start(bf16[96,2048]{1,0:T(8,128)(2,1)S(1)} %fusion.3.refs_0_), channel_id=1, source_target_pairs={{0,8},{4,12},{8,0},{12,4},{1,9},{5,13},{9,1},{13,5},{2,10},{6,14},... | collective-permute-start | bytes 1179656 | tf_op jit(solution)/shard_map/ppermute | solution.py:22
  136.0 11.4 %collective-permute-done.32.refs_0_ = bf16[96,2048]{1,0:T(8,128)(2,1)S(1)} collective-permute-done((bf16[96,2048]{1,0:T(8,128)(2,1)S(1)}, bf16[96,2048]{1,0:T(8,128)(2,1)S(1)}, u32[]{:S(2)}, u32[]{:S(2)}) %collective-permute-start.32) | collective-permute-done | bytes 393248 | tf_op jit(solution)/shard_map/ppermute | solution.py:22
  151.7 7.8 %collective-permute-done.34.refs_2_ = bf16[96,2048]{1,0:T(8,128)(2,1)S(1)} collective-permute-done((bf16[96,2048]{1,0:T(8,128)(2,1)S(1)}, bf16[96,2048]{1,0:T(8,128)(2,1)S(1)}, u32[]{:S(2)}, u32[]{:S(2)}) %collective-permute-start.34) | collective-permute-done | bytes 393248 | tf_op jit(solution)/shard_map/ppermute | solution.py:22
  164.2 6.5 %shard_map.134.act_ref = bf16[384,1024]{1,0:T(8,128)(2,1)} custom-call(s32[4]{0:T(128)S(1)} %pad_add_fusion.6.info_ref, bf16[96,2048]{1,0:T(8,128)(2,1)S(1)} %collective-permute-done.32.refs_0_, bf16[96,2048]{1,0:T(8,128)(2,1)S(1)} %collective-permute-done.33.refs_1_, bf16[96,2048]{1,0:T(8,128)(2,1)S(1)} %collective-permute-done.34.refs_2_, ...), custom_call_target="tpu_custom_call" | custom-call | flops 3221225472 | bytes 8388608 | tf_op jit(solution)/shard_map/pallas_call | solution.py:303
  170.7 3.2 %collective-permute-done.29.refs_5_ = bf16[512,512]{1,0:T(8,128)(2,1)S(1)} collective-permute-done((bf16[512,512]{1,0:T(8,128)(2,1)S(1)}, bf16[512,512]{1,0:T(8,128)(2,1)S(1)}, u32[]{:S(2)}, u32[]{:S(2)}) %collective-permute-start.29) | collective-permute-done | bytes 524320 | tf_op jit(solution)/shard_map/ppermute | solution.py:22
  175.0 4.9 %shard_map.135 = (f32[192,2048]{1,0:T(8,128)S(1)}, f32[192,2048]{1,0:T(8,128)}) custom-call(s32[4]{0:T(128)S(1)} %pad_add_fusion.6.info_ref, bf16[384,1024]{1,0:T(8,128)(2,1)S(1)} %copy-done.3, bf16[512,2048]{1,0:T(8,128)(2,1)} %down_ref.3, bf16[512,512]{1,0:T(8,128)(2,1)S(1)} %collective-permute-done.25.refs_0_, ...), custom_call_target="tpu_custom_call" | custom-call | flops 1610612736 | bytes 7340032 | tf_op jit(solution)/shard_map/pallas_call | solution.py:344
  180.0 6.5 %shard_map.132.act_ref = bf16[384,1024]{1,0:T(8,128)(2,1)} custom-call(s32[4]{0:T(128)S(1)} %pad_add_fusion.6.info_ref, bf16[96,2048]{1,0:T(8,128)(2,1)S(1)} %fusion.3.refs_0_, bf16[96,2048]{1,0:T(8,128)(2,1)S(1)} %collective-permute-done.9.refs_1_, bf16[96,2048]{1,0:T(8,128)(2,1)S(1)} %collective-permute-done.10.refs_2_, ...), custom_call_target="tpu_custom_call" | custom-call | flops 3221225472 | bytes 8388608 | tf_op jit(solution)/shard_map/pallas_call | solution.py:303
  187.6 4.8 %shard_map.133 = (f32[192,2048]{1,0:T(8,128)S(1)}, f32[192,2048]{1,0:T(8,128)}) custom-call(s32[4]{0:T(128)S(1)} %pad_add_fusion.6.info_ref, bf16[384,1024]{1,0:T(8,128)(2,1)S(1)} %copy-done.2, bf16[512,2048]{1,0:T(8,128)(2,1)} %down_ref.3, bf16[512,512]{1,0:T(8,128)(2,1)S(1)} %collective-permute-done.25.refs_0_, ...), custom_call_target="tpu_custom_call" | custom-call | flops 1610612736 | bytes 7340032 | tf_op jit(solution)/shard_map/pallas_call | solution.py:344
  197.9 7.2 %collective-permute-done.37 = bf16[96,2048]{1,0:T(8,128)(2,1)S(1)} collective-permute-done((bf16[96,2048]{1,0:T(8,128)(2,1)S(1)}, bf16[96,2048]{1,0:T(8,128)(2,1)S(1)}, u32[]{:S(2)}, u32[]{:S(2)}) %collective-permute-start.37) | collective-permute-done | bytes 393248 | tf_op jit(solution)/shard_map/ppermute | solution.py:22
  206.0 6.6 %collective-permute-done.31 = bf16[96,2048]{1,0:T(8,128)(2,1)S(1)} collective-permute-done((bf16[96,2048]{1,0:T(8,128)(2,1)S(1)}, bf16[96,2048]{1,0:T(8,128)(2,1)S(1)}, u32[]{:S(2)}, u32[]{:S(2)}) %collective-permute-start.31) | collective-permute-done | bytes 393248 | tf_op jit(solution)/shard_map/ppermute | solution.py:22
  212.6 11.3 %collective-permute-done.38 = bf16[96,2048]{1,0:T(8,128)(2,1)S(1)} collective-permute-done((bf16[96,2048]{1,0:T(8,128)(2,1)S(1)}, bf16[96,2048]{1,0:T(8,128)(2,1)S(1)}, u32[]{:S(2)}, u32[]{:S(2)}) %collective-permute-start.38) | collective-permute-done | bytes 393248 | tf_op jit(solution)/shard_map/ppermute | solution.py:22
  (152 shorter events, 61.6 us)
Async XLA Ops:
  3.5 26.6 %collective-permute-start.1 = (bf16[96,2048]{1,0:T(8,128)(2,1)S(1)}, bf16[96,2048]{1,0:T(8,128)(2,1)}, u32[]{:S(2)}, u32[]{:S(2)}) collective-permute-start(bf16[96,2048]{1,0:T(8,128)(2,1)S(1)} %get-tuple-element.41.n0), channel_id=1, source_target_pairs={{0,2},{1,3},{2,0},{3,1},{4,6},{5,7},{6,4},{7,5},{8,10},{9,11},{10,... | collective-permute-start | bytes 1179656 | tf_op jit(solution)/shard_map/ppermute | solution.py:22
  6.5 35.2 %collective-permute-start = (bf16[96,2048]{1,0:T(8,128)(2,1)S(1)}, bf16[96,2048]{1,0:T(8,128)(2,1)}, u32[]{:S(2)}, u32[]{:S(2)}) collective-permute-start(bf16[96,2048]{1,0:T(8,128)(2,1)S(1)} %get-tuple-element.41.n0), channel_id=1, source_target_pairs={{0,1},{1,0},{2,3},{3,2},{4,5},{5,4},{6,7},{7,6},{8,9},{9,8},{10,11... | collective-permute-start | bytes 1179656 | tf_op jit(solution)/shard_map/ppermute | solution.py:22
  6.5 20.3 %collective-permute-start.4 = (bf16[128,2048]{1,0:T(8,128)(2,1)}, bf16[128,2048]{1,0:T(8,128)(2,1)S(1)}, u32[]{:S(2)}, u32[]{:S(2)}) collective-permute-start(bf16[128,2048]{1,0:T(8,128)(2,1)} %get-tuple-element.46), channel_id=1, source_target_pairs={{0,2},{1,3},{2,0},{3,1},{4,6},{5,7},{6,4},{7,5},{8,10},{9,11},{10,... | collective-permute-start | bytes 1572872 | tf_op jit(solution)/shard_map/ppermute | solution.py:22
  6.5 23.9 %collective-permute-start.3 = (bf16[128,2048]{1,0:T(8,128)(2,1)S(1)}, bf16[128,2048]{1,0:T(8,128)(2,1)}, u32[]{:S(2)}, u32[]{:S(2)}) collective-permute-start(bf16[128,2048]{1,0:T(8,128)(2,1)S(1)} %get-tuple-element.45.near), channel_id=1, source_target_pairs={{0,16},{16,0},{1,17},{17,1},{2,18},{18,2},{3,19},{19,3},{4,20},{20... | collective-permute-start | bytes 1572872 | tf_op jit(solution)/shard_map/ppermute | solution.py:22
  15.5 31.2 %collective-permute-start.12 = (bf16[512,512]{1,0:T(8,128)(2,1)}, bf16[512,512]{1,0:T(8,128)(2,1)S(1)}, u32[]{:S(2)}, u32[]{:S(2)}) collective-permute-start(bf16[512,512]{1,0:T(8,128)(2,1)} %get-tuple-element.51), channel_id=1, source_target_pairs={{0,4},{4,0},{8,12},{12,8},{1,5},{5,1},{9,13},{13,9},{2,6},{6,2},{1... | collective-permute-start | bytes 1572872 | tf_op jit(solution)/shard_map/ppermute | solution.py:22
  30.4 26.7 %collective-permute-start.13 = (bf16[512,512]{1,0:T(8,128)(2,1)}, bf16[512,512]{1,0:T(8,128)(2,1)S(1)}, u32[]{:S(2)}, u32[]{:S(2)}) collective-permute-start(bf16[512,512]{1,0:T(8,128)(2,1)} %copy-done.16), channel_id=1, source_target_pairs={{0,8},{4,12},{8,0},{12,4},{1,9},{5,13},{9,1},{13,5},{2,10},{6,14},... | collective-permute-start | bytes 1572872 | tf_op jit(solution)/shard_map/ppermute | solution.py:22
  46.8 14.4 %collective-permute-start.18 = (bf16[512,512]{1,0:T(8,128)(2,1)S(1)}, bf16[512,512]{1,0:T(8,128)(2,1)S(1)}, u32[]{:S(2)}, u32[]{:S(2)}) collective-permute-start(bf16[512,512]{1,0:T(8,128)(2,1)S(1)} %collective-permute-done.12.refs_6_), channel_id=1, source_target_pairs={{0,16},{16,0},{1,17},{17,1},{2,18},{18,2},{3,19},{19,3},{4,20},{20... | collective-permute-start | bytes 1572872 | tf_op jit(solution)/shard_map/ppermute | solution.py:22
  54.4 34.4 %collective-permute-start.7 = (f32[192,2048]{1,0:T(8,128)S(1)}, f32[192,2048]{1,0:T(8,128)S(1)}, u32[]{:S(2)}, u32[]{:S(2)}) collective-permute-start(f32[192,2048]{1,0:T(8,128)S(1)} %get-tuple-element.50), channel_id=1, source_target_pairs={{0,1},{1,0},{2,3},{3,2},{4,5},{5,4},{6,7},{7,6},{8,9},{9,8},{10,11... | collective-permute-start | bytes 4718600 | tf_op jit(solution)/shard_map/ppermute | solution.py:22
  54.7 19.5 %collective-permute-start.14 = (bf16[512,512]{1,0:T(8,128)(2,1)S(1)}, bf16[512,512]{1,0:T(8,128)(2,1)S(1)}, u32[]{:S(2)}, u32[]{:S(2)}) collective-permute-start(bf16[512,512]{1,0:T(8,128)(2,1)S(1)} %copy-done.15), channel_id=1, source_target_pairs={{0,4},{4,0},{8,12},{12,8},{1,5},{5,1},{9,13},{13,9},{2,6},{6,2},{1... | collective-permute-start | bytes 1572872 | tf_op jit(solution)/shard_map/ppermute | solution.py:22
  61.2 13.5 %collective-permute-start.19 = (bf16[512,512]{1,0:T(8,128)(2,1)S(1)}, bf16[512,512]{1,0:T(8,128)(2,1)S(1)}, u32[]{:S(2)}, u32[]{:S(2)}) collective-permute-start(bf16[512,512]{1,0:T(8,128)(2,1)S(1)} %collective-permute-done.13.refs_7_), channel_id=1, source_target_pairs={{0,16},{16,0},{1,17},{17,1},{2,18},{18,2},{3,19},{19,3},{4,20},{20... | collective-permute-start | bytes 1572872 | tf_op jit(solution)/shard_map/ppermute | solution.py:22
  62.6 25.5 %collective-permute-start.16 = (bf16[512,512]{1,0:T(8,128)(2,1)S(1)}, bf16[512,512]{1,0:T(8,128)(2,1)S(1)}, u32[]{:S(2)}, u32[]{:S(2)}) collective-permute-start(bf16[512,512]{1,0:T(8,128)(2,1)S(1)} %copy-done.13), channel_id=1, source_target_pairs={{0,8},{4,12},{8,0},{12,4},{1,9},{5,13},{9,1},{13,5},{2,10},{6,14},... | collective-permute-start | bytes 1572872 | tf_op jit(solution)/shard_map/ppermute | solution.py:22
  76.1 21.5 %collective-permute-start.15 = (bf16[512,512]{1,0:T(8,128)(2,1)S(1)}, bf16[512,512]{1,0:T(8,128)(2,1)S(1)}, u32[]{:S(2)}, u32[]{:S(2)}) collective-permute-start(bf16[512,512]{1,0:T(8,128)(2,1)S(1)} %collective-permute-done.13.refs_7_), channel_id=1, source_target_pairs={{0,4},{4,0},{8,12},{12,8},{1,5},{5,1},{9,13},{13,9},{2,6},{6,2},{1... | collective-permute-start | bytes 1572872 | tf_op jit(solution)/shard_map/ppermute | solution.py:22
  88.1 24.6 %collective-permute-start.24 = (bf16[512,512]{1,0:T(8,128)(2,1)S(1)}, bf16[512,512]{1,0:T(8,128)(2,1)S(1)}, u32[]{:S(2)}, u32[]{:S(2)}) collective-permute-start(bf16[512,512]{1,0:T(8,128)(2,1)S(1)} %copy-done.11), channel_id=1, source_target_pairs={{0,8},{4,12},{8,0},{12,4},{1,9},{5,13},{9,1},{13,5},{2,10},{6,14},... | collective-permute-start | bytes 1572872 | tf_op jit(solution)/shard_map/ppermute | solution.py:22
  88.9 24.5 %collective-permute-start.8 = (bf16[96,2048]{1,0:T(8,128)(2,1)S(1)}, bf16[96,2048]{1,0:T(8,128)(2,1)S(1)}, u32[]{:S(2)}, u32[]{:S(2)}) collective-permute-start(bf16[96,2048]{1,0:T(8,128)(2,1)S(1)} %fusion.11), channel_id=1, source_target_pairs={{0,2},{1,3},{2,0},{3,1},{4,6},{5,7},{6,4},{7,5},{8,10},{9,11},{10,... | collective-permute-start | bytes 1179656 | tf_op jit(solution)/shard_map/ppermute | solution.py:22
  97.6 22.8 %collective-permute-start.17 = (bf16[512,512]{1,0:T(8,128)(2,1)S(1)}, bf16[512,512]{1,0:T(8,128)(2,1)S(1)}, u32[]{:S(2)}, u32[]{:S(2)}) collective-permute-start(bf16[512,512]{1,0:T(8,128)(2,1)S(1)} %collective-permute-done.16.refs_10_), channel_id=1, source_target_pairs={{0,4},{4,0},{8,12},{12,8},{1,5},{5,1},{9,13},{13,9},{2,6},{6,2},{1... | collective-permute-start | bytes 1572872 | tf_op jit(solution)/shard_map/ppermute | solution.py:22
  100.5 19.9 %collective-permute-start.22 = (bf16[512,512]{1,0:T(8,128)(2,1)S(1)}, bf16[512,512]{1,0:T(8,128)(2,1)S(1)}, u32[]{:S(2)}, u32[]{:S(2)}) collective-permute-start(bf16[512,512]{1,0:T(8,128)(2,1)S(1)} %collective-permute-done.15.refs_8_), channel_id=1, source_target_pairs={{0,16},{16,0},{1,17},{17,1},{2,18},{18,2},{3,19},{19,3},{4,20},{20... | collective-permute-start | bytes 1572872 | tf_op jit(solution)/shard_map/ppermute | solution.py:22
  112.7 15.5 %collective-permute-start.25 = (bf16[512,512]{1,0:T(8,128)(2,1)S(1)}, bf16[512,512]{1,0:T(8,128)(2,1)S(1)}, u32[]{:S(2)}, u32[]{:S(2)}) collective-permute-start(bf16[512,512]{1,0:T(8,128)(2,1)S(1)} %copy-done.9), channel_id=1, source_target_pairs={{0,4},{4,0},{8,12},{12,8},{1,5},{5,1},{9,13},{13,9},{2,6},{6,2},{1... | collective-permute-start | bytes 1572872 | tf_op jit(solution)/shard_map/ppermute | solution.py:22
  131.6 18.2 %collective-permute-start.27 = (bf16[512,512]{1,0:T(8,128)(2,1)S(1)}, bf16[512,512]{1,0:T(8,128)(2,1)S(1)}, u32[]{:S(2)}, u32[]{:S(2)}) collective-permute-start(bf16[512,512]{1,0:T(8,128)(2,1)S(1)} %collective-permute-done.25.refs_0_), channel_id=1, source_target_pairs={{0,16},{16,0},{1,17},{17,1},{2,18},{18,2},{3,19},{19,3},{4,20},{20... | collective-permute-start | bytes 1572872 | tf_op jit(solution)/shard_map/ppermute | solution.py:22
  132.4 15.1 %collective-permute-start.32 = (bf16[96,2048]{1,0:T(8,128)(2,1)S(1)}, bf16[96,2048]{1,0:T(8,128)(2,1)S(1)}, u32[]{:S(2)}, u32[]{:S(2)}) collective-permute-start(bf16[96,2048]{1,0:T(8,128)(2,1)S(1)} %fusion.3.refs_0_), channel_id=1, source_target_pairs={{0,8},{4,12},{8,0},{12,4},{1,9},{5,13},{9,1},{13,5},{2,10},{6,14},... | collective-permute-start | bytes 1179656 | tf_op jit(solution)/shard_map/ppermute | solution.py:22
  160.0 13.9 %collective-permute-start.29 = (bf16[512,512]{1,0:T(8,128)(2,1)S(1)}, bf16[512,512]{1,0:T(8,128)(2,1)S(1)}, u32[]{:S(2)}, u32[]{:S(2)}) collective-permute-start(bf16[512,512]{1,0:T(8,128)(2,1)S(1)} %collective-permute-done.26.refs_2_), channel_id=1, source_target_pairs={{0,16},{16,0},{1,17},{17,1},{2,18},{18,2},{3,19},{19,3},{4,20},{20... | collective-permute-start | bytes 1572872 | tf_op jit(solution)/shard_map/ppermute | solution.py:22
  161.2 18.7 %collective-permute-start.9 = (bf16[96,2048]{1,0:T(8,128)(2,1)S(1)}, bf16[96,2048]{1,0:T(8,128)(2,1)S(1)}, u32[]{:S(2)}, u32[]{:S(2)}) collective-permute-start(bf16[96,2048]{1,0:T(8,128)(2,1)S(1)} %fusion.3.refs_0_), channel_id=1, source_target_pairs={{0,1},{1,0},{2,3},{3,2},{4,5},{5,4},{6,7},{7,6},{8,9},{9,8},{10,11... | collective-permute-start | bytes 1179656 | tf_op jit(solution)/shard_map/ppermute | solution.py:22
  164.2 15.7 %collective-permute-start.11 = (bf16[96,2048]{1,0:T(8,128)(2,1)S(1)}, bf16[96,2048]{1,0:T(8,128)(2,1)S(1)}, u32[]{:S(2)}, u32[]{:S(2)}) collective-permute-start(bf16[96,2048]{1,0:T(8,128)(2,1)S(1)} %collective-permute-done.10.refs_2_), channel_id=1, source_target_pairs={{0,1},{1,0},{2,3},{3,2},{4,5},{5,4},{6,7},{7,6},{8,9},{9,8},{10,11... | collective-permute-start | bytes 1179656 | tf_op jit(solution)/shard_map/ppermute | solution.py:22
  196.3 16.3 %collective-permute-start.31 = (bf16[96,2048]{1,0:T(8,128)(2,1)S(1)}, bf16[96,2048]{1,0:T(8,128)(2,1)S(1)}, u32[]{:S(2)}, u32[]{:S(2)}) collective-permute-start(bf16[96,2048]{1,0:T(8,128)(2,1)S(1)} %fusion.8), channel_id=1, source_target_pairs={{0,2},{1,3},{2,0},{3,1},{4,6},{5,7},{6,4},{7,5},{8,10},{9,11},{10,... | collective-permute-start | bytes 1179656 | tf_op jit(solution)/shard_map/ppermute | solution.py:22
  205.2 18.7 %collective-permute-start.38 = (bf16[96,2048]{1,0:T(8,128)(2,1)S(1)}, bf16[96,2048]{1,0:T(8,128)(2,1)S(1)}, u32[]{:S(2)}, u32[]{:S(2)}) collective-permute-start(bf16[96,2048]{1,0:T(8,128)(2,1)S(1)} %fusion.7), channel_id=1, source_target_pairs={{0,8},{4,12},{8,0},{12,4},{1,9},{5,13},{9,1},{13,5},{2,10},{6,14},... | collective-permute-start | bytes 1179656 | tf_op jit(solution)/shard_map/ppermute | solution.py:22
  (40 other events, 548.4 us)

commit v3 on v0

v3 whole, which is shorter than its diff:
```python
import math

import jax
import jax.numpy as jnp
import numpy as np
from jax import lax
from jax.experimental import pallas as pl
from jax.experimental.pallas import tpu as pltpu
from jax.sharding import PartitionSpec as P

HEAD_DIM = 128
EPSILON = 1e-05
ROPE_BASE = 10000.0
VMEM_LIMIT = 60 * 1024 * 1024
TILE = 256
MASKED = -1e30
FAR_PARTS = 4
MEMBER, WITHIN, MINE, LEAVING, SOURCE = range(5)


def swap(value, axis, mask):
    pairs = [(source, source ^ mask) for source in range(lax.axis_size(axis))]
    return lax.ppermute(value, axis, pairs)


def layer_norm(rows):
    center = rows - jnp.mean(rows, axis=-1, keepdims=True)
    spread = jnp.mean(center * center, axis=-1, keepdims=True)
    return center * lax.rsqrt(spread + EPSILON)


def vmem():
    return pl.BlockSpec(memory_space=pltpu.VMEM)


def smem():
    return pl.BlockSpec(memory_space=pltpu.SMEM)


def anywhere():
    return pl.BlockSpec(memory_space=pl.ANY)


def params():
    return pltpu.CompilerParams(vmem_limit_bytes=VMEM_LIMIT)


def cost(gate=True):
    return pl.CostEstimate(flops=10**11 if gate else 0, bytes_accessed=0, transcendentals=0)


def prepare(info, tokens, entries, *weights):
    rows, columns = entries.shape
    stack, depth, width = len(weights), weights[0].shape[0], weights[0].shape[1] // 4

    def body(info_ref, token_ref, entry_ref, *refs):
        sources, normed, blocks = refs[:stack], refs[stack], refs[stack + 1 : stack + 5]
        outs, sems = refs[stack + 5 : -1], refs[-1]
        copies = cut_copies(info_ref, sources, outs, sems)
        part = blocks[0].shape[1] // 2
        for mask, out in enumerate(blocks):
            begin = pl.multiple_of((info_ref[MEMBER] ^ mask) * part, part)
            out[:, :part] = entry_ref[:, pl.ds(begin, part)]
            out[:, part:] = entry_ref[:, pl.ds(4 * part + begin, part)]
        normed[...] = layer_norm(token_ref[...].astype(jnp.float32)).astype(jnp.bfloat16)
        for copy in copies:
            copy.wait()

    return pl.pallas_call(
        body,
        in_specs=[smem(), vmem(), vmem()] + [anywhere()] * stack,
        out_specs=[vmem()] * 7,
        out_shape=[jax.ShapeDtypeStruct(tokens.shape, jnp.bfloat16)]
        + [jax.ShapeDtypeStruct((rows, columns // 4), jnp.bfloat16)] * 4
        + [jax.ShapeDtypeStruct((stack * depth, width), jnp.bfloat16)] * 2,
        scratch_shapes=[pltpu.SemaphoreType.DMA((2, stack))],
        compiler_params=params(),
        cost_estimate=cost(False),
    )(info, tokens, entries, *weights)


def cut_copies(info, sources, outs, sems):
    rows = sources[0].shape[0]
    width = outs[0].shape[1]
    copies = []
    for at, out in enumerate(outs):
        there = pl.ds(pl.multiple_of(info[(LEAVING, MINE)[at]] * width, width), width)
        for which, source in enumerate(sources):
            place = out.at[pl.ds(which * rows, rows), :]
            copies.append(pltpu.make_async_copy(source.at[:, there], place, sems.at[at, which]))
    for copy in copies:
        copy.start()
    return copies


def cut(info, *weights):
    rows, columns = weights[0].shape
    width = columns // 4
    count, stack = 2, len(weights)

    def body(info_ref, *refs):
        for copy in cut_copies(info_ref, refs[:stack], refs[stack:-1], refs[-1]):
            copy.wait()

    return pl.pallas_call(
        body,
        in_specs=[smem()] + [anywhere()] * stack,
        out_specs=[vmem()] * count,
        out_shape=[jax.ShapeDtypeStruct((stack * rows, width), jnp.bfloat16)] * count,
        scratch_shapes=[pltpu.SemaphoreType.DMA((count, stack))],
        compiler_params=params(),
        cost_estimate=cost(False),
    )(info, *weights)


def project_body(n0, n1, n2, n3, cosine, sine, wq, wk, wv, q_ref, k_ref, v_ref, rows):
    count = n0.shape[0]

    @pl.when(pl.program_id(0) == 0)
    def _():
        for at, part in enumerate((n0, n1, n2, n3)):
            rows[pl.ds(at * count, count), :] = part[...]

    x = rows[...]
    width = wq.shape[1]
    for weight, out, turned in ((wq, q_ref, True), (wk, k_ref, True), (wv, v_ref, False)):
        product = jnp.dot(x, weight[...], preferred_element_type=jnp.float32)
        if not turned:
            out[...] = product.astype(jnp.bfloat16)
            continue
        for at in range(0, width, HEAD_DIM):
            head = product[:, at : at + HEAD_DIM]
            other = pltpu.roll(head, HEAD_DIM // 2, 1)
            out[:, at : at + HEAD_DIM] = (head * cosine[...] + other * sine[...]).astype(
                jnp.bfloat16
            )


def project(parts, cosine, sine, wq, wk, wv):
    count, depth = parts[0].shape
    rows, width = 4 * count, wq.shape[1]
    whole = lambda shape: pl.BlockSpec(shape, lambda i: (0, 0))
    column = pl.BlockSpec((depth, TILE), lambda i: (0, i))
    out = pl.BlockSpec((rows, TILE), lambda i: (0, i))
    shape = jax.ShapeDtypeStruct((rows, width), jnp.bfloat16)
    return pl.pallas_call(
        project_body,
        grid=(width // TILE,),
        in_specs=[whole((count, depth))] * 4 + [whole((rows, HEAD_DIM))] * 2 + [column] * 3,
        out_specs=[out] * 3,
        out_shape=[shape] * 3,
        scratch_shapes=[pltpu.VMEM((rows, depth), jnp.bfloat16)],
        compiler_params=params(),
        cost_estimate=cost(False),
    )(*parts, cosine, sine, wq, wk, wv)


def attend_body(traded, q, k, v, *refs):
    own, came, refs = refs[:4], refs[4:8], refs[8:]
    of_row, of_column, wo, near, refs = refs[0], refs[1], refs[2], refs[3], refs[4:]
    far, (mixed, cached, weight, sems) = refs[:-4], refs[-4:]
    load = pltpu.make_async_copy(wo, weight, sems.at[4])
    count = own[0].shape[0]

    def fetch(blocks):
        copies = [
            pltpu.make_async_copy(block, cached.at[pl.ds(at * count, count), :], sems.at[at])
            for at, block in enumerate(blocks)
        ]
        for copy in copies:
            copy.start()
        load.start()
        for copy in copies:
            copy.wait()

    @pl.when(traded[0] == 1)
    def _():
        fetch(came)

    @pl.when(traded[0] != 1)
    def _():
        fetch(own)

    rows, width = q.shape
    heads = width // HEAD_DIM
    low, high = of_row[:, 0:1], of_row[:, 1:2]
    first, place = of_row[:, 2:3], of_row[:, 3:4]
    column = of_column[0:1, :]
    fresh = of_column[1:2, :rows]
    on_cached = (column >= low) & (column < high)
    on_fresh = (fresh >= first) & (fresh <= place)
    scale = 1.0 / math.sqrt(HEAD_DIM)
    contract_last = (((1,), (1,)), ((), ()))
    for head in range(heads):
        at = slice(head * HEAD_DIM, (head + 1) * HEAD_DIM)
        after = slice(width + head * HEAD_DIM, width + (head + 1) * HEAD_DIM)
        query = q[:, at]
        old = lax.dot_general(
            query, cached[:, at], contract_last, preferred_element_type=jnp.float32
        )
        new = lax.dot_general(query, k[:, at], contract_last, preferred_element_type=jnp.float32)
        old = jnp.where(on_cached, old * scale, MASKED)
        new = jnp.where(on_fresh, new * scale, MASKED)
        top = jnp.maximum(
            jnp.max(old, axis=-1, keepdims=True), jnp.max(new, axis=-1, keepdims=True)
        )
        old = jnp.exp(old - top)
        new = jnp.exp(new - top)
        share = 1.0 / (jnp.sum(old, axis=-1, keepdims=True) + jnp.sum(new, axis=-1, keepdims=True))
        sums = jnp.dot(
            (old * share).astype(jnp.bfloat16), cached[:, after], preferred_element_type=jnp.float32
        ) + jnp.dot(
            (new * share).astype(jnp.bfloat16), v[:, at], preferred_element_type=jnp.float32
        )
        mixed[:, at] = sums.astype(jnp.bfloat16)
    load.wait()
    left = mixed[...]
    for at in range(0, near.shape[1], TILE):
        part = jnp.dot(left, weight[:, at : at + TILE], preferred_element_type=jnp.float32)
        split_rows(part, at, near, far)


def split_rows(part, at, near, far):
    count, width = part.shape[0] // 4, far[0].shape[1]
    far, there = far[at // width], at % width
    near[:count, at : at + TILE] = part[:count]
    near[count:, at : at + TILE] = part[2 * count : 3 * count]
    far[:count, there : there + TILE] = part[count : 2 * count].astype(jnp.bfloat16)
    far[count:, there : there + TILE] = part[3 * count :].astype(jnp.bfloat16)


def split_shapes(rows, depth):
    return [jax.ShapeDtypeStruct((rows // 2, depth), jnp.float32)] + [
        jax.ShapeDtypeStruct((rows // 2, depth // FAR_PARTS), jnp.bfloat16)
    ] * FAR_PARTS


def attend(traded, q, k, v, own, came, of_row, of_column, wo):
    rows, width = q.shape
    depth = wo.shape[1]
    cached = of_column.shape[1]
    keys = cached + rows
    return pl.pallas_call(
        attend_body,
        in_specs=[smem()] + [vmem()] * 3 + [anywhere()] * 8 + [vmem()] * 2 + [anywhere()],
        out_specs=[vmem()] * (1 + FAR_PARTS),
        out_shape=split_shapes(rows, depth),
        scratch_shapes=[
            pltpu.VMEM((rows, width), jnp.bfloat16),
            pltpu.VMEM((cached, 2 * width), jnp.bfloat16),
            pltpu.VMEM(wo.shape, jnp.bfloat16),
            pltpu.SemaphoreType.DMA((5,)),
        ],
        compiler_params=params(),
        cost_estimate=cost(False),
    )(traded, q, k, v, *own, *came, of_row, of_column, wo)


def load_pieces(masks, info, wholes, pieces, held, sems):
    shard, width = wholes[0].shape[0], pieces[0].shape[1]
    columns = pl.ds(pl.multiple_of(info[MINE] * width, width), width)
    copies = []
    for at, mask in enumerate(masks):
        there = pl.ds(pl.multiple_of((info[WITHIN] ^ mask) * shard, shard), shard)
        for which, whole in enumerate(wholes):
            source = pieces[at - 1].at[pl.ds(which * shard, shard), :] if at else whole.at[:, columns]
            place = held.at[which, there, :]
            copies.append(pltpu.make_async_copy(source, place, sems.at[at, which]))
    for copy in copies:
        copy.start()
    return copies


def gate_up(masks, info, parts, gate, up, arrived):
    count, depth = parts[0].shape
    rows = len(parts) * count
    blocks, pieces = len(parts), len(arrived)
    width = arrived[0].shape[1]

    def body(info_ref, *refs):
        part_refs, refs = refs[:blocks], refs[blocks:]
        wholes, refs = refs[:2], refs[2:]
        piece_refs, refs = refs[:pieces], refs[pieces:]
        act_refs, (x, held, sems) = refs[:-3], refs[-3:]
        copies = load_pieces(masks, info_ref, wholes, piece_refs, held, sems)
        for at, block in enumerate(part_refs):
            x[pl.ds(at * count, count), :] = block[...]
        for copy in copies:
            copy.wait()
        for at in range(0, width, TILE):
            g = jnp.dot(x[...], held[0, :, at : at + TILE], preferred_element_type=jnp.float32)
            u = jnp.dot(x[...], held[1, :, at : at + TILE], preferred_element_type=jnp.float32)
            act = (g / (1.0 + jnp.exp(-g)) * u).astype(jnp.bfloat16)
            for group, act_ref in enumerate(act_refs):
                act_ref[:, at : at + TILE] = act[group * 4 * count : (group + 1) * 4 * count]

    return pl.pallas_call(
        body,
        in_specs=[smem()] + [vmem()] * blocks + [anywhere()] * (2 + pieces),
        out_specs=[vmem()] * (blocks // 4),
        out_shape=[jax.ShapeDtypeStruct((4 * count, width), jnp.bfloat16)] * (blocks // 4),
        scratch_shapes=[
            pltpu.VMEM((rows, depth), jnp.bfloat16),
            pltpu.VMEM((2, depth, width), jnp.bfloat16),
            pltpu.SemaphoreType.DMA((pieces + 1, 2)),
        ],
        compiler_params=params(),
        cost_estimate=cost(False),
    )(info, *parts, gate, up, *arrived)


def down_rows(masks, info, acts, down, arrived):
    rows, width = acts[0].shape
    groups, parts, pieces = len(acts), 1 + FAR_PARTS, len(arrived)
    depth = arrived[0].shape[0] * len(masks)

    def body(info_ref, *refs):
        act_refs, down_ref, refs = refs[:groups], refs[groups], refs[groups + 1 :]
        piece_refs, outs, (held, sems) = refs[:pieces], refs[pieces:-2], refs[-2:]
        for copy in load_pieces(masks, info_ref, [down_ref], piece_refs, held, sems):
            copy.wait()
        for group, act in enumerate(act_refs):
            near, *far = outs[group * parts : (group + 1) * parts]
            for at in range(0, depth, TILE):
                part = lax.dot_general(
                    act[...],
                    held[0, at : at + TILE, :],
                    (((1,), (1,)), ((), ())),
                    preferred_element_type=jnp.float32,
                )
                split_rows(part, at, near, far)

    sums = pl.pallas_call(
        body,
        in_specs=[smem()] + [vmem()] * groups + [anywhere()] * (1 + pieces),
        out_specs=[vmem()] * (groups * parts),
        out_shape=split_shapes(rows, depth) * groups,
        scratch_shapes=[
            pltpu.VMEM((1, depth, width), jnp.bfloat16),
            pltpu.SemaphoreType.DMA((pieces + 1, 1)),
        ],
        compiler_params=params(),
        cost_estimate=cost(False),
    )(info, *acts, down, *arrived)
    return [sums[at * parts : (at + 1) * parts] for at in range(groups)]


def gather_rows(rows, across=None):
    if across is None:
        across = swap(rows, "mp", 2)
    return [rows, swap(rows, "mp", 1), across, swap(across, "mp", 1)]


def over_core(parts):
    return [parts[0]] + [swap(part, "mp", 1) for part in parts[1:]]


def reduce_rows(near, *came, split=1):
    count = near.shape[0] // 2
    each = len(came) // split
    kept, sent = [], []
    for at in range(0, len(came), each):
        both = jnp.concatenate(came[at : at + each], axis=1).astype(jnp.float32)
        begin = at * came[0].shape[1]
        both = both + near[:, begin : begin + both.shape[1]]
        kept.append(both)
        sent.append(both[count:].astype(jnp.bfloat16))
    return kept, [swap(going, "mp", 2) for going in sent], sent


def over_cores(near, *far):
    came = jnp.concatenate([swap(part, "mp", 1) for part in far], axis=1)
    return near + came.astype(jnp.float32)


def total(kept, came):
    return [part[: more.shape[0]] + more.astype(jnp.float32) for part, more in zip(kept, came)]


def after(value, *earlier):
    return lax.optimization_barrier((value,) + earlier)[0] if earlier else value


def without(held, mask):
    return {at: piece for at, piece in held.items() if at != mask}


def join(*values):
    return lax.optimization_barrier(values)


def over_bits(held, bits):
    for bit in bits:
        held.update({mask ^ bit: swap(piece, "dp", bit) for mask, piece in list(held.items())})
    return held


def facts_body(info, lengths, requests, frequency, cosine, sine, of_row, of_column):
    rows = requests.shape[1]
    member, source = info[MEMBER], info[SOURCE]

    def places(size, axis, shape):
        at = lax.broadcasted_iota(jnp.int32, shape, axis)
        step = size // 4
        block = sum((at >= edge).astype(jnp.int32) for edge in (step, 2 * step, 3 * step))
        return at + ((member ^ block) - block) * step

    place = places(rows, 0, (rows, 1))
    request = requests[...]
    first, low = jnp.zeros_like(place), jnp.zeros_like(place)
    begin = lengths[source, 0]
    length = jnp.zeros_like(place) + begin
    for label in range(1, lengths.shape[1]):
        start = jnp.sum((request < label).astype(jnp.int32), axis=1, keepdims=True)
        reached = place >= start
        first = jnp.where(reached, start, first)
        low = jnp.where(reached, begin, low)
        length = jnp.where(reached, lengths[source, label], length)
        begin = begin + lengths[source, label]
    angle = (length + place - first).astype(jnp.float32) * frequency[...]
    cosine[...] = jnp.cos(angle)
    lane = lax.broadcasted_iota(jnp.int32, (1, HEAD_DIM), 1)
    sine[...] = jnp.sin(angle) * jnp.where(lane < HEAD_DIM // 2, -1.0, 1.0)
    column = lax.broadcasted_iota(jnp.int32, of_row.shape, 1)
    of_row[...] = jnp.where(
        column == 0, low, jnp.where(column == 1, low + length, jnp.where(column == 2, first, place))
    )
    of_column[0:1, :] = places(of_column.shape[1], 1, (1, of_column.shape[1]))
    of_column[1:2, :] = places(rows, 1, (1, of_column.shape[1]))


def row_facts(info, lengths, requests, cached):
    rows = requests.shape[1]
    half = HEAD_DIM // 2
    frequency = ROPE_BASE ** (-np.arange(half, dtype=np.float32) / np.float32(half))
    frequency = jnp.asarray(np.concatenate([frequency, frequency])[None], jnp.float32)
    turn = jax.ShapeDtypeStruct((rows, HEAD_DIM), jnp.float32)
    return pl.pallas_call(
        facts_body,
        in_specs=[smem(), smem(), vmem(), vmem()],
        out_specs=[vmem()] * 4,
        out_shape=[
            turn,
            turn,
            jax.ShapeDtypeStruct((rows, 8), jnp.int32),
            jax.ShapeDtypeStruct((8, cached), jnp.int32),
        ],
        compiler_params=params(),
        cost_estimate=cost(True),
    )(info, lengths, requests, frequency)


def finish_body(tokens, *refs):
    parts, (state, normed) = refs[:-2], refs[-2:]
    count = len(parts) // 2
    sums = jnp.concatenate(
        [
            parts[at][: tokens.shape[0], :] + parts[count + at][...].astype(jnp.float32)
            for at in range(count)
        ],
        axis=1,
    )
    rows = (tokens[...].astype(jnp.float32) + sums).astype(jnp.bfloat16)
    state[...] = rows
    normed[...] = layer_norm(rows.astype(jnp.float32)).astype(jnp.bfloat16)


def finish(tokens, kept, came):
    shape = jax.ShapeDtypeStruct(tokens.shape, jnp.bfloat16)
    return pl.pallas_call(
        finish_body,
        in_specs=[vmem()] * (1 + len(kept) + len(came)),
        out_specs=[vmem()] * 2,
        out_shape=[shape] * 2,
        compiler_params=params(),
        cost_estimate=cost(False),
    )(tokens, *kept, *came)


def local(
    tokens,
    request_ids,
    cache_entries,
    cached_lengths,
    traded,
    query_weight,
    key_weight,
    value_weight,
    output_weight,
    gate_weight,
    up_weight,
    down_weight,
):
    replica = lax.axis_index("rep")
    within = lax.axis_index("dp")
    member = lax.axis_index("mp")
    planes = lax.axis_size("dp")
    pair = planes // 2
    bits = [1 << at for at in range(planes.bit_length() - 1) if 1 << at != pair]
    place = (within // pair) % 2
    mine, leaving = 2 * place + replica, 2 * (1 - place) + replica
    source = jnp.where(traded[0] == 1, 1 - replica, replica) * planes + within
    info = jnp.stack([member, within, mine, leaving, source]).astype(jnp.int32)

    normed, *blocks, wide_leaving, wide_mine = prepare(
        info, tokens, cache_entries, gate_weight, up_weight
    )
    blocks = [blocks[0]] + [swap(blocks[mask], "mp", mask) for mask in (1, 2, 3)]
    facts = row_facts(info, cached_lengths, request_ids, 4 * cache_entries.shape[0])
    down_cut = cut(info, after(down_weight, wide_mine))
    came = [swap(block, "rep", 1) for block in blocks[:2]]
    came, blocks, facts, down_cut = join(came, blocks, facts, down_cut)
    came += [swap(block, "rep", 1) for block in blocks[2:]]
    parts = gather_rows(normed)

    def near_side(piece):
        return without(over_bits({0: piece}, bits), 0)

    def across(piece):
        return {pair: swap(piece, "dp", pair)}

    def far_side(held):
        return without(over_bits(dict(held), bits), pair)

    wide = {**across(wide_leaving), **near_side(wide_mine)}

    q, k, v = project(parts, facts[0], facts[1], query_weight, key_weight, value_weight)
    came, q = join(came, q)
    near, *far = attend(traded, q, k, v, blocks, came, facts[2], facts[3], output_weight)
    far = [swap(part, "mp", 1) for part in far]
    far, wide = join(far, wide)
    kept, came, _ = reduce_rows(near, *far, split=2)
    wide.update(far_side({pair: wide[pair]}))
    state_own, normed_own = finish(tokens, kept, came)

    rows_z = swap(normed_own, "dp", pair)
    rows_x = swap(normed_own, "rep", 1)
    over_chip = swap(rows_x, "mp", 2)
    rows_z, wide, over_chip = join(rows_z, wide, over_chip)
    parts = gather_rows(normed_own) + gather_rows(rows_x, over_chip)
    rows_both = swap(rows_z, "rep", 1)
    back = {**across(after(down_cut[0], rows_z)), **near_side(after(down_cut[1], rows_z))}
    parts += gather_rows(rows_z)
    masks = [0] + list(wide)
    in_order = lambda held: [held[mask] for mask in masks[1:]]
    acts = gate_up(masks, info, parts, gate_weight, up_weight, in_order(wide))
    acts, back = join(acts, back)
    back.update(far_side({pair: back[pair]}))
    parts = gather_rows(rows_both)
    parts[0] = after(parts[0], acts[0])
    acts += gate_up(masks, info, parts, gate_weight, up_weight, in_order(wide))

    def sums_of(*groups):
        return down_rows(masks, info, groups, down_weight, in_order(back))

    def crossed(value, axis, mask):
        return swap(value.astype(jnp.bfloat16), axis, mask).astype(jnp.float32)

    found_both, found_z = sums_of(acts[3], acts[2])
    kept, came, sent = reduce_rows(*over_core(found_both))
    kept_z, came_z, sent_z = reduce_rows(*over_core(found_z))
    found_x, found = sums_of(after(acts[1], *sent, *sent_z), acts[0])
    came, found_x, found = join(came, found_x, found)
    (of_both,), (of_z,) = total(kept, came), total(kept_z, came_z)
    sent = (of_z + crossed(of_both, "rep", 1)).astype(jnp.bfloat16)
    of_z = swap(sent, "dp", pair).astype(jnp.float32)
    (of_x,) = total(*reduce_rows(*over_core(found_x))[:2])
    (of_own,) = total(*reduce_rows(*over_core(found))[:2])
    of_x = after(of_x, sent)
    columns = of_x.shape[1]
    of_x = [crossed(of_x[:, at : at + columns // 2], "rep", 1) for at in (0, columns // 2)]
    of_own = of_own + jnp.concatenate(of_x, axis=1)
    return (state_own.astype(jnp.float32) + (of_own + of_z)).astype(jnp.bfloat16)


def solution(mesh):
    in_specs = (
        P(("rep", "dp", "mp"), None),
        P(("rep", "dp"), None),
        P(("rep", "dp", "mp"), None),
        P(),
        P("dp"),
        P(None, "mp"),
        P(None, "mp"),
        P(None, "mp"),
        P("mp", None),
        P("dp", "mp"),
        P("dp", "mp"),
        P("dp", "mp"),
    )
    out_specs = P(("rep", "dp", "mp"), None)
    return jax.shard_map(local, mesh=mesh, in_specs=in_specs, out_specs=out_specs, check_vma=False)
```

time: 674 us -> 219 us (0.32)
  waiting for transfers between devices: 569 us -> 97.3 us
  Pallas kernels: 0 us -> 56.4 us
  starting transfers between devices: 6.98 us -> 49.9 us
  matrix products: 41 us -> 0 us
  local copies, waits for them, and re-layouts: 26.4 us -> 5.71 us
  between operations: 14.3 us -> 1.16 us
  other arithmetic: 16.2 us -> 7.6 us
    all_gather x5 -> x0, waiting for transfers between devices: 459 us -> none  [the longest x1 151 us: local(): gate = add_rows(lax.all_gather(gate_weight, 'dp', axis=0, tiled=True))]
    ppermute x1 -> x61, waiting for transfers between devices: 20.3 us -> 97.3 us  [swap(): return lax.ppermute(value, axis, pairs)]
    reduce_scatter x2 -> x0, waiting for transfers between devices: 75.9 us -> none  [the longest x1 39.6 us: local(): lax.psum_scatter(jnp.dot(mixed, output_weight, preferred_element_type=jnp...]
    pallas_call x0 -> x10, Pallas kernels: none -> 56.4 us  [the longest x2 17 us: gate_up(): pl.pallas_call(body, in_specs=[smem()] + [vmem()] * blocks + [anywhere()]...]
    ppermute x1 -> x61, starting transfers between devices: 3 us -> 49.9 us  [swap(): return lax.ppermute(value, axis, pairs)]
    dot_general x8 -> x0, matrix products: 41 us -> none  [the longest x1 15.9 us: local(): lax.dot_general(activated, lax.all_gather(down_weight, 'dp', axis=0, tile...]
    reshape x4 -> x0, local copies, waits for them, and re-layouts: 15 us -> none  [the longest x1 9.46 us: local(): stored.reshape(stored.shape[0], 2, D)]
    all_to_all x1 -> x0, waiting for transfers between devices: 12 us -> none  [local(): lax.all_to_all(stored.reshape(stored.shape[0], 2, D), 'mp', split_axis=2,...]
  transfers between devices with their start and end apart: 9 -> 61, of which waited for: 8 -> 31; matrix products, arithmetic and copies ran while one was open for 5% -> 3% of each run, Pallas kernels for 0% -> 21%
where the time goes in v3:
time: 219 us; the launch traced here: 218 us
  waiting for transfers between devices  97.3 us (44%)
  Pallas kernels  56.4 us (26%)
  starting transfers between devices  49.9 us (23%)
  other arithmetic  7.6 us (3%)
  local copies, waits for them, and re-layouts  5.71 us (3%)
    ppermute x61, waiting for transfers between devices, swap(): return lax.ppermute(value, axis, pairs)  97.3 us
    ppermute x61, starting transfers between devices, swap(): return lax.ppermute(value, axis, pairs)  49.9 us
    pallas_call x2, Pallas kernels, gate_up(): pl.pallas_call(body, in_specs=[smem()] + [vmem()] * blocks + [anywhere()]...  17 us
    pallas_call x2, Pallas kernels, down_rows(): pl.pallas_call(body, in_specs=[smem()] + [vmem()] * groups + [anywhere()]...  11.6 us
    pallas_call x1, Pallas kernels, attend(): pl.pallas_call(attend_body, in_specs=[smem()] + [vmem()] * 3 + [anywhere(...  8.25 us
    pallas_call x1, Pallas kernels, project(): pl.pallas_call(project_body, grid=(width // TILE,), in_specs=[whole((coun...  6.58 us
    unnamed x70, local copies, waits for them, and re-layouts  4.89 us
    pallas_call x1, Pallas kernels, prepare(): pl.pallas_call(body, in_specs=[smem(), vmem(), vmem()] + [anywhere()] * s...  4.73 us
  transfers between devices with their start and end apart: 61, of which 31 were waited for; matrix products, arithmetic and copies ran while one was open for 3% of the time, Pallas kernels for 21%

profile of v3, /device:TPU:0, one launch (start us, length us, event | category | flops | bytes accessed | tf_op | source)
XLA Modules:
  0.0 218.1 jit_solution(11060614665513437202)
XLA Ops:
  1.2 4.7 %shard_map.127 = (bf16[96,2048]{1,0:T(8,128)(2,1)}, bf16[128,1024]{1,0:T(8,128)(2,1)}, bf16[128,1024]{1,0:T(8,128)(2,1)}, bf16[128,1024]{1,0:T(8,128)(2,1)}, bf1...) custom-call(s32[5]{0:T(128)} %stack.23.info_ref.info, bf16[96,2048]{1,0:T(8,128)(2,1)} %tokens.1, ...), custom_call_target="tpu_custom_call" | custom-call | tf_op jit(solution)/shard_map/pallas_call | solution.py:69
  6.0 3.0 %collective-permute-start.8 = (bf16[96,2048]{1,0:T(8,128)(2,1)}, bf16[96,2048]{1,0:T(8,128)(2,1)S(1)}, u32[]{:S(2)}, u32[]{:S(2)}) collective-permute-start(bf16[96,2048]{1,0:T(8,128)(2,1)} %get-tuple-element.117.n0), channel_id=1, source_target_pairs={{0,2},{1,3},{2,0},{3,1},{4,6},{5,7},{6,4},{7,5},{8,10},{9,11},{10,... | collective-permute-start | bytes 1179656 | tf_op jit(solution)/shard_map/ppermute | solution.py:23
  12.4 12.4 %collective-permute-done.3.refs_2_ = bf16[128,1024]{1,0:T(8,128)(2,1)S(1)} collective-permute-done((bf16[128,1024]{1,0:T(8,128)(2,1)}, bf16[128,1024]{1,0:T(8,128)(2,1)S(1)}, u32[]{:S(2)}, u32[]{:S(2)}) %collective-permute-start.3) | collective-permute-done | bytes 262176 | tf_op jit(solution)/shard_map/ppermute | solution.py:23
  24.8 3.1 %collective-permute-start.15 = (bf16[1024,512]{1,0:T(8,128)(2,1)}, bf16[1024,512]{1,0:T(8,128)(2,1)S(1)}, u32[]{:S(2)}, u32[]{:S(2)}) collective-permute-start(bf16[1024,512]{1,0:T(8,128)(2,1)} %get-tuple-element.136), channel_id=1, source_target_pairs={{0,8},{4,12},{8,0},{12,4},{1,9},{5,13},{9,1},{13,5},{2,10},{6,14},... | collective-permute-start | bytes 3145736 | tf_op jit(solution)/shard_map/ppermute | solution.py:23
  42.3 6.6 %shard_map.130 = (bf16[384,512]{1,0:T(8,128)(2,1)}, bf16[384,512]{1,0:T(8,128)(2,1)}, bf16[384,512]{1,0:T(8,128)(2,1)}) custom-call(bf16[96,2048]{1,0:T(8,128)(2,1)} %get-tuple-element.117.n0, bf16[96,2048]{1,0:T(8,128)(2,1)} %copy-done.20, bf16[96,2048]{1,0:T(8,128)(2,1)} %copy-done.15, bf16[96,2048]{1,0:T(8,128)(2,1)} %copy-done.23, ...), custom_call_target="tpu_custom_call" | custom-call | tf_op jit(solution)/shard_map/pallas_call | solution.py:146
  48.9 4.0 %collective-permute-done.6.refs_7_ = bf16[128,1024]{1,0:T(8,128)(2,1)} collective-permute-done((bf16[128,1024]{1,0:T(8,128)(2,1)S(1)}, bf16[128,1024]{1,0:T(8,128)(2,1)}, u32[]{:S(2)}, u32[]{:S(2)}) %collective-permute-start.6) | collective-permute-done | bytes 262176 | tf_op jit(solution)/shard_map/ppermute | solution.py:23
  52.8 8.3 %shard_map.131 = (f32[192,2048]{1,0:T(8,128)}, bf16[192,512]{1,0:T(8,128)(2,1)}, bf16[192,512]{1,0:T(8,128)(2,1)}, bf16[192,512]{1,0:T(8,128)(2,1)}, bf16[192,512]{1,0:T(8,128)(2,1)}) custom-call(s32[1]{0:T(128)S(6)} %copy.14.traded, bf16[384,512]{1,0:T(8,128)(2,1)} %get-tuple-element.121.q, bf16[384,512]{1,0:T(8,128)(2,1)} %get-tuple-element.122.k, ...), custom_call_target="tpu_custom_call" | custom-call | tf_op jit(solution)/shard_map/pallas_call | solution.py:243
  64.5 7.5 %collective-permute-done.15.refs_15_.refs_7_ = bf16[1024,512]{1,0:T(8,128)(2,1)S(1)} collective-permute-done((bf16[1024,512]{1,0:T(8,128)(2,1)}, bf16[1024,512]{1,0:T(8,128)(2,1)S(1)}, u32[]{:S(2)}, u32[]{:S(2)}) %collective-permute-start.15) | collective-permute-done | bytes 1048608 | tf_op jit(solution)/shard_map/ppermute | solution.py:23
  72.0 4.2 %collective-permute-done.14.refs_14_.refs_6_ = bf16[1024,512]{1,0:T(8,128)(2,1)S(1)} collective-permute-done((bf16[1024,512]{1,0:T(8,128)(2,1)}, bf16[1024,512]{1,0:T(8,128)(2,1)S(1)}, u32[]{:S(2)}, u32[]{:S(2)}) %collective-permute-start.14) | collective-permute-done | bytes 1048608 | tf_op jit(solution)/shard_map/ppermute | solution.py:23
  81.2 5.7 %collective-permute-done.16.refs_2_ = bf16[96,1024]{1,0:T(8,128)(2,1)S(1)} collective-permute-done((bf16[96,1024]{1,0:T(8,128)(2,1)S(1)}, bf16[96,1024]{1,0:T(8,128)(2,1)S(1)}, u32[]{:S(2)}, u32[]{:S(2)}) %collective-permute-start.16) | collective-permute-done | bytes 196640 | tf_op jit(solution)/shard_map/ppermute | solution.py:23
  86.9 3.2 %collective-permute-done.17.refs_3_ = bf16[96,1024]{1,0:T(8,128)(2,1)S(1)} collective-permute-done((bf16[96,1024]{1,0:T(8,128)(2,1)S(1)}, bf16[96,1024]{1,0:T(8,128)(2,1)S(1)}, u32[]{:S(2)}, u32[]{:S(2)}) %collective-permute-start.17) | collective-permute-done | bytes 196640 | tf_op jit(solution)/shard_map/ppermute | solution.py:23
  96.8 4.5 %collective-permute-start.18 = (bf16[96,2048]{1,0:T(8,128)(2,1)}, bf16[96,2048]{1,0:T(8,128)(2,1)S(1)}, u32[]{:S(2)}, u32[]{:S(2)}) collective-permute-start(bf16[96,2048]{1,0:T(8,128)(2,1)} %get-tuple-element.143.refs_0_), channel_id=1, source_target_pairs={{0,8},{4,12},{8,0},{12,4},{1,9},{5,13},{9,1},{13,5},{2,10},{6,14},... | collective-permute-start | bytes 1179656 | tf_op jit(solution)/shard_map/ppermute | solution.py:23
  106.4 11.4 %collective-permute-done.18.refs_8_ = bf16[96,2048]{1,0:T(8,128)(2,1)S(1)} collective-permute-done((bf16[96,2048]{1,0:T(8,128)(2,1)}, bf16[96,2048]{1,0:T(8,128)(2,1)S(1)}, u32[]{:S(2)}, u32[]{:S(2)}) %collective-permute-start.18) | collective-permute-done | bytes 393248 | tf_op jit(solution)/shard_map/ppermute | solution.py:23
  119.5 3.3 %collective-permute-start.32 = (bf16[512,512]{1,0:T(8,128)(2,1)}, bf16[512,512]{1,0:T(8,128)(2,1)S(1)}, u32[]{:S(2)}, u32[]{:S(2)}) collective-permute-start(bf16[512,512]{1,0:T(8,128)(2,1)} %get-tuple-element.157), channel_id=1, source_target_pairs={{0,8},{4,12},{8,0},{12,4},{1,9},{5,13},{9,1},{13,5},{2,10},{6,14},... | collective-permute-start | bytes 1572872 | tf_op jit(solution)/shard_map/ppermute | solution.py:23
  122.8 6.7 %collective-permute-done.29.refs_10_ = bf16[96,2048]{1,0:T(8,128)(2,1)S(1)} collective-permute-done((bf16[96,2048]{1,0:T(8,128)(2,1)S(1)}, bf16[96,2048]{1,0:T(8,128)(2,1)S(1)}, u32[]{:S(2)}, u32[]{:S(2)}) %collective-permute-start.29) | collective-permute-done | bytes 393248 | tf_op jit(solution)/shard_map/ppermute | solution.py:23
  132.0 10.6 %shard_map.133 = (bf16[384,512]{1,0:T(8,128)(2,1)}, bf16[384,512]{1,0:T(8,128)(2,1)}, bf16[384,512]{1,0:T(8,128)(2,1)}) custom-call(s32[5]{0:T(128)} %stack.23.info_ref.info, bf16[96,2048]{1,0:T(8,128)(2,1)} %get-tuple-element.143.refs_0_, bf16[96,2048]{1,0:T(8,128)(2,1)} %copy-done.17, bf16[96,2048]{1,0:T(8,128)(2,1)} %copy-done.12, ...), custom_call_target="tpu_custom_call" | custom-call | tf_op jit(solution)/shard_map/pallas_call | solution.py:297
  149.4 6.4 %shard_map.134.refs_0_ = bf16[384,512]{1,0:T(8,128)(2,1)} custom-call(s32[5]{0:T(128)} %stack.23.info_ref.info, bf16[96,2048]{1,0:T(8,128)(2,1)} %copy-done.14, bf16[96,2048]{1,0:T(8,128)(2,1)} %copy-done.25, bf16[96,2048]{1,0:T(8,128)(2,1)} %collective-permute-done.34.refs_2_, bf16[96,2048]{1,0:T(8,128)(2,1)} %copy-done.26, bf16[512,2048]{1,0:T(8,128)(2,1)} %refs_4_.1, ...), custom_call_target="tpu_custom_call" | custom-call | tf_op jit(solution)/shard_map/pallas_call | solution.py:297
  158.3 5.8 %shard_map.135 = (f32[192,2048]{1,0:T(8,128)}, bf16[192,512]{1,0:T(8,128)(2,1)}, bf16[192,512]{1,0:T(8,128)(2,1)}, bf16[192,512]{1,0:T(8,128)(2,1)}, bf16[192,51...) custom-call(s32[5]{0:T(128)} %stack.23.info_ref.info, ...), custom_call_target="tpu_custom_call" | custom-call | tf_op jit(solution)/shard_map/pallas_call | solution.py:333
  170.9 5.8 %shard_map.136 = (f32[192,2048]{1,0:T(8,128)}, bf16[192,512]{1,0:T(8,128)(2,1)}, bf16[192,512]{1,0:T(8,128)(2,1)}, bf16[192,512]{1,0:T(8,128)(2,1)}, bf16[192,51...) custom-call(s32[5]{0:T(128)} %stack.23.info_ref.info, ...), custom_call_target="tpu_custom_call" | custom-call | tf_op jit(solution)/shard_map/pallas_call | solution.py:333
  176.7 3.9 %collective-permute-done.41 = bf16[96,2048]{1,0:T(8,128)(2,1)} collective-permute-done((bf16[96,2048]{1,0:T(8,128)(2,1)S(1)}, bf16[96,2048]{1,0:T(8,128)(2,1)}, u32[]{:S(2)}, u32[]{:S(2)}) %collective-permute-start.41) | collective-permute-done | bytes 393248 | tf_op jit(solution)/shard_map/ppermute | solution.py:23
  188.3 7.3 %collective-permute-done.57 = bf16[96,2048]{1,0:T(8,128)(2,1)S(1)} collective-permute-done((bf16[96,2048]{1,0:T(8,128)(2,1)S(1)}, bf16[96,2048]{1,0:T(8,128)(2,1)S(1)}, u32[]{:S(2)}, u32[]{:S(2)}) %collective-permute-start.57) | collective-permute-done | bytes 393248 | tf_op jit(solution)/shard_map/ppermute | solution.py:23
  196.7 3.3 %collective-permute-start.60 = (bf16[96,2048]{1,0:T(8,128)(2,1)S(1)}, bf16[96,2048]{1,0:T(8,128)(2,1)S(1)}, u32[]{:S(2)}, u32[]{:S(2)}) collective-permute-start(bf16[96,2048]{1,0:T(8,128)(2,1)S(1)} %fusion.2), channel_id=1, source_target_pairs={{0,8},{4,12},{8,0},{12,4},{1,9},{5,13},{9,1},{13,5},{2,10},{6,14},... | collective-permute-start | bytes 1179656 | tf_op jit(solution)/shard_map/ppermute | solution.py:23
  200.1 5.2 %collective-permute-done.55 = bf16[96,2048]{1,0:T(8,128)(2,1)S(1)} collective-permute-done((bf16[96,2048]{1,0:T(8,128)(2,1)S(1)}, bf16[96,2048]{1,0:T(8,128)(2,1)S(1)}, u32[]{:S(2)}, u32[]{:S(2)}) %collective-permute-start.55) | collective-permute-done | bytes 393248 | tf_op jit(solution)/shard_map/ppermute | solution.py:23
  207.5 5.8 %collective-permute-done.58 = bf16[96,1024]{1,0:T(8,128)(2,1)S(1)} collective-permute-done((bf16[96,1024]{1,0:T(8,128)(2,1)S(1)}, bf16[96,1024]{1,0:T(8,128)(2,1)S(1)}, u32[]{:S(2)}, u32[]{:S(2)}) %collective-permute-start.58) | collective-permute-done | bytes 196640 | tf_op jit(solution)/shard_map/ppermute | solution.py:23
  (195 shorter events, 74.3 us)
Async XLA Ops:
  6.0 26.0 %collective-permute-start.8 = (bf16[96,2048]{1,0:T(8,128)(2,1)}, bf16[96,2048]{1,0:T(8,128)(2,1)S(1)}, u32[]{:S(2)}, u32[]{:S(2)}) collective-permute-start(bf16[96,2048]{1,0:T(8,128)(2,1)} %get-tuple-element.117.n0), channel_id=1, source_target_pairs={{0,2},{1,3},{2,0},{3,1},{4,6},{5,7},{6,4},{7,5},{8,10},{9,11},{10,... | collective-permute-start | bytes 1179656 | tf_op jit(solution)/shard_map/ppermute | solution.py:23
  9.0 15.8 %collective-permute-start.3 = (bf16[128,1024]{1,0:T(8,128)(2,1)}, bf16[128,1024]{1,0:T(8,128)(2,1)S(1)}, u32[]{:S(2)}, u32[]{:S(2)}) collective-permute-start(bf16[128,1024]{1,0:T(8,128)(2,1)} %get-tuple-element.103), channel_id=1, source_target_pairs={{0,2},{1,3},{2,0},{3,1},{4,6},{5,7},{6,4},{7,5},{8,10},{9,11},{10,... | collective-permute-start | bytes 786440 | tf_op jit(solution)/shard_map/ppermute | solution.py:23
  9.2 19.8 %collective-permute-start.4 = (bf16[128,1024]{1,0:T(8,128)(2,1)}, bf16[128,1024]{1,0:T(8,128)(2,1)S(1)}, u32[]{:S(2)}, u32[]{:S(2)}) collective-permute-start(bf16[128,1024]{1,0:T(8,128)(2,1)} %get-tuple-element.104), channel_id=1, source_target_pairs={{0,3},{1,2},{2,1},{3,0},{4,7},{5,6},{6,5},{7,4},{8,11},{9,10},{10,... | collective-permute-start | bytes 786440 | tf_op jit(solution)/shard_map/ppermute | solution.py:23
  10.9 19.6 %collective-permute-start = (bf16[128,1024]{1,0:T(8,128)(2,1)}, bf16[128,1024]{1,0:T(8,128)(2,1)S(1)}, u32[]{:S(2)}, u32[]{:S(2)}) collective-permute-start(bf16[128,1024]{1,0:T(8,128)(2,1)} %get-tuple-element.124.refs_0_), channel_id=1, source_target_pairs={{0,16},{16,0},{1,17},{17,1},{2,18},{18,2},{3,19},{19,3},{4,20},{20... | collective-permute-start | bytes 786440 | tf_op jit(solution)/shard_map/ppermute | solution.py:23
  12.4 28.4 %collective-permute-start.7 = (bf16[96,2048]{1,0:T(8,128)(2,1)}, bf16[96,2048]{1,0:T(8,128)(2,1)S(1)}, u32[]{:S(2)}, u32[]{:S(2)}) collective-permute-start(bf16[96,2048]{1,0:T(8,128)(2,1)} %get-tuple-element.117.n0), channel_id=1, source_target_pairs={{0,1},{1,0},{2,3},{3,2},{4,5},{5,4},{6,7},{7,6},{8,9},{9,8},{10,11... | collective-permute-start | bytes 1179656 | tf_op jit(solution)/shard_map/ppermute | solution.py:23
  24.8 47.2 %collective-permute-start.15 = (bf16[1024,512]{1,0:T(8,128)(2,1)}, bf16[1024,512]{1,0:T(8,128)(2,1)S(1)}, u32[]{:S(2)}, u32[]{:S(2)}) collective-permute-start(bf16[1024,512]{1,0:T(8,128)(2,1)} %get-tuple-element.136), channel_id=1, source_target_pairs={{0,8},{4,12},{8,0},{12,4},{1,9},{5,13},{9,1},{13,5},{2,10},{6,14},... | collective-permute-start | bytes 3145736 | tf_op jit(solution)/shard_map/ppermute | solution.py:23
  28.9 47.2 %collective-permute-start.14 = (bf16[1024,512]{1,0:T(8,128)(2,1)}, bf16[1024,512]{1,0:T(8,128)(2,1)S(1)}, u32[]{:S(2)}, u32[]{:S(2)}) collective-permute-start(bf16[1024,512]{1,0:T(8,128)(2,1)} %get-tuple-element.109), channel_id=1, source_target_pairs={{0,4},{4,0},{8,12},{12,8},{1,5},{5,1},{9,13},{13,9},{2,6},{6,2},{1... | collective-permute-start | bytes 3145736 | tf_op jit(solution)/shard_map/ppermute | solution.py:23
  40.8 12.1 %collective-permute-start.6 = (bf16[128,1024]{1,0:T(8,128)(2,1)S(1)}, bf16[128,1024]{1,0:T(8,128)(2,1)}, u32[]{:S(2)}, u32[]{:S(2)}) collective-permute-start(bf16[128,1024]{1,0:T(8,128)(2,1)S(1)} %collective-permute-done.4.refs_3_), channel_id=1, source_target_pairs={{0,16},{16,0},{1,17},{17,1},{2,18},{18,2},{3,19},{19,3},{4,20},{20... | collective-permute-start | bytes 786440 | tf_op jit(solution)/shard_map/ppermute | solution.py:23
  76.2 41.6 %collective-permute-start.19 = (bf16[1024,512]{1,0:T(8,128)(2,1)S(1)}, bf16[1024,512]{1,0:T(8,128)(2,1)S(1)}, u32[]{:S(2)}, u32[]{:S(2)}) collective-permute-start(bf16[1024,512]{1,0:T(8,128)(2,1)S(1)} %collective-permute-done.15.refs_15_.refs_7_), channel_id=1, source_target_pairs={{0,4},{4,0},{8,12},{12,8},{1,5},{5,1},{9,13},{13,9},{2,6},{6,2},{1... | collective-permute-start | bytes 3145736 | tf_op jit(solution)/shard_map/ppermute | solution.py:23
  96.8 20.9 %collective-permute-start.18 = (bf16[96,2048]{1,0:T(8,128)(2,1)}, bf16[96,2048]{1,0:T(8,128)(2,1)S(1)}, u32[]{:S(2)}, u32[]{:S(2)}) collective-permute-start(bf16[96,2048]{1,0:T(8,128)(2,1)} %get-tuple-element.143.refs_0_), channel_id=1, source_target_pairs={{0,8},{4,12},{8,0},{12,4},{1,9},{5,13},{9,1},{13,5},{2,10},{6,14},... | collective-permute-start | bytes 1179656 | tf_op jit(solution)/shard_map/ppermute | solution.py:23
  103.9 13.8 %collective-permute-start.21 = (bf16[96,2048]{1,0:T(8,128)(2,1)S(1)}, bf16[96,2048]{1,0:T(8,128)(2,1)S(1)}, u32[]{:S(2)}, u32[]{:S(2)}) collective-permute-start(bf16[96,2048]{1,0:T(8,128)(2,1)S(1)} %collective-permute-done.20.refs_4_), channel_id=1, source_target_pairs={{0,2},{1,3},{2,0},{3,1},{4,6},{5,7},{6,4},{7,5},{8,10},{9,11},{10,... | collective-permute-start | bytes 1179656 | tf_op jit(solution)/shard_map/ppermute | solution.py:23
  105.8 12.8 %collective-permute-start.23 = (bf16[96,2048]{1,0:T(8,128)(2,1)}, bf16[96,2048]{1,0:T(8,128)(2,1)S(1)}, u32[]{:S(2)}, u32[]{:S(2)}) collective-permute-start(bf16[96,2048]{1,0:T(8,128)(2,1)} %get-tuple-element.143.refs_0_), channel_id=1, source_target_pairs={{0,1},{1,0},{2,3},{3,2},{4,5},{5,4},{6,7},{7,6},{8,9},{9,8},{10,11... | collective-permute-start | bytes 1179656 | tf_op jit(solution)/shard_map/ppermute | solution.py:23
  105.8 13.3 %collective-permute-start.25 = (bf16[96,2048]{1,0:T(8,128)(2,1)S(1)}, bf16[96,2048]{1,0:T(8,128)(2,1)S(1)}, u32[]{:S(2)}, u32[]{:S(2)}) collective-permute-start(bf16[96,2048]{1,0:T(8,128)(2,1)S(1)} %collective-permute-done.24.refs_2_), channel_id=1, source_target_pairs={{0,1},{1,0},{2,3},{3,2},{4,5},{5,4},{6,7},{7,6},{8,9},{9,8},{10,11... | collective-permute-start | bytes 1179656 | tf_op jit(solution)/shard_map/ppermute | solution.py:23
  118.3 11.1 %collective-permute-start.29 = (bf16[96,2048]{1,0:T(8,128)(2,1)S(1)}, bf16[96,2048]{1,0:T(8,128)(2,1)S(1)}, u32[]{:S(2)}, u32[]{:S(2)}) collective-permute-start(bf16[96,2048]{1,0:T(8,128)(2,1)S(1)} %collective-permute-done.18.refs_8_), channel_id=1, source_target_pairs={{0,2},{1,3},{2,0},{3,1},{4,6},{5,7},{6,4},{7,5},{8,10},{9,11},{10,... | collective-permute-start | bytes 1179656 | tf_op jit(solution)/shard_map/ppermute | solution.py:23
  119.2 24.5 %collective-permute-start.31 = (bf16[512,512]{1,0:T(8,128)(2,1)}, bf16[512,512]{1,0:T(8,128)(2,1)S(1)}, u32[]{:S(2)}, u32[]{:S(2)}) collective-permute-start(bf16[512,512]{1,0:T(8,128)(2,1)} %get-tuple-element.155), channel_id=1, source_target_pairs={{0,4},{4,0},{8,12},{12,8},{1,5},{5,1},{9,13},{13,9},{2,6},{6,2},{1... | collective-permute-start | bytes 1572872 | tf_op jit(solution)/shard_map/ppermute | solution.py:23
  119.5 26.3 %collective-permute-start.32 = (bf16[512,512]{1,0:T(8,128)(2,1)}, bf16[512,512]{1,0:T(8,128)(2,1)S(1)}, u32[]{:S(2)}, u32[]{:S(2)}) collective-permute-start(bf16[512,512]{1,0:T(8,128)(2,1)} %get-tuple-element.157), channel_id=1, source_target_pairs={{0,8},{4,12},{8,0},{12,4},{1,9},{5,13},{9,1},{13,5},{2,10},{6,14},... | collective-permute-start | bytes 1572872 | tf_op jit(solution)/shard_map/ppermute | solution.py:23
  129.5 16.6 %collective-permute-start.34 = (bf16[96,2048]{1,0:T(8,128)(2,1)S(1)}, bf16[96,2048]{1,0:T(8,128)(2,1)}, u32[]{:S(2)}, u32[]{:S(2)}) collective-permute-start(bf16[96,2048]{1,0:T(8,128)(2,1)S(1)} %collective-permute-done.22.refs_0_), channel_id=1, source_target_pairs={{0,2},{1,3},{2,0},{3,1},{4,6},{5,7},{6,4},{7,5},{8,10},{9,11},{10,... | collective-permute-start | bytes 1179656 | tf_op jit(solution)/shard_map/ppermute | solution.py:23
  145.8 11.7 %collective-permute-start.36 = (bf16[512,512]{1,0:T(8,128)(2,1)S(1)}, bf16[512,512]{1,0:T(8,128)(2,1)S(1)}, u32[]{:S(2)}, u32[]{:S(2)}) collective-permute-start(bf16[512,512]{1,0:T(8,128)(2,1)S(1)} %collective-permute-done.32.refs_4_), channel_id=1, source_target_pairs={{0,4},{4,0},{8,12},{12,8},{1,5},{5,1},{9,13},{13,9},{2,6},{6,2},{1... | collective-permute-start | bytes 1572872 | tf_op jit(solution)/shard_map/ppermute | solution.py:23
  168.4 12.1 %collective-permute-start.41 = (bf16[96,2048]{1,0:T(8,128)(2,1)S(1)}, bf16[96,2048]{1,0:T(8,128)(2,1)}, u32[]{:S(2)}, u32[]{:S(2)}) collective-permute-start(bf16[96,2048]{1,0:T(8,128)(2,1)S(1)} %slice.105), channel_id=1, source_target_pairs={{0,2},{1,3},{2,0},{3,1},{4,6},{5,7},{6,4},{7,5},{8,10},{9,11},{10,... | collective-permute-start | bytes 1179656 | tf_op jit(solution)/shard_map/ppermute | solution.py:23
  169.8 18.5 %collective-permute-start.56 = (bf16[96,2048]{1,0:T(8,128)(2,1)S(1)}, bf16[96,2048]{1,0:T(8,128)(2,1)}, u32[]{:S(2)}, u32[]{:S(2)}) collective-permute-start(bf16[96,2048]{1,0:T(8,128)(2,1)S(1)} %slice.104), channel_id=1, source_target_pairs={{0,2},{1,3},{2,0},{3,1},{4,6},{5,7},{6,4},{7,5},{8,10},{9,11},{10,... | collective-permute-start | bytes 1179656 | tf_op jit(solution)/shard_map/ppermute | solution.py:23
  184.4 11.2 %collective-permute-start.57 = (bf16[96,2048]{1,0:T(8,128)(2,1)S(1)}, bf16[96,2048]{1,0:T(8,128)(2,1)S(1)}, u32[]{:S(2)}, u32[]{:S(2)}) collective-permute-start(bf16[96,2048]{1,0:T(8,128)(2,1)S(1)} %fusion), channel_id=1, source_target_pairs={{0,16},{16,0},{1,17},{17,1},{2,18},{18,2},{3,19},{19,3},{4,20},{20... | collective-permute-start | bytes 1179656 | tf_op jit(solution)/shard_map/ppermute | solution.py:23
  185.7 21.8 %collective-permute-start.50 = (bf16[96,2048]{1,0:T(8,128)(2,1)S(1)}, bf16[96,2048]{1,0:T(8,128)(2,1)S(1)}, u32[]{:S(2)}, u32[]{:S(2)}) collective-permute-start(bf16[96,2048]{1,0:T(8,128)(2,1)S(1)} %slice.103), channel_id=1, source_target_pairs={{0,2},{1,3},{2,0},{3,1},{4,6},{5,7},{6,4},{7,5},{8,10},{9,11},{10,... | collective-permute-start | bytes 1179656 | tf_op jit(solution)/shard_map/ppermute | solution.py:23
  187.3 17.9 %collective-permute-start.55 = (bf16[96,2048]{1,0:T(8,128)(2,1)S(1)}, bf16[96,2048]{1,0:T(8,128)(2,1)S(1)}, u32[]{:S(2)}, u32[]{:S(2)}) collective-permute-start(bf16[96,2048]{1,0:T(8,128)(2,1)S(1)} %slice.102), channel_id=1, source_target_pairs={{0,2},{1,3},{2,0},{3,1},{4,6},{5,7},{6,4},{7,5},{8,10},{9,11},{10,... | collective-permute-start | bytes 1179656 | tf_op jit(solution)/shard_map/ppermute | solution.py:23
  196.7 20.4 %collective-permute-start.60 = (bf16[96,2048]{1,0:T(8,128)(2,1)S(1)}, bf16[96,2048]{1,0:T(8,128)(2,1)S(1)}, u32[]{:S(2)}, u32[]{:S(2)}) collective-permute-start(bf16[96,2048]{1,0:T(8,128)(2,1)S(1)} %fusion.2), channel_id=1, source_target_pairs={{0,8},{4,12},{8,0},{12,4},{1,9},{5,13},{9,1},{13,5},{2,10},{6,14},... | collective-permute-start | bytes 1179656 | tf_op jit(solution)/shard_map/ppermute | solution.py:23
  (72 other events, 467.2 us)

commit v4 on v3

--- a/solution.py
+++ b/solution.py
@@ -14,7 +14,6 @@
 VMEM_LIMIT = 60 * 1024 * 1024
 TILE = 256
 MASKED = -1e30
-FAR_PARTS = 4
 MEMBER, WITHIN, MINE, LEAVING, SOURCE = range(5)
 
 
@@ -157,8 +156,8 @@
 
 def attend_body(traded, q, k, v, *refs):
     own, came, refs = refs[:4], refs[4:8], refs[8:]
-    of_row, of_column, wo, near, refs = refs[0], refs[1], refs[2], refs[3], refs[4:]
-    far, (mixed, cached, weight, sems) = refs[:-4], refs[-4:]
+    of_row, of_column, wo, refs = refs[0], refs[1], refs[2], refs[3:]
+    outs, (mixed, cached, weight, sems) = refs[:-4], refs[-4:]
     load = pltpu.make_async_copy(wo, weight, sems.at[4])
     count = own[0].shape[0]
 
@@ -215,24 +214,23 @@
         mixed[:, at] = sums.astype(jnp.bfloat16)
     load.wait()
     left = mixed[...]
-    for at in range(0, near.shape[1], TILE):
+    for at in range(0, weight.shape[1], TILE):
         part = jnp.dot(left, weight[:, at : at + TILE], preferred_element_type=jnp.float32)
-        split_rows(part, at, near, far)
-
-
-def split_rows(part, at, near, far):
-    count, width = part.shape[0] // 4, far[0].shape[1]
-    far, there = far[at // width], at % width
-    near[:count, at : at + TILE] = part[:count]
-    near[count:, at : at + TILE] = part[2 * count : 3 * count]
-    far[:count, there : there + TILE] = part[count : 2 * count].astype(jnp.bfloat16)
-    far[count:, there : there + TILE] = part[3 * count :].astype(jnp.bfloat16)
+        split_rows(part, at, outs)
+
+
+def split_rows(part, at, outs):
+    count = part.shape[0] // 4
+    for out, block in zip(outs, (0, 2, 1, 3)):
+        rows = part[block * count : (block + 1) * count]
+        out[:, at : at + TILE] = rows.astype(out.dtype)
 
 
 def split_shapes(rows, depth):
-    return [jax.ShapeDtypeStruct((rows // 2, depth), jnp.float32)] + [
-        jax.ShapeDtypeStruct((rows // 2, depth // FAR_PARTS), jnp.bfloat16)
-    ] * FAR_PARTS
+    return [
+        jax.ShapeDtypeStruct((rows // 4, depth), kind)
+        for kind in (jnp.float32, jnp.float32, jnp.bfloat16, jnp.bfloat16)
+    ]
 
 
 def attend(traded, q, k, v, own, came, of_row, of_column, wo):
@@ -243,7 +241,7 @@
     return pl.pallas_call(
         attend_body,
         in_specs=[smem()] + [vmem()] * 3 + [anywhere()] * 8 + [vmem()] * 2 + [anywhere()],
-        out_specs=[vmem()] * (1 + FAR_PARTS),
+        out_specs=[vmem()] * 4,
         out_shape=split_shapes(rows, depth),
         scratch_shapes=[
             pltpu.VMEM((rows, width), jnp.bfloat16),
@@ -309,9 +307,9 @@
     )(info, *parts, gate, up, *arrived)
 
 
-def down_rows(masks, info, acts, down, arrived):
+def down_rows(masks, info, acts, down, arrived, gate=False):
     rows, width = acts[0].shape
-    groups, parts, pieces = len(acts), 1 + FAR_PARTS, len(arrived)
+    groups, pieces = len(acts), len(arrived)
     depth = arrived[0].shape[0] * len(masks)
 
     def body(info_ref, *refs):
@@ -320,7 +318,6 @@
         for copy in load_pieces(masks, info_ref, [down_ref], piece_refs, held, sems):
             copy.wait()
         for group, act in enumerate(act_refs):
-            near, *far = outs[group * parts : (group + 1) * parts]
             for at in range(0, depth, TILE):
                 part = lax.dot_general(
                     act[...],
@@ -328,21 +325,21 @@
                     (((1,), (1,)), ((), ())),
                     preferred_element_type=jnp.float32,
                 )
-                split_rows(part, at, near, far)
+                split_rows(part, at, outs[4 * group : 4 * group + 4])
 
     sums = pl.pallas_call(
         body,
         in_specs=[smem()] + [vmem()] * groups + [anywhere()] * (1 + pieces),
-        out_specs=[vmem()] * (groups * parts),
+        out_specs=[vmem()] * (4 * groups),
         out_shape=split_shapes(rows, depth) * groups,
         scratch_shapes=[
             pltpu.VMEM((1, depth, width), jnp.bfloat16),
             pltpu.SemaphoreType.DMA((pieces + 1, 1)),
         ],
         compiler_params=params(),
-        cost_estimate=cost(False),
+        cost_estimate=cost(gate),
     )(info, *acts, down, *arrived)
-    return [sums[at * parts : (at + 1) * parts] for at in range(groups)]
+    return [sums[4 * at : 4 * at + 4] for at in range(groups)]
 
 
 def gather_rows(rows, across=None):
@@ -351,30 +348,14 @@
     return [rows, swap(rows, "mp", 1), across, swap(across, "mp", 1)]
 
 
-def over_core(parts):
-    return [parts[0]] + [swap(part, "mp", 1) for part in parts[1:]]
-
-
-def reduce_rows(near, *came, split=1):
-    count = near.shape[0] // 2
-    each = len(came) // split
-    kept, sent = [], []
-    for at in range(0, len(came), each):
-        both = jnp.concatenate(came[at : at + each], axis=1).astype(jnp.float32)
-        begin = at * came[0].shape[1]
-        both = both + near[:, begin : begin + both.shape[1]]
-        kept.append(both)
-        sent.append(both[count:].astype(jnp.bfloat16))
-    return kept, [swap(going, "mp", 2) for going in sent], sent
-
-
-def over_cores(near, *far):
-    came = jnp.concatenate([swap(part, "mp", 1) for part in far], axis=1)
-    return near + came.astype(jnp.float32)
+def reduce_rows(own, across, far_own, far_across):
+    sent = (across + swap(far_across, "mp", 1).astype(jnp.float32)).astype(jnp.bfloat16)
+    return (own, swap(far_own, "mp", 1)), swap(sent, "mp", 2), sent
 
 
 def total(kept, came):
-    return [part[: more.shape[0]] + more.astype(jnp.float32) for part, more in zip(kept, came)]
+    own, other = kept
+    return own + other.astype(jnp.float32) + came.astype(jnp.float32)
 
 
 def after(value, *earlier):
@@ -446,35 +427,8 @@
             jax.ShapeDtypeStruct((8, cached), jnp.int32),
         ],
         compiler_params=params(),
-        cost_estimate=cost(True),
+        cost_estimate=cost(False),
     )(info, lengths, requests, frequency)
-
-
-def finish_body(tokens, *refs):
-    parts, (state, normed) = refs[:-2], refs[-2:]
-    count = len(parts) // 2
-    sums = jnp.concatenate(
-        [
-            parts[at][: tokens.shape[0], :] + parts[count + at][...].astype(jnp.float32)
-            for at in range(count)
-        ],
-        axis=1,
-    )
-    rows = (tokens[...].astype(jnp.float32) + sums).astype(jnp.bfloat16)
-    state[...] = rows
-    normed[...] = layer_norm(rows.astype(jnp.float32)).astype(jnp.bfloat16)
-
-
-def finish(tokens, kept, came):
-    shape = jax.ShapeDtypeStruct(tokens.shape, jnp.bfloat16)
-    return pl.pallas_call(
-        finish_body,
-        in_specs=[vmem()] * (1 + len(kept) + len(came)),
-        out_specs=[vmem()] * 2,
-        out_shape=[shape] * 2,
-        compiler_params=params(),
-        cost_estimate=cost(False),
-    )(tokens, *kept, *came)
 
 
 def local(
@@ -507,11 +461,10 @@
     )
     blocks = [blocks[0]] + [swap(blocks[mask], "mp", mask) for mask in (1, 2, 3)]
     facts = row_facts(info, cached_lengths, request_ids, 4 * cache_entries.shape[0])
-    down_cut = cut(info, after(down_weight, wide_mine))
-    came = [swap(block, "rep", 1) for block in blocks[:2]]
-    came, blocks, facts, down_cut = join(came, blocks, facts, down_cut)
-    came += [swap(block, "rep", 1) for block in blocks[2:]]
-    parts = gather_rows(normed)
+    came = [swap(block, "rep", 1) for block in blocks]
+    over_chip = swap(normed, "mp", 2)
+    over_chip, came[0], came[1] = join(over_chip, came[0], came[1])
+    parts = gather_rows(normed, over_chip)
 
     def near_side(piece):
         return without(over_bits({0: piece}, bits), 0)
@@ -522,50 +475,55 @@
     def far_side(held):
         return without(over_bits(dict(held), bits), pair)
 
-    wide = {**across(wide_leaving), **near_side(wide_mine)}
+    wide = {**across(wide_leaving), **near_side(after(wide_mine, blocks[1]))}
 
     q, k, v = project(parts, facts[0], facts[1], query_weight, key_weight, value_weight)
     came, q = join(came, q)
-    near, *far = attend(traded, q, k, v, blocks, came, facts[2], facts[3], output_weight)
-    far = [swap(part, "mp", 1) for part in far]
-    far, wide = join(far, wide)
-    kept, came, _ = reduce_rows(near, *far, split=2)
+    sums = attend(traded, q, k, v, blocks, came, facts[2], facts[3], output_weight)
+    sums, wide = join(sums, wide)
+    kept, came, sent = reduce_rows(*sums)
+    down_cut = cut(info, after(down_weight, sent))
+    kept, came, down_cut = join(kept, came, down_cut)
     wide.update(far_side({pair: wide[pair]}))
-    state_own, normed_own = finish(tokens, kept, came)
+    state_own = (tokens.astype(jnp.float32) + total(kept, came)).astype(jnp.bfloat16)
+    normed_own = layer_norm(state_own.astype(jnp.float32)).astype(jnp.bfloat16)
 
     rows_z = swap(normed_own, "dp", pair)
     rows_x = swap(normed_own, "rep", 1)
-    over_chip = swap(rows_x, "mp", 2)
+    over_chip = swap(normed_own, "mp", 2), swap(rows_x, "mp", 2)
     rows_z, wide, over_chip = join(rows_z, wide, over_chip)
-    parts = gather_rows(normed_own) + gather_rows(rows_x, over_chip)
+    parts = gather_rows(normed_own, over_chip[0]) + gather_rows(rows_x, over_chip[1])
     rows_both = swap(rows_z, "rep", 1)
     back = {**across(after(down_cut[0], rows_z)), **near_side(after(down_cut[1], rows_z))}
     parts += gather_rows(rows_z)
     masks = [0] + list(wide)
     in_order = lambda held: [held[mask] for mask in masks[1:]]
     acts = gate_up(masks, info, parts, gate_weight, up_weight, in_order(wide))
+    parts = gather_rows(rows_both)
+    parts[0] = after(parts[0], acts[0])
     acts, back = join(acts, back)
     back.update(far_side({pair: back[pair]}))
-    parts = gather_rows(rows_both)
-    parts[0] = after(parts[0], acts[0])
     acts += gate_up(masks, info, parts, gate_weight, up_weight, in_order(wide))
 
-    def sums_of(*groups):
-        return down_rows(masks, info, groups, down_weight, in_order(back))
+    def sums_of(*groups, gate=False):
+        return down_rows(masks, info, groups, down_weight, in_order(back), gate)
 
     def crossed(value, axis, mask):
         return swap(value.astype(jnp.bfloat16), axis, mask).astype(jnp.float32)
 
     found_both, found_z = sums_of(acts[3], acts[2])
-    kept, came, sent = reduce_rows(*over_core(found_both))
-    kept_z, came_z, sent_z = reduce_rows(*over_core(found_z))
-    found_x, found = sums_of(after(acts[1], *sent, *sent_z), acts[0])
+    kept, came, sent = reduce_rows(*found_both)
+    kept_z, came_z, sent_z = reduce_rows(*found_z)
+    found_x, found = sums_of(after(acts[1], sent, sent_z), acts[0], gate=True)
     came, found_x, found = join(came, found_x, found)
-    (of_both,), (of_z,) = total(kept, came), total(kept_z, came_z)
+    of_both, of_z = total(kept, came), total(kept_z, came_z)
+    of_both = of_both.astype(jnp.bfloat16)
     sent = (of_z + crossed(of_both, "rep", 1)).astype(jnp.bfloat16)
     of_z = swap(sent, "dp", pair).astype(jnp.float32)
-    (of_x,) = total(*reduce_rows(*over_core(found_x))[:2])
-    (of_own,) = total(*reduce_rows(*over_core(found))[:2])
+    found_x, found = after((found_x, found), of_both)
+    kept, came, sent_x = reduce_rows(*found_x)
+    of_x = total(kept, came)
+    of_own = total(*reduce_rows(*after(found, sent_x))[:2])
     of_x = after(of_x, sent)
     columns = of_x.shape[1]
     of_x = [crossed(of_x[:, at : at + columns // 2], "rep", 1) for at in (0, columns // 2)]

time: 219 us -> 195 us (0.89)
  starting transfers between devices: 49.9 us -> 37.2 us
  waiting for transfers between devices: 97.3 us -> 91.4 us
  Pallas kernels: 56.4 us -> 53.8 us
    ppermute x61 -> x50, starting transfers between devices: 49.9 us -> 37.2 us  [swap(): return lax.ppermute(value, axis, pairs)]
    ppermute x61 -> x50, waiting for transfers between devices: 97.3 us -> 91.4 us  [swap(): return lax.ppermute(value, axis, pairs)]
    add x6 -> x1, other arithmetic: 4.37 us -> 0.13 us  [total(): return own + other.astype(jnp.float32) + came.astype(jnp.float32)]
    pallas_call x1 -> x0, Pallas kernels: 2.76 us -> none  [finish(): pl.pallas_call(finish_body, in_specs=[vmem()] * (1 + len(kept) + len(came...]
    convert_element_type x1 -> x7, other arithmetic: 1.07 us -> 3.75 us  [the longest x5 3.4 us: reduce_rows(): (across + swap(far_across, 'mp', 1).astype(jnp.float32)).astype(jnp.bfloa...]
    unnamed x70 -> x76, local copies, waits for them, and re-layouts: 4.89 us -> 3.21 us
  transfers between devices with their start and end apart: 61 -> 50, of which waited for: 31 -> 23; matrix products, arithmetic and copies ran while one was open for 3% -> 3% of each run, Pallas kernels for 21% -> 22%
where the time goes in v4:
time: 195 us
  waiting for transfers between devices  91.4 us (47%)
  Pallas kernels  53.8 us (28%)
  starting transfers between devices  37.2 us (19%)
  other arithmetic  7.12 us (4%)
  local copies, waits for them, and re-layouts  3.86 us (2%)
    ppermute x50, waiting for transfers between devices, swap(): return lax.ppermute(value, axis, pairs)  91.4 us
    ppermute x50, starting transfers between devices, swap(): return lax.ppermute(value, axis, pairs)  37.2 us
    pallas_call x2, Pallas kernels, gate_up(): pl.pallas_call(body, in_specs=[smem()] + [vmem()] * blocks + [anywhere()]...  16.7 us
    pallas_call x2, Pallas kernels, down_rows(): pl.pallas_call(body, in_specs=[smem()] + [vmem()] * groups + [anywhere()]...  11.8 us
    pallas_call x1, Pallas kernels, attend(): pl.pallas_call(attend_body, in_specs=[smem()] + [vmem()] * 3 + [anywhere(...  8.39 us
    pallas_call x1, Pallas kernels, project(): pl.pallas_call(project_body, grid=(width // TILE,), in_specs=[whole((coun...  6.61 us
    pallas_call x1, Pallas kernels, prepare(): pl.pallas_call(body, in_specs=[smem(), vmem(), vmem()] + [anywhere()] * s...  4.74 us
  transfers between devices with their start and end apart: 50, of which 23 were waited for; matrix products, arithmetic and copies ran while one was open for 3% of the time, Pallas kernels for 22%

profile of v4, /device:TPU:0, one launch (start us, length us, event | category | flops | bytes accessed | tf_op | source)
XLA Modules:
  0.0 194.6 jit_solution(9160840597577080464)
XLA Ops:
  1.3 4.7 %shard_map.127 = (bf16[96,2048]{1,0:T(8,128)(2,1)}, bf16[128,1024]{1,0:T(8,128)(2,1)}, bf16[128,1024]{1,0:T(8,128)(2,1)}, bf16[128,1024]{1,0:T(8,128)(2,1)}, bf1...) custom-call(s32[5]{0:T(128)} %stack.23.info_ref.info, bf16[96,2048]{1,0:T(8,128)(2,1)} %token_ref.1, ...), custom_call_target="tpu_custom_call" | custom-call | tf_op jit(solution)/shard_map/pallas_call | solution.py:68
  6.6 2.6 %collective-permute-start = (bf16[96,2048]{1,0:T(8,128)(2,1)}, bf16[96,2048]{1,0:T(8,128)(2,1)S(1)}, u32[]{:S(2)}, u32[]{:S(2)}) collective-permute-start(bf16[96,2048]{1,0:T(8,128)(2,1)} %get-tuple-element.102.n0), channel_id=1, source_target_pairs={{0,2},{1,3},{2,0},{3,1},{4,6},{5,7},{6,4},{7,5},{8,10},{9,11},{10,... | collective-permute-start | bytes 1179656 | tf_op jit(solution)/shard_map/ppermute | solution.py:22
  9.1 2.6 %collective-permute-start.11 = (bf16[1024,512]{1,0:T(8,128)(2,1)}, bf16[1024,512]{1,0:T(8,128)(2,1)S(1)}, u32[]{:S(2)}, u32[]{:S(2)}) collective-permute-start(bf16[1024,512]{1,0:T(8,128)(2,1)} %get-tuple-element.128), channel_id=1, source_target_pairs={{0,8},{4,12},{8,0},{12,4},{1,9},{5,13},{9,1},{13,5},{2,10},{6,14},... | collective-permute-start | bytes 3145736 | tf_op jit(solution)/shard_map/ppermute | solution.py:22
  15.3 7.4 %collective-permute-done.1.refs_4_ = bf16[128,1024]{1,0:T(8,128)(2,1)S(1)} collective-permute-done((bf16[128,1024]{1,0:T(8,128)(2,1)}, bf16[128,1024]{1,0:T(8,128)(2,1)S(1)}, u32[]{:S(2)}, u32[]{:S(2)}) %collective-permute-start.1) | collective-permute-done | bytes 262176 | tf_op jit(solution)/shard_map/ppermute | solution.py:22
  23.3 3.7 %collective-permute-done.3.refs_5_ = bf16[128,1024]{1,0:T(8,128)(2,1)S(1)} collective-permute-done((bf16[128,1024]{1,0:T(8,128)(2,1)S(1)}, bf16[128,1024]{1,0:T(8,128)(2,1)S(1)}, u32[]{:S(2)}, u32[]{:S(2)}) %collective-permute-start.3) | collective-permute-done | bytes 262176 | tf_op jit(solution)/shard_map/ppermute | solution.py:22
  29.5 5.6 %collective-permute-done.6.refs_3_ = bf16[128,1024]{1,0:T(8,128)(2,1)} collective-permute-done((bf16[128,1024]{1,0:T(8,128)(2,1)}, bf16[128,1024]{1,0:T(8,128)(2,1)}, u32[]{:S(2)}, u32[]{:S(2)}) %collective-permute-start.6) | collective-permute-done | bytes 262176 | tf_op jit(solution)/shard_map/ppermute | solution.py:22
  37.1 2.6 %shard_map.128 = (f32[384,128]{1,0:T(8,128)}, f32[384,128]{1,0:T(8,128)}, s32[384,8]{1,0:T(8,128)}, s32[8,512]{1,0:T(8,128)}) custom-call(s32[5]{0:T(128)} %stack.23.info_ref.info, s32[8,8]{1,0:T(8,128)} %lengths.1, s32[1,384]{1,0:T(1,128)} %requests.1, f32[1,128]{1,0:T(1,128)} %constant.52.clone.frequency), custom_call_target="tpu_custom_call" | custom-call | tf_op jit(solution)/shard_map/pallas_call | solution.py:419
  40.5 6.6 %shard_map.129 = (bf16[384,512]{1,0:T(8,128)(2,1)}, bf16[384,512]{1,0:T(8,128)(2,1)}, bf16[384,512]{1,0:T(8,128)(2,1)}) custom-call(bf16[96,2048]{1,0:T(8,128)(2,1)} %get-tuple-element.102.n0, bf16[96,2048]{1,0:T(8,128)(2,1)} %copy-done.26, bf16[96,2048]{1,0:T(8,128)(2,1)} %copy-done.21, bf16[96,2048]{1,0:T(8,128)(2,1)} %copy-done.28, ...), custom_call_target="tpu_custom_call" | custom-call | tf_op jit(solution)/shard_map/pallas_call | solution.py:145
  48.4 8.4 %shard_map.130 = (f32[96,2048]{1,0:T(8,128)}, f32[96,2048]{1,0:T(8,128)}, bf16[96,2048]{1,0:T(8,128)(2,1)}, bf16[96,2048]{1,0:T(8,128)(2,1)}) custom-call(s32[1]{0:T(128)S(6)} %copy.14.traded, bf16[384,512]{1,0:T(8,128)(2,1)} %get-tuple-element.113.q, bf16[384,512]{1,0:T(8,128)(2,1)} %get-tuple-element.114.k, bf16[384,512]{1,0:T(8,128)(2,1)} %get-tuple-element.115.v, ...), custom_call_target="tpu_custom_call" | custom-call | tf_op jit(solution)/shard_map/pallas_call | solution.py:241
  64.1 2.9 %shard_map.131 = (bf16[512,512]{1,0:T(8,128)(2,1)}, bf16[512,512]{1,0:T(8,128)(2,1)}) custom-call(s32[5]{0:T(128)} %stack.23.info_ref.info, bf16[512,2048]{1,0:T(8,128)(2,1)} %refs_2_.3), custom_call_target="tpu_custom_call" | custom-call | tf_op jit(solution)/shard_map/pallas_call | solution.py:104
  67.0 6.7 %collective-permute-done.14 = bf16[96,2048]{1,0:T(8,128)(2,1)} collective-permute-done((bf16[96,2048]{1,0:T(8,128)(2,1)}, bf16[96,2048]{1,0:T(8,128)(2,1)}, u32[]{:S(2)}, u32[]{:S(2)}) %collective-permute-start.14) | collective-permute-done | bytes 393248 | tf_op jit(solution)/shard_map/ppermute | solution.py:22
  79.6 6.6 %collective-permute-done.18.refs_4_ = bf16[96,2048]{1,0:T(8,128)(2,1)S(1)} collective-permute-done((bf16[96,2048]{1,0:T(8,128)(2,1)S(1)}, bf16[96,2048]{1,0:T(8,128)(2,1)S(1)}, u32[]{:S(2)}, u32[]{:S(2)}) %collective-permute-start.18) | collective-permute-done | bytes 393248 | tf_op jit(solution)/shard_map/ppermute | solution.py:22
  87.1 9.3 %collective-permute-done.16.refs_16_.refs_8_ = bf16[1024,512]{1,0:T(8,128)(2,1)S(1)} collective-permute-done((bf16[1024,512]{1,0:T(8,128)(2,1)S(1)}, bf16[1024,512]{1,0:T(8,128)(2,1)S(1)}, u32[]{:S(2)}, u32[]{:S(2)}) %collective-permute-start.16) | collective-permute-done | bytes 1048608 | tf_op jit(solution)/shard_map/ppermute | solution.py:22
  103.7 4.8 %collective-permute-done.26.refs_10_ = bf16[96,2048]{1,0:T(8,128)(2,1)S(1)} collective-permute-done((bf16[96,2048]{1,0:T(8,128)(2,1)S(1)}, bf16[96,2048]{1,0:T(8,128)(2,1)S(1)}, u32[]{:S(2)}, u32[]{:S(2)}) %collective-permute-start.26) | collective-permute-done | bytes 393248 | tf_op jit(solution)/shard_map/ppermute | solution.py:22
  111.1 10.6 %shard_map.132 = (bf16[384,512]{1,0:T(8,128)(2,1)}, bf16[384,512]{1,0:T(8,128)(2,1)}, bf16[384,512]{1,0:T(8,128)(2,1)}) custom-call(s32[5]{0:T(128)} %stack.23.info_ref.info, bf16[96,2048]{1,0:T(8,128)(2,1)} %copy-done.3, bf16[96,2048]{1,0:T(8,128)(2,1)} %copy-done.20, bf16[96,2048]{1,0:T(8,128)(2,1)} %copy-done.16, bf16[96,2048]{1,0:T(8,128)(2,1)} %copy-done.23, ...), custom_call_target="tpu_custom_call" | custom-call | tf_op jit(solution)/shard_map/pallas_call | solution.py:295
  121.7 2.6 %collective-permute-done.31.refs_3_ = bf16[512,512]{1,0:T(8,128)(2,1)S(1)} collective-permute-done((bf16[512,512]{1,0:T(8,128)(2,1)}, bf16[512,512]{1,0:T(8,128)(2,1)S(1)}, u32[]{:S(2)}, u32[]{:S(2)}) %collective-permute-start.31) | collective-permute-done | bytes 524320 | tf_op jit(solution)/shard_map/ppermute | solution.py:22
  124.2 3.1 %collective-permute-done.32.refs_4_ = bf16[512,512]{1,0:T(8,128)(2,1)S(1)} collective-permute-done((bf16[512,512]{1,0:T(8,128)(2,1)}, bf16[512,512]{1,0:T(8,128)(2,1)S(1)}, u32[]{:S(2)}, u32[]{:S(2)}) %collective-permute-start.32) | collective-permute-done | bytes 524320 | tf_op jit(solution)/shard_map/ppermute | solution.py:22
  130.7 6.2 %shard_map.133.refs_0_ = bf16[384,512]{1,0:T(8,128)(2,1)} custom-call(s32[5]{0:T(128)} %stack.23.info_ref.info, bf16[96,2048]{1,0:T(8,128)(2,1)} %copy-done.18, bf16[96,2048]{1,0:T(8,128)(2,1)} %copy-done.29, bf16[96,2048]{1,0:T(8,128)(2,1)} %collective-permute-done.29.refs_2_, bf16[96,2048]{1,0:T(8,128)(2,1)} %copy-done.30, bf16[512,2048]{1,0:T(8,128)(2,1)} %refs_4_.1, ...), custom_call_target="tpu_custom_call" | custom-call | tf_op jit(solution)/shard_map/pallas_call | solution.py:295
  139.3 5.9 %shard_map.134 = (f32[96,2048]{1,0:T(8,128)}, f32[96,2048]{1,0:T(8,128)}, bf16[96,2048]{1,0:T(8,128)(2,1)}, bf16[96,2048]{1,0:T(8,128)(2,1)}, f32[96,2048]{1,0:T...) custom-call(s32[5]{0:T(128)} %stack.23.info_ref.info, ...), custom_call_target="tpu_custom_call" | custom-call | tf_op jit(solution)/shard_map/pallas_call | solution.py:330
  149.3 6.0 %shard_map.135 = (f32[96,2048]{1,0:T(8,128)}, f32[96,2048]{1,0:T(8,128)}, bf16[96,2048]{1,0:T(8,128)(2,1)}, bf16[96,2048]{1,0:T(8,128)(2,1)}, f32[96,2048]{1,0:T...) custom-call(s32[5]{0:T(128)} %stack.23.info_ref.info, ...), custom_call_target="tpu_custom_call" | custom-call | flops 99999997952 | tf_op jit(solution)/shard_map/pallas_call | solution.py:330
  155.4 4.2 %collective-permute-done.35 = bf16[96,2048]{1,0:T(8,128)(2,1)S(1)} collective-permute-done((bf16[96,2048]{1,0:T(8,128)(2,1)S(1)}, bf16[96,2048]{1,0:T(8,128)(2,1)S(1)}, u32[]{:S(2)}, u32[]{:S(2)}) %collective-permute-start.35) | collective-permute-done | bytes 393248 | tf_op jit(solution)/shard_map/ppermute | solution.py:22
  163.4 8.9 %collective-permute-done.45 = bf16[96,2048]{1,0:T(8,128)(2,1)S(1)} collective-permute-done((bf16[96,2048]{1,0:T(8,128)(2,1)S(1)}, bf16[96,2048]{1,0:T(8,128)(2,1)S(1)}, u32[]{:S(2)}, u32[]{:S(2)}) %collective-permute-start.45) | collective-permute-done | bytes 393248 | tf_op jit(solution)/shard_map/ppermute | solution.py:22
  175.1 5.7 %collective-permute-done.43 = bf16[96,2048]{1,0:T(8,128)(2,1)S(1)} collective-permute-done((bf16[96,2048]{1,0:T(8,128)(2,1)S(1)}, bf16[96,2048]{1,0:T(8,128)(2,1)S(1)}, u32[]{:S(2)}, u32[]{:S(2)}) %collective-permute-start.43) | collective-permute-done | bytes 393248 | tf_op jit(solution)/shard_map/ppermute | solution.py:22
  183.0 10.5 %collective-permute-done.49 = bf16[96,2048]{1,0:T(8,128)(2,1)S(1)} collective-permute-done((bf16[96,2048]{1,0:T(8,128)(2,1)S(1)}, bf16[96,2048]{1,0:T(8,128)(2,1)S(1)}, u32[]{:S(2)}, u32[]{:S(2)}) %collective-permute-start.49) | collective-permute-done | bytes 393248 | tf_op jit(solution)/shard_map/ppermute | solution.py:22
  (177 shorter events, 55.5 us)
Async XLA Ops:
  6.6 16.7 %collective-permute-start = (bf16[96,2048]{1,0:T(8,128)(2,1)}, bf16[96,2048]{1,0:T(8,128)(2,1)S(1)}, u32[]{:S(2)}, u32[]{:S(2)}) collective-permute-start(bf16[96,2048]{1,0:T(8,128)(2,1)} %get-tuple-element.102.n0), channel_id=1, source_target_pairs={{0,2},{1,3},{2,0},{3,1},{4,6},{5,7},{6,4},{7,5},{8,10},{9,11},{10,... | collective-permute-start | bytes 1179656 | tf_op jit(solution)/shard_map/ppermute | solution.py:22
  9.1 48.9 %collective-permute-start.11 = (bf16[1024,512]{1,0:T(8,128)(2,1)}, bf16[1024,512]{1,0:T(8,128)(2,1)S(1)}, u32[]{:S(2)}, u32[]{:S(2)}) collective-permute-start(bf16[1024,512]{1,0:T(8,128)(2,1)} %get-tuple-element.128), channel_id=1, source_target_pairs={{0,8},{4,12},{8,0},{12,4},{1,9},{5,13},{9,1},{13,5},{2,10},{6,14},... | collective-permute-start | bytes 3145736 | tf_op jit(solution)/shard_map/ppermute | solution.py:22
  11.7 46.5 %collective-permute-start.10 = (bf16[1024,512]{1,0:T(8,128)(2,1)}, bf16[1024,512]{1,0:T(8,128)(2,1)S(1)}, u32[]{:S(2)}, u32[]{:S(2)}) collective-permute-start(bf16[1024,512]{1,0:T(8,128)(2,1)} %get-tuple-element.127), channel_id=1, source_target_pairs={{0,4},{4,0},{8,12},{12,8},{1,5},{5,1},{9,13},{13,9},{2,6},{6,2},{1... | collective-permute-start | bytes 3145736 | tf_op jit(solution)/shard_map/ppermute | solution.py:22
  14.8 12.2 %collective-permute-start.3 = (bf16[128,1024]{1,0:T(8,128)(2,1)S(1)}, bf16[128,1024]{1,0:T(8,128)(2,1)S(1)}, u32[]{:S(2)}, u32[]{:S(2)}) collective-permute-start(bf16[128,1024]{1,0:T(8,128)(2,1)S(1)} %collective-permute-done.2.refs_1_), channel_id=1, source_target_pairs={{0,16},{16,0},{1,17},{17,1},{2,18},{18,2},{3,19},{19,3},{4,20},{20... | collective-permute-start | bytes 786440 | tf_op jit(solution)/shard_map/ppermute | solution.py:22
  23.3 13.3 %collective-permute-start.8 = (bf16[96,2048]{1,0:T(8,128)(2,1)}, bf16[96,2048]{1,0:T(8,128)(2,1)S(1)}, u32[]{:S(2)}, u32[]{:S(2)}) collective-permute-start(bf16[96,2048]{1,0:T(8,128)(2,1)} %get-tuple-element.102.n0), channel_id=1, source_target_pairs={{0,1},{1,0},{2,3},{3,2},{4,5},{5,4},{6,7},{7,6},{8,9},{9,8},{10,11... | collective-permute-start | bytes 1179656 | tf_op jit(solution)/shard_map/ppermute | solution.py:22
  35.1 12.1 %collective-permute-start.5 = (bf16[128,1024]{1,0:T(8,128)(2,1)}, bf16[128,1024]{1,0:T(8,128)(2,1)}, u32[]{:S(2)}, u32[]{:S(2)}) collective-permute-start(bf16[128,1024]{1,0:T(8,128)(2,1)} %collective-permute-done.4.refs_2_), channel_id=1, source_target_pairs={{0,16},{16,0},{1,17},{17,1},{2,18},{18,2},{3,19},{19,3},{4,20},{20... | collective-permute-start | bytes 786440 | tf_op jit(solution)/shard_map/ppermute | solution.py:22
  36.6 11.9 %collective-permute-start.7 = (bf16[128,1024]{1,0:T(8,128)(2,1)}, bf16[128,1024]{1,0:T(8,128)(2,1)}, u32[]{:S(2)}, u32[]{:S(2)}) collective-permute-start(bf16[128,1024]{1,0:T(8,128)(2,1)} %collective-permute-done.6.refs_3_), channel_id=1, source_target_pairs={{0,16},{16,0},{1,17},{17,1},{2,18},{18,2},{3,19},{19,3},{4,20},{20... | collective-permute-start | bytes 786440 | tf_op jit(solution)/shard_map/ppermute | solution.py:22
  62.1 11.5 %collective-permute-start.14 = (bf16[96,2048]{1,0:T(8,128)(2,1)}, bf16[96,2048]{1,0:T(8,128)(2,1)}, u32[]{:S(2)}, u32[]{:S(2)}) collective-permute-start(bf16[96,2048]{1,0:T(8,128)(2,1)} %add_convert_fusion.7), channel_id=1, source_target_pairs={{0,2},{1,3},{2,0},{3,1},{4,6},{5,7},{6,4},{7,5},{8,10},{9,11},{10,... | collective-permute-start | bytes 1179656 | tf_op jit(solution)/shard_map/ppermute | solution.py:22
  63.0 33.3 %collective-permute-start.16 = (bf16[1024,512]{1,0:T(8,128)(2,1)S(1)}, bf16[1024,512]{1,0:T(8,128)(2,1)S(1)}, u32[]{:S(2)}, u32[]{:S(2)}) collective-permute-start(bf16[1024,512]{1,0:T(8,128)(2,1)S(1)} %collective-permute-done.11.refs_15_.refs_7_), channel_id=1, source_target_pairs={{0,4},{4,0},{8,12},{12,8},{1,5},{5,1},{9,13},{13,9},{2,6},{6,2},{1... | collective-permute-start | bytes 3145736 | tf_op jit(solution)/shard_map/ppermute | solution.py:22
  77.4 19.0 %collective-permute-start.17 = (bf16[96,2048]{1,0:T(8,128)(2,1)S(1)}, bf16[96,2048]{1,0:T(8,128)(2,1)S(1)}, u32[]{:S(2)}, u32[]{:S(2)}) collective-permute-start(bf16[96,2048]{1,0:T(8,128)(2,1)S(1)} %fusion.3.refs_0_), channel_id=1, source_target_pairs={{0,2},{1,3},{2,0},{3,1},{4,6},{5,7},{6,4},{7,5},{8,10},{9,11},{10,... | collective-permute-start | bytes 1179656 | tf_op jit(solution)/shard_map/ppermute | solution.py:22
  78.2 18.1 %collective-permute-start.15 = (bf16[96,2048]{1,0:T(8,128)(2,1)S(1)}, bf16[96,2048]{1,0:T(8,128)(2,1)S(1)}, u32[]{:S(2)}, u32[]{:S(2)}) collective-permute-start(bf16[96,2048]{1,0:T(8,128)(2,1)S(1)} %fusion.3.refs_0_), channel_id=1, source_target_pairs={{0,8},{4,12},{8,0},{12,4},{1,9},{5,13},{9,1},{13,5},{2,10},{6,14},... | collective-permute-start | bytes 1179656 | tf_op jit(solution)/shard_map/ppermute | solution.py:22
  97.0 11.5 %collective-permute-start.26 = (bf16[96,2048]{1,0:T(8,128)(2,1)S(1)}, bf16[96,2048]{1,0:T(8,128)(2,1)S(1)}, u32[]{:S(2)}, u32[]{:S(2)}) collective-permute-start(bf16[96,2048]{1,0:T(8,128)(2,1)S(1)} %collective-permute-done.15.refs_8_), channel_id=1, source_target_pairs={{0,2},{1,3},{2,0},{3,1},{4,6},{5,7},{6,4},{7,5},{8,10},{9,11},{10,... | collective-permute-start | bytes 1179656 | tf_op jit(solution)/shard_map/ppermute | solution.py:22
  99.7 24.5 %collective-permute-start.31 = (bf16[512,512]{1,0:T(8,128)(2,1)}, bf16[512,512]{1,0:T(8,128)(2,1)S(1)}, u32[]{:S(2)}, u32[]{:S(2)}) collective-permute-start(bf16[512,512]{1,0:T(8,128)(2,1)} %get-tuple-element.152), channel_id=1, source_target_pairs={{0,4},{4,0},{8,12},{12,8},{1,5},{5,1},{9,13},{13,9},{2,6},{6,2},{1... | collective-permute-start | bytes 1572872 | tf_op jit(solution)/shard_map/ppermute | solution.py:22
  101.7 25.6 %collective-permute-start.32 = (bf16[512,512]{1,0:T(8,128)(2,1)}, bf16[512,512]{1,0:T(8,128)(2,1)S(1)}, u32[]{:S(2)}, u32[]{:S(2)}) collective-permute-start(bf16[512,512]{1,0:T(8,128)(2,1)} %get-tuple-element.154), channel_id=1, source_target_pairs={{0,8},{4,12},{8,0},{12,4},{1,9},{5,13},{9,1},{13,5},{2,10},{6,14},... | collective-permute-start | bytes 1572872 | tf_op jit(solution)/shard_map/ppermute | solution.py:22
  109.4 18.0 %collective-permute-start.29 = (bf16[96,2048]{1,0:T(8,128)(2,1)S(1)}, bf16[96,2048]{1,0:T(8,128)(2,1)}, u32[]{:S(2)}, u32[]{:S(2)}) collective-permute-start(bf16[96,2048]{1,0:T(8,128)(2,1)S(1)} %collective-permute-done.20.refs_0_), channel_id=1, source_target_pairs={{0,2},{1,3},{2,0},{3,1},{4,6},{5,7},{6,4},{7,5},{8,10},{9,11},{10,... | collective-permute-start | bytes 1179656 | tf_op jit(solution)/shard_map/ppermute | solution.py:22
  145.7 13.9 %collective-permute-start.37 = (bf16[96,2048]{1,0:T(8,128)(2,1)}, bf16[96,2048]{1,0:T(8,128)(2,1)S(1)}, u32[]{:S(2)}, u32[]{:S(2)}) collective-permute-start(bf16[96,2048]{1,0:T(8,128)(2,1)} %get-tuple-element.182), channel_id=1, source_target_pairs={{0,1},{1,0},{2,3},{3,2},{4,5},{5,4},{6,7},{7,6},{8,9},{9,8},{10,11... | collective-permute-start | bytes 1179656 | tf_op jit(solution)/shard_map/ppermute | solution.py:22
  160.3 12.0 %collective-permute-start.45 = (bf16[96,2048]{1,0:T(8,128)(2,1)S(1)}, bf16[96,2048]{1,0:T(8,128)(2,1)S(1)}, u32[]{:S(2)}, u32[]{:S(2)}) collective-permute-start(bf16[96,2048]{1,0:T(8,128)(2,1)S(1)} %add_convert_fusion.4), channel_id=1, source_target_pairs={{0,2},{1,3},{2,0},{3,1},{4,6},{5,7},{6,4},{7,5},{8,10},{9,11},{10,... | collective-permute-start | bytes 1179656 | tf_op jit(solution)/shard_map/ppermute | solution.py:22
  161.8 13.3 %collective-permute-start.42 = (bf16[96,2048]{1,0:T(8,128)(2,1)}, bf16[96,2048]{1,0:T(8,128)(2,1)S(1)}, u32[]{:S(2)}, u32[]{:S(2)}) collective-permute-start(bf16[96,2048]{1,0:T(8,128)(2,1)} %get-tuple-element.195), channel_id=1, source_target_pairs={{0,1},{1,0},{2,3},{3,2},{4,5},{5,4},{6,7},{7,6},{8,9},{9,8},{10,11... | collective-permute-start | bytes 1179656 | tf_op jit(solution)/shard_map/ppermute | solution.py:22
  161.9 18.9 %collective-permute-start.43 = (bf16[96,2048]{1,0:T(8,128)(2,1)S(1)}, bf16[96,2048]{1,0:T(8,128)(2,1)S(1)}, u32[]{:S(2)}, u32[]{:S(2)}) collective-permute-start(bf16[96,2048]{1,0:T(8,128)(2,1)S(1)} %add_convert_fusion.2), channel_id=1, source_target_pairs={{0,2},{1,3},{2,0},{3,1},{4,6},{5,7},{6,4},{7,5},{8,10},{9,11},{10,... | collective-permute-start | bytes 1179656 | tf_op jit(solution)/shard_map/ppermute | solution.py:22
  163.2 19.8 %collective-permute-start.39 = (bf16[96,2048]{1,0:T(8,128)(2,1)S(1)}, bf16[96,2048]{1,0:T(8,128)(2,1)S(1)}, u32[]{:S(2)}, u32[]{:S(2)}) collective-permute-start(bf16[96,2048]{1,0:T(8,128)(2,1)S(1)} %copy-done.35), channel_id=1, source_target_pairs={{0,1},{1,0},{2,3},{3,2},{4,5},{5,4},{6,7},{7,6},{8,9},{9,8},{10,11... | collective-permute-start | bytes 1179656 | tf_op jit(solution)/shard_map/ppermute | solution.py:22
  172.5 20.9 %collective-permute-start.49 = (bf16[96,2048]{1,0:T(8,128)(2,1)S(1)}, bf16[96,2048]{1,0:T(8,128)(2,1)S(1)}, u32[]{:S(2)}, u32[]{:S(2)}) collective-permute-start(bf16[96,2048]{1,0:T(8,128)(2,1)S(1)} %add_convert_fusion), channel_id=1, source_target_pairs={{0,8},{4,12},{8,0},{12,4},{1,9},{5,13},{9,1},{13,5},{2,10},{6,14},... | collective-permute-start | bytes 1179656 | tf_op jit(solution)/shard_map/ppermute | solution.py:22
  174.1 19.3 %collective-permute-start.41 = (bf16[96,2048]{1,0:T(8,128)(2,1)S(1)}, bf16[96,2048]{1,0:T(8,128)(2,1)S(1)}, u32[]{:S(2)}, u32[]{:S(2)}) collective-permute-start(bf16[96,2048]{1,0:T(8,128)(2,1)S(1)} %add_convert_fusion.1), channel_id=1, source_target_pairs={{0,2},{1,3},{2,0},{3,1},{4,6},{5,7},{6,4},{7,5},{8,10},{9,11},{10,... | collective-permute-start | bytes 1179656 | tf_op jit(solution)/shard_map/ppermute | solution.py:22
  180.9 12.6 %collective-permute-start.47 = (bf16[96,1024]{1,0:T(8,128)(2,1)S(1)}, bf16[96,1024]{1,0:T(8,128)(2,1)S(1)}, u32[]{:S(2)}, u32[]{:S(2)}) collective-permute-start(bf16[96,1024]{1,0:T(8,128)(2,1)S(1)} %get-tuple-element.201), channel_id=1, source_target_pairs={{0,16},{16,0},{1,17},{17,1},{2,18},{18,2},{3,19},{19,3},{4,20},{20... | collective-permute-start | bytes 589832 | tf_op jit(solution)/shard_map/ppermute | solution.py:22
  181.6 11.8 %collective-permute-start.48 = (bf16[96,1024]{1,0:T(8,128)(2,1)S(1)}, bf16[96,1024]{1,0:T(8,128)(2,1)S(1)}, u32[]{:S(2)}, u32[]{:S(2)}) collective-permute-start(bf16[96,1024]{1,0:T(8,128)(2,1)S(1)} %get-tuple-element.202), channel_id=1, source_target_pairs={{0,16},{16,0},{1,17},{17,1},{2,18},{18,2},{3,19},{19,3},{4,20},{20... | collective-permute-start | bytes 589832 | tf_op jit(solution)/shard_map/ppermute | solution.py:22
  (64 other events, 632.0 us)

commit v5 on v4

--- a/solution.py
+++ b/solution.py
@@ -11,7 +11,8 @@
 HEAD_DIM = 128
 EPSILON = 1e-05
 ROPE_BASE = 10000.0
-VMEM_LIMIT = 60 * 1024 * 1024
+VMEM_LIMIT = 28 * 1024 * 1024
+VMEM_WHOLE = 60 * 1024 * 1024
 TILE = 256
 MASKED = -1e30
 MEMBER, WITHIN, MINE, LEAVING, SOURCE = range(5)
@@ -40,8 +41,8 @@
     return pl.BlockSpec(memory_space=pl.ANY)
 
 
-def params():
-    return pltpu.CompilerParams(vmem_limit_bytes=VMEM_LIMIT)
+def params(limit=VMEM_LIMIT):
+    return pltpu.CompilerParams(vmem_limit_bytes=limit)
 
 
 def cost(gate=True):
@@ -53,27 +54,29 @@
     stack, depth, width = len(weights), weights[0].shape[0], weights[0].shape[1] // 4
 
     def body(info_ref, token_ref, entry_ref, *refs):
-        sources, normed, blocks = refs[:stack], refs[stack], refs[stack + 1 : stack + 5]
-        outs, sems = refs[stack + 5 : -1], refs[-1]
+        sources, normed, blocks = refs[:stack], refs[stack : stack + 2], refs[stack + 2 : stack + 6]
+        outs, sems = refs[stack + 6 : -1], refs[-1]
         copies = cut_copies(info_ref, sources, outs, sems)
         part = blocks[0].shape[1] // 2
         for mask, out in enumerate(blocks):
             begin = pl.multiple_of((info_ref[MEMBER] ^ mask) * part, part)
             out[:, :part] = entry_ref[:, pl.ds(begin, part)]
             out[:, part:] = entry_ref[:, pl.ds(4 * part + begin, part)]
-        normed[...] = layer_norm(token_ref[...].astype(jnp.float32)).astype(jnp.bfloat16)
+        found = layer_norm(token_ref[...].astype(jnp.float32)).astype(jnp.bfloat16)
+        for half, out in enumerate(normed):
+            out[...] = found[:, half * out.shape[1] : (half + 1) * out.shape[1]]
         for copy in copies:
             copy.wait()
 
     return pl.pallas_call(
         body,
         in_specs=[smem(), vmem(), vmem()] + [anywhere()] * stack,
-        out_specs=[vmem()] * 7,
-        out_shape=[jax.ShapeDtypeStruct(tokens.shape, jnp.bfloat16)]
+        out_specs=[vmem()] * 8,
+        out_shape=[jax.ShapeDtypeStruct((tokens.shape[0], tokens.shape[1] // 2), jnp.bfloat16)] * 2
         + [jax.ShapeDtypeStruct((rows, columns // 4), jnp.bfloat16)] * 4
         + [jax.ShapeDtypeStruct((stack * depth, width), jnp.bfloat16)] * 2,
         scratch_shapes=[pltpu.SemaphoreType.DMA((2, stack))],
-        compiler_params=params(),
+        compiler_params=params(VMEM_WHOLE),
         cost_estimate=cost(False),
     )(info, tokens, entries, *weights)
 
@@ -112,13 +115,16 @@
     )(info, *weights)
 
 
-def project_body(n0, n1, n2, n3, cosine, sine, wq, wk, wv, q_ref, k_ref, v_ref, rows):
-    count = n0.shape[0]
+def project_body(*refs):
+    parts, refs = refs[:8], refs[8:]
+    cosine, sine, wq, wk, wv, q_ref, k_ref, v_ref, rows = refs
+    count, half = parts[0].shape
 
     @pl.when(pl.program_id(0) == 0)
     def _():
-        for at, part in enumerate((n0, n1, n2, n3)):
-            rows[pl.ds(at * count, count), :] = part[...]
+        for at, part in enumerate(parts):
+            begin = at % 2 * half
+            rows[pl.ds(at // 2 * count, count), begin : begin + half] = part[...]
 
     x = rows[...]
     width = wq.shape[1]
@@ -136,7 +142,7 @@
 
 
 def project(parts, cosine, sine, wq, wk, wv):
-    count, depth = parts[0].shape
+    count, depth = parts[0].shape[0], 2 * parts[0].shape[1]
     rows, width = 4 * count, wq.shape[1]
     whole = lambda shape: pl.BlockSpec(shape, lambda i: (0, 0))
     column = pl.BlockSpec((depth, TILE), lambda i: (0, i))
@@ -145,7 +151,7 @@
     return pl.pallas_call(
         project_body,
         grid=(width // TILE,),
-        in_specs=[whole((count, depth))] * 4 + [whole((rows, HEAD_DIM))] * 2 + [column] * 3,
+        in_specs=[whole((count, depth // 2))] * 8 + [whole((rows, HEAD_DIM))] * 2 + [column] * 3,
         out_specs=[out] * 3,
         out_shape=[shape] * 3,
         scratch_shapes=[pltpu.VMEM((rows, depth), jnp.bfloat16)],
@@ -456,15 +462,16 @@
     source = jnp.where(traded[0] == 1, 1 - replica, replica) * planes + within
     info = jnp.stack([member, within, mine, leaving, source]).astype(jnp.int32)
 
-    normed, *blocks, wide_leaving, wide_mine = prepare(
+    *normed, blocks_0, blocks_1, blocks_2, blocks_3, wide_leaving, wide_mine = prepare(
         info, tokens, cache_entries, gate_weight, up_weight
     )
-    blocks = [blocks[0]] + [swap(blocks[mask], "mp", mask) for mask in (1, 2, 3)]
+    blocks = [blocks_0, swap(blocks_1, "mp", 1), swap(blocks_2, "mp", 2), swap(blocks_3, "mp", 3)]
     facts = row_facts(info, cached_lengths, request_ids, 4 * cache_entries.shape[0])
     came = [swap(block, "rep", 1) for block in blocks]
-    over_chip = swap(normed, "mp", 2)
+    over_chip = [swap(half, "mp", 2) for half in normed]
     over_chip, came[0], came[1] = join(over_chip, came[0], came[1])
-    parts = gather_rows(normed, over_chip)
+    parts = [gather_rows(*halves) for halves in zip(normed, over_chip)]
+    parts = [half for pair_of in zip(*parts) for half in pair_of]
 
     def near_side(piece):
         return without(over_bits({0: piece}, bits), 0)

time: 195 us -> 187 us (0.959)
  Pallas kernels: 53.8 us -> 30.8 us
  starting transfers between devices: 37.2 us -> 47.6 us
  waiting for transfers between devices: 91.4 us -> 98.3 us
  other arithmetic: 7.12 us -> 2.77 us
    ppermute x50 -> x53, starting transfers between devices: 37.2 us -> 47.6 us  [swap(): return lax.ppermute(value, axis, pairs)]
    pallas_call x2, Pallas kernels: 16.7 us -> 9.45 us  [gate_up(): pl.pallas_call(body, in_specs=[smem()] + [vmem()] * blocks + [anywhere()]...]
    ppermute x50 -> x53, waiting for transfers between devices: 91.4 us -> 98.3 us  [swap(): return lax.ppermute(value, axis, pairs)]
    pallas_call x2, Pallas kernels: 11.8 us -> 5.46 us  [down_rows(): pl.pallas_call(body, in_specs=[smem()] + [vmem()] * groups + [anywhere()]...]
    pallas_call x1, Pallas kernels: 8.39 us -> 4.74 us  [attend(): pl.pallas_call(attend_body, in_specs=[smem()] + [vmem()] * 3 + [anywhere(...]
    pallas_call x1, Pallas kernels: 6.61 us -> 3.57 us  [project(): pl.pallas_call(project_body, grid=(width // TILE,), in_specs=[whole((coun...]
    convert_element_type x5, other arithmetic: 3.4 us -> 0.39 us  [reduce_rows(): (across + swap(far_across, 'mp', 1).astype(jnp.float32)).astype(jnp.bfloa...]
    unnamed x76 -> x30, local copies, waits for them, and re-layouts: 3.21 us -> 5.08 us
  transfers between devices with their start and end apart: 50 -> 53, of which waited for: 23 -> 24; matrix products, arithmetic and copies ran while one was open for 3% -> 1% of each run, Pallas kernels for 22% -> 13%
where the time goes in v5:
time: 187 us; the launch traced here: 186 us
  waiting for transfers between devices  98.3 us (53%)
  starting transfers between devices  47.6 us (25%)
  Pallas kernels  30.8 us (16%)
  local copies, waits for them, and re-layouts  5.79 us (3%)
  other arithmetic  2.77 us (1%)
    ppermute x53, waiting for transfers between devices, swap(): return lax.ppermute(value, axis, pairs)  98.3 us
    ppermute x53, starting transfers between devices, swap(): return lax.ppermute(value, axis, pairs)  47.6 us
    pallas_call x2, Pallas kernels, gate_up(): pl.pallas_call(body, in_specs=[smem()] + [vmem()] * blocks + [anywhere()]...  9.45 us
    pallas_call x2, Pallas kernels, down_rows(): pl.pallas_call(body, in_specs=[smem()] + [vmem()] * groups + [anywhere()]...  5.46 us
    unnamed x30, local copies, waits for them, and re-layouts  5.08 us
    pallas_call x1, Pallas kernels, prepare(): pl.pallas_call(body, in_specs=[smem(), vmem(), vmem()] + [anywhere()] * s...  4.88 us
    pallas_call x1, Pallas kernels, attend(): pl.pallas_call(attend_body, in_specs=[smem()] + [vmem()] * 3 + [anywhere(...  4.74 us
  transfers between devices with their start and end apart: 53, of which 24 were waited for; matrix products, arithmetic and copies ran while one was open for 1% of the time, Pallas kernels for 13%

profile of v5, /device:TPU:0, one launch (start us, length us, event | category | flops | bytes accessed | tf_op | source)
XLA Modules:
  0.0 186.3 jit_solution(13396223569039787227)
XLA Ops:
  1.4 4.9 %shard_map.127 = (bf16[96,1024]{1,0:T(8,128)(2,1)}, bf16[96,1024]{1,0:T(8,128)(2,1)}, bf16[128,1024]{1,0:T(8,128)(2,1)}, bf16[128,1024]{1,0:T(8,128)(2,1)}, bf16...) custom-call(s32[5]{0:T(128)} %stack.23.info_ref.info, ...), custom_call_target="tpu_custom_call" | custom-call | tf_op jit(solution)/shard_map/pallas_call | solution.py:71
  6.8 3.7 %collective-permute-start.14 = (bf16[1024,512]{1,0:T(8,128)(2,1)}, bf16[1024,512]{1,0:T(8,128)(2,1)S(1)}, u32[]{:S(2)}, u32[]{:S(2)}) collective-permute-start(bf16[1024,512]{1,0:T(8,128)(2,1)} %get-tuple-element.132), channel_id=1, source_target_pairs={{0,8},{4,12},{8,0},{12,4},{1,9},{5,13},{9,1},{13,5},{2,10},{6,14},... | collective-permute-start | bytes 3145736 | tf_op jit(solution)/shard_map/ppermute | solution.py:23
  15.5 4.4 %collective-permute-done.refs_4_ = bf16[96,1024]{1,0:T(8,128)(2,1)S(1)} collective-permute-done((bf16[96,1024]{1,0:T(8,128)(2,1)}, bf16[96,1024]{1,0:T(8,128)(2,1)S(1)}, u32[]{:S(2)}, u32[]{:S(2)}) %collective-permute-start) | collective-permute-done | bytes 196640 | tf_op jit(solution)/shard_map/ppermute | solution.py:23
  25.3 2.8 %collective-permute-done.4.refs_5_ = bf16[128,1024]{1,0:T(8,128)(2,1)S(1)} collective-permute-done((bf16[128,1024]{1,0:T(8,128)(2,1)S(1)}, bf16[128,1024]{1,0:T(8,128)(2,1)S(1)}, u32[]{:S(2)}, u32[]{:S(2)}) %collective-permute-start.4) | collective-permute-done | bytes 262176 | tf_op jit(solution)/shard_map/ppermute | solution.py:23
  29.7 3.4 %collective-permute-done.5.refs_2_ = bf16[128,1024]{1,0:T(8,128)(2,1)S(1)} collective-permute-done((bf16[128,1024]{1,0:T(8,128)(2,1)}, bf16[128,1024]{1,0:T(8,128)(2,1)S(1)}, u32[]{:S(2)}, u32[]{:S(2)}) %collective-permute-start.5) | collective-permute-done | bytes 262176 | tf_op jit(solution)/shard_map/ppermute | solution.py:23
  34.6 3.4 %collective-permute-done.7.refs_3_ = bf16[128,1024]{1,0:T(8,128)(2,1)S(1)} collective-permute-done((bf16[128,1024]{1,0:T(8,128)(2,1)}, bf16[128,1024]{1,0:T(8,128)(2,1)S(1)}, u32[]{:S(2)}, u32[]{:S(2)}) %collective-permute-start.7) | collective-permute-done | bytes 262176 | tf_op jit(solution)/shard_map/ppermute | solution.py:23
  46.5 3.6 %shard_map.129 = (bf16[384,512]{1,0:T(8,128)(2,1)S(1)}, bf16[384,512]{1,0:T(8,128)(2,1)S(1)}, bf16[384,512]{1,0:T(8,128)(2,1)S(1)}) custom-call(bf16[96,1024]{1,0:T(8,128)(2,1)S(1)} %copy-done.8, bf16[96,1024]{1,0:T(8,128)(2,1)S(1)} %copy-done.9, bf16[96,1024]{1,0:T(8,128)(2,1)S(1)} %collective-permute-done.9.refs_2_, ...), custom_call_target="tpu_custom_call" | custom-call | tf_op jit(solution)/shard_map/pallas_call | solution.py:151
  50.1 4.7 %shard_map.130 = (f32[96,2048]{1,0:T(8,128)S(1)}, f32[96,2048]{1,0:T(8,128)S(1)}, bf16[96,2048]{1,0:T(8,128)(2,1)S(1)}, bf16[96,2048]{1,0:T(8,128)(2,1)S(1)}) custom-call(s32[1]{0:T(128)S(6)} %copy.14.traded, bf16[384,512]{1,0:T(8,128)(2,1)S(1)} %get-tuple-element.117.q, bf16[384,512]{1,0:T(8,128)(2,1)S(1)} %get-tuple-element.118.k, ...), custom_call_target="tpu_custom_call" | custom-call | tf_op jit(solution)/shard_map/pallas_call | solution.py:247
  63.0 7.2 %collective-permute-done.17 = bf16[96,2048]{1,0:T(8,128)(2,1)S(1)} collective-permute-done((bf16[96,2048]{1,0:T(8,128)(2,1)S(1)}, bf16[96,2048]{1,0:T(8,128)(2,1)S(1)}, u32[]{:S(2)}, u32[]{:S(2)}) %collective-permute-start.17) | collective-permute-done | bytes 393248 | tf_op jit(solution)/shard_map/ppermute | solution.py:23
  76.2 5.3 %collective-permute-done.21.refs_4_ = bf16[96,2048]{1,0:T(8,128)(2,1)S(1)} collective-permute-done((bf16[96,2048]{1,0:T(8,128)(2,1)S(1)}, bf16[96,2048]{1,0:T(8,128)(2,1)S(1)}, u32[]{:S(2)}, u32[]{:S(2)}) %collective-permute-start.21) | collective-permute-done | bytes 393248 | tf_op jit(solution)/shard_map/ppermute | solution.py:23
  83.1 10.9 %collective-permute-done.19.refs_16_.refs_8_ = bf16[1024,512]{1,0:T(8,128)(2,1)S(1)} collective-permute-done((bf16[1024,512]{1,0:T(8,128)(2,1)S(1)}, bf16[1024,512]{1,0:T(8,128)(2,1)S(1)}, u32[]{:S(2)}, u32[]{:S(2)}) %collective-permute-start.19) | collective-permute-done | bytes 1048608 | tf_op jit(solution)/shard_map/ppermute | solution.py:23
  96.7 2.4 %collective-permute-start.34 = (bf16[512,512]{1,0:T(8,128)(2,1)S(1)}, bf16[512,512]{1,0:T(8,128)(2,1)S(1)}, u32[]{:S(2)}, u32[]{:S(2)}) collective-permute-start(bf16[512,512]{1,0:T(8,128)(2,1)S(1)} %get-tuple-element.156), channel_id=1, source_target_pairs={{0,4},{4,0},{8,12},{12,8},{1,5},{5,1},{9,13},{13,9},{2,6},{6,2},{1... | collective-permute-start | bytes 1572872 | tf_op jit(solution)/shard_map/ppermute | solution.py:23
  101.0 5.2 %collective-permute-done.29.refs_10_ = bf16[96,2048]{1,0:T(8,128)(2,1)S(1)} collective-permute-done((bf16[96,2048]{1,0:T(8,128)(2,1)S(1)}, bf16[96,2048]{1,0:T(8,128)(2,1)S(1)}, u32[]{:S(2)}, u32[]{:S(2)}) %collective-permute-start.29) | collective-permute-done | bytes 393248 | tf_op jit(solution)/shard_map/ppermute | solution.py:23
  107.9 6.6 %shard_map.132 = (bf16[384,512]{1,0:T(8,128)(2,1)S(1)}, bf16[384,512]{1,0:T(8,128)(2,1)S(1)}, bf16[384,512]{1,0:T(8,128)(2,1)S(1)}) custom-call(s32[5]{0:T(128)S(1)} %copy-done.10, bf16[96,2048]{1,0:T(8,128)(2,1)S(1)} %fusion.3.refs_0_, bf16[96,2048]{1,0:T(8,128)(2,1)S(1)} %collective-permute-done.24.refs_1_, ...), custom_call_target="tpu_custom_call" | custom-call | tf_op jit(solution)/shard_map/pallas_call | solution.py:301
  114.5 6.8 %collective-permute-done.34.refs_3_ = bf16[512,512]{1,0:T(8,128)(2,1)S(1)} collective-permute-done((bf16[512,512]{1,0:T(8,128)(2,1)S(1)}, bf16[512,512]{1,0:T(8,128)(2,1)S(1)}, u32[]{:S(2)}, u32[]{:S(2)}) %collective-permute-start.34) | collective-permute-done | bytes 524320 | tf_op jit(solution)/shard_map/ppermute | solution.py:23
  121.3 3.0 %collective-permute-done.35.refs_4_ = bf16[512,512]{1,0:T(8,128)(2,1)S(1)} collective-permute-done((bf16[512,512]{1,0:T(8,128)(2,1)S(1)}, bf16[512,512]{1,0:T(8,128)(2,1)S(1)}, u32[]{:S(2)}, u32[]{:S(2)}) %collective-permute-start.35) | collective-permute-done | bytes 524320 | tf_op jit(solution)/shard_map/ppermute | solution.py:23
  126.5 2.9 %shard_map.133.refs_0_ = bf16[384,512]{1,0:T(8,128)(2,1)S(1)} custom-call(s32[5]{0:T(128)S(1)} %copy-done.10, bf16[96,2048]{1,0:T(8,128)(2,1)S(1)} %collective-permute-done.23.refs_0_, bf16[96,2048]{1,0:T(8,128)(2,1)S(1)} %collective-permute-done.31.refs_1_, bf16[96,2048]{1,0:T(8,128)(2,1)S(1)} %collective-permute-done.32.refs_2_, ...), custom_call_target="tpu_custom_call" | custom-call | tf_op jit(solution)/shard_map/pallas_call | solution.py:301
  129.4 6.2 %collective-permute-done.36.refs_5_ = bf16[512,512]{1,0:T(8,128)(2,1)S(1)} collective-permute-done((bf16[512,512]{1,0:T(8,128)(2,1)S(1)}, bf16[512,512]{1,0:T(8,128)(2,1)S(1)}, u32[]{:S(2)}, u32[]{:S(2)}) %collective-permute-start.36) | collective-permute-done | bytes 524320 | tf_op jit(solution)/shard_map/ppermute | solution.py:23
  135.6 2.6 %shard_map.134 = (f32[96,2048]{1,0:T(8,128)S(1)}, f32[96,2048]{1,0:T(8,128)S(1)}, bf16[96,2048]{1,0:T(8,128)(2,1)S(1)}, bf16[96,2048]{1,0:T(8,128)(2,1)S(1)}, f3...) custom-call(s32[5]{0:T(128)S(1)} %copy-done.10, ...), custom_call_target="tpu_custom_call" | custom-call | tf_op jit(solution)/shard_map/pallas_call | solution.py:336
  141.8 2.8 %shard_map.135 = (f32[96,2048]{1,0:T(8,128)S(1)}, f32[96,2048]{1,0:T(8,128)S(1)}, bf16[96,2048]{1,0:T(8,128)(2,1)S(1)}, bf16[96,2048]{1,0:T(8,128)(2,1)S(1)}, f3...) custom-call(s32[5]{0:T(128)S(1)} %copy-done.10, ...), custom_call_target="tpu_custom_call" | custom-call | flops 99999997952 | tf_op jit(solution)/shard_map/pallas_call | solution.py:336
  144.6 6.7 %collective-permute-done.38 = bf16[96,2048]{1,0:T(8,128)(2,1)S(1)} collective-permute-done((bf16[96,2048]{1,0:T(8,128)(2,1)S(1)}, bf16[96,2048]{1,0:T(8,128)(2,1)S(1)}, u32[]{:S(2)}, u32[]{:S(2)}) %collective-permute-start.38) | collective-permute-done | bytes 393248 | tf_op jit(solution)/shard_map/ppermute | solution.py:23
  155.6 8.5 %collective-permute-done.48 = bf16[96,2048]{1,0:T(8,128)(2,1)S(1)} collective-permute-done((bf16[96,2048]{1,0:T(8,128)(2,1)S(1)}, bf16[96,2048]{1,0:T(8,128)(2,1)S(1)}, u32[]{:S(2)}, u32[]{:S(2)}) %collective-permute-start.48) | collective-permute-done | bytes 393248 | tf_op jit(solution)/shard_map/ppermute | solution.py:23
  167.5 4.9 %collective-permute-done.46 = bf16[96,2048]{1,0:T(8,128)(2,1)S(1)} collective-permute-done((bf16[96,2048]{1,0:T(8,128)(2,1)S(1)}, bf16[96,2048]{1,0:T(8,128)(2,1)S(1)}, u32[]{:S(2)}, u32[]{:S(2)}) %collective-permute-start.46) | collective-permute-done | bytes 393248 | tf_op jit(solution)/shard_map/ppermute | solution.py:23
  174.7 10.4 %collective-permute-done.52 = bf16[96,2048]{1,0:T(8,128)(2,1)S(1)} collective-permute-done((bf16[96,2048]{1,0:T(8,128)(2,1)S(1)}, bf16[96,2048]{1,0:T(8,128)(2,1)S(1)}, u32[]{:S(2)}, u32[]{:S(2)}) %collective-permute-start.52) | collective-permute-done | bytes 393248 | tf_op jit(solution)/shard_map/ppermute | solution.py:23
  (137 shorter events, 62.1 us)
Async XLA Ops:
  6.8 50.2 %collective-permute-start.14 = (bf16[1024,512]{1,0:T(8,128)(2,1)}, bf16[1024,512]{1,0:T(8,128)(2,1)S(1)}, u32[]{:S(2)}, u32[]{:S(2)}) collective-permute-start(bf16[1024,512]{1,0:T(8,128)(2,1)} %get-tuple-element.132), channel_id=1, source_target_pairs={{0,8},{4,12},{8,0},{12,4},{1,9},{5,13},{9,1},{13,5},{2,10},{6,14},... | collective-permute-start | bytes 3145736 | tf_op jit(solution)/shard_map/ppermute | solution.py:23
  10.4 46.7 %collective-permute-start.13 = (bf16[1024,512]{1,0:T(8,128)(2,1)}, bf16[1024,512]{1,0:T(8,128)(2,1)S(1)}, u32[]{:S(2)}, u32[]{:S(2)}) collective-permute-start(bf16[1024,512]{1,0:T(8,128)(2,1)} %get-tuple-element.131), channel_id=1, source_target_pairs={{0,4},{4,0},{8,12},{12,8},{1,5},{5,1},{9,13},{13,9},{2,6},{6,2},{1... | collective-permute-start | bytes 3145736 | tf_op jit(solution)/shard_map/ppermute | solution.py:23
  28.1 11.3 %collective-permute-start.11 = (bf16[96,1024]{1,0:T(8,128)(2,1)S(1)}, bf16[96,1024]{1,0:T(8,128)(2,1)S(1)}, u32[]{:S(2)}, u32[]{:S(2)}) collective-permute-start(bf16[96,1024]{1,0:T(8,128)(2,1)S(1)} %collective-permute-done.refs_4_), channel_id=1, source_target_pairs={{0,1},{1,0},{2,3},{3,2},{4,5},{5,4},{6,7},{7,6},{8,9},{9,8},{10,11... | collective-permute-start | bytes 589832 | tf_op jit(solution)/shard_map/ppermute | solution.py:23
  33.1 17.0 %collective-permute-start.6 = (bf16[128,1024]{1,0:T(8,128)(2,1)S(1)}, bf16[128,1024]{1,0:T(8,128)(2,1)S(1)}, u32[]{:S(2)}, u32[]{:S(2)}) collective-permute-start(bf16[128,1024]{1,0:T(8,128)(2,1)S(1)} %collective-permute-done.5.refs_2_), channel_id=1, source_target_pairs={{0,16},{16,0},{1,17},{17,1},{2,18},{18,2},{3,19},{19,3},{4,20},{20... | collective-permute-start | bytes 786440 | tf_op jit(solution)/shard_map/ppermute | solution.py:23
  37.9 12.2 %collective-permute-start.8 = (bf16[128,1024]{1,0:T(8,128)(2,1)S(1)}, bf16[128,1024]{1,0:T(8,128)(2,1)S(1)}, u32[]{:S(2)}, u32[]{:S(2)}) collective-permute-start(bf16[128,1024]{1,0:T(8,128)(2,1)S(1)} %collective-permute-done.7.refs_3_), channel_id=1, source_target_pairs={{0,16},{16,0},{1,17},{17,1},{2,18},{18,2},{3,19},{19,3},{4,20},{20... | collective-permute-start | bytes 786440 | tf_op jit(solution)/shard_map/ppermute | solution.py:23
  60.6 33.3 %collective-permute-start.19 = (bf16[1024,512]{1,0:T(8,128)(2,1)S(1)}, bf16[1024,512]{1,0:T(8,128)(2,1)S(1)}, u32[]{:S(2)}, u32[]{:S(2)}) collective-permute-start(bf16[1024,512]{1,0:T(8,128)(2,1)S(1)} %collective-permute-done.14.refs_15_.refs_7_), channel_id=1, source_target_pairs={{0,4},{4,0},{8,12},{12,8},{1,5},{5,1},{9,13},{13,9},{2,6},{6,2},{1... | collective-permute-start | bytes 3145736 | tf_op jit(solution)/shard_map/ppermute | solution.py:23
  72.7 21.3 %collective-permute-start.20 = (bf16[96,2048]{1,0:T(8,128)(2,1)S(1)}, bf16[96,2048]{1,0:T(8,128)(2,1)S(1)}, u32[]{:S(2)}, u32[]{:S(2)}) collective-permute-start(bf16[96,2048]{1,0:T(8,128)(2,1)S(1)} %fusion.3.refs_0_), channel_id=1, source_target_pairs={{0,2},{1,3},{2,0},{3,1},{4,6},{5,7},{6,4},{7,5},{8,10},{9,11},{10,... | collective-permute-start | bytes 1179656 | tf_op jit(solution)/shard_map/ppermute | solution.py:23
  74.2 19.8 %collective-permute-start.18 = (bf16[96,2048]{1,0:T(8,128)(2,1)S(1)}, bf16[96,2048]{1,0:T(8,128)(2,1)S(1)}, u32[]{:S(2)}, u32[]{:S(2)}) collective-permute-start(bf16[96,2048]{1,0:T(8,128)(2,1)S(1)} %fusion.3.refs_0_), channel_id=1, source_target_pairs={{0,8},{4,12},{8,0},{12,4},{1,9},{5,13},{9,1},{13,5},{2,10},{6,14},... | collective-permute-start | bytes 1179656 | tf_op jit(solution)/shard_map/ppermute | solution.py:23
  81.5 12.5 %collective-permute-start.22 = (bf16[96,2048]{1,0:T(8,128)(2,1)S(1)}, bf16[96,2048]{1,0:T(8,128)(2,1)S(1)}, u32[]{:S(2)}, u32[]{:S(2)}) collective-permute-start(bf16[96,2048]{1,0:T(8,128)(2,1)S(1)} %collective-permute-done.21.refs_4_), channel_id=1, source_target_pairs={{0,2},{1,3},{2,0},{3,1},{4,6},{5,7},{6,4},{7,5},{8,10},{9,11},{10,... | collective-permute-start | bytes 1179656 | tf_op jit(solution)/shard_map/ppermute | solution.py:23
  83.1 12.0 %collective-permute-start.24 = (bf16[96,2048]{1,0:T(8,128)(2,1)S(1)}, bf16[96,2048]{1,0:T(8,128)(2,1)S(1)}, u32[]{:S(2)}, u32[]{:S(2)}) collective-permute-start(bf16[96,2048]{1,0:T(8,128)(2,1)S(1)} %fusion.3.refs_0_), channel_id=1, source_target_pairs={{0,1},{1,0},{2,3},{3,2},{4,5},{5,4},{6,7},{7,6},{8,9},{9,8},{10,11... | collective-permute-start | bytes 1179656 | tf_op jit(solution)/shard_map/ppermute | solution.py:23
  94.7 11.5 %collective-permute-start.29 = (bf16[96,2048]{1,0:T(8,128)(2,1)S(1)}, bf16[96,2048]{1,0:T(8,128)(2,1)S(1)}, u32[]{:S(2)}, u32[]{:S(2)}) collective-permute-start(bf16[96,2048]{1,0:T(8,128)(2,1)S(1)} %collective-permute-done.18.refs_8_), channel_id=1, source_target_pairs={{0,2},{1,3},{2,0},{3,1},{4,6},{5,7},{6,4},{7,5},{8,10},{9,11},{10,... | collective-permute-start | bytes 1179656 | tf_op jit(solution)/shard_map/ppermute | solution.py:23
  96.7 24.6 %collective-permute-start.34 = (bf16[512,512]{1,0:T(8,128)(2,1)S(1)}, bf16[512,512]{1,0:T(8,128)(2,1)S(1)}, u32[]{:S(2)}, u32[]{:S(2)}) collective-permute-start(bf16[512,512]{1,0:T(8,128)(2,1)S(1)} %get-tuple-element.156), channel_id=1, source_target_pairs={{0,4},{4,0},{8,12},{12,8},{1,5},{5,1},{9,13},{13,9},{2,6},{6,2},{1... | collective-permute-start | bytes 1572872 | tf_op jit(solution)/shard_map/ppermute | solution.py:23
  99.1 25.2 %collective-permute-start.35 = (bf16[512,512]{1,0:T(8,128)(2,1)S(1)}, bf16[512,512]{1,0:T(8,128)(2,1)S(1)}, u32[]{:S(2)}, u32[]{:S(2)}) collective-permute-start(bf16[512,512]{1,0:T(8,128)(2,1)S(1)} %get-tuple-element.158), channel_id=1, source_target_pairs={{0,8},{4,12},{8,0},{12,4},{1,9},{5,13},{9,1},{13,5},{2,10},{6,14},... | collective-permute-start | bytes 1572872 | tf_op jit(solution)/shard_map/ppermute | solution.py:23
  106.3 18.0 %collective-permute-start.32 = (bf16[96,2048]{1,0:T(8,128)(2,1)S(1)}, bf16[96,2048]{1,0:T(8,128)(2,1)S(1)}, u32[]{:S(2)}, u32[]{:S(2)}) collective-permute-start(bf16[96,2048]{1,0:T(8,128)(2,1)S(1)} %collective-permute-done.23.refs_0_), channel_id=1, source_target_pairs={{0,2},{1,3},{2,0},{3,1},{4,6},{5,7},{6,4},{7,5},{8,10},{9,11},{10,... | collective-permute-start | bytes 1179656 | tf_op jit(solution)/shard_map/ppermute | solution.py:23
  124.2 11.4 %collective-permute-start.36 = (bf16[512,512]{1,0:T(8,128)(2,1)S(1)}, bf16[512,512]{1,0:T(8,128)(2,1)S(1)}, u32[]{:S(2)}, u32[]{:S(2)}) collective-permute-start(bf16[512,512]{1,0:T(8,128)(2,1)S(1)} %collective-permute-done.35.refs_4_), channel_id=1, source_target_pairs={{0,4},{4,0},{8,12},{12,8},{1,5},{5,1},{9,13},{13,9},{2,6},{6,2},{1... | collective-permute-start | bytes 1572872 | tf_op jit(solution)/shard_map/ppermute | solution.py:23
  138.8 12.5 %collective-permute-start.40 = (bf16[96,2048]{1,0:T(8,128)(2,1)S(1)}, bf16[96,2048]{1,0:T(8,128)(2,1)S(1)}, u32[]{:S(2)}, u32[]{:S(2)}) collective-permute-start(bf16[96,2048]{1,0:T(8,128)(2,1)S(1)} %get-tuple-element.186), channel_id=1, source_target_pairs={{0,1},{1,0},{2,3},{3,2},{4,5},{5,4},{6,7},{7,6},{8,9},{9,8},{10,11... | collective-permute-start | bytes 1179656 | tf_op jit(solution)/shard_map/ppermute | solution.py:23
  152.1 12.0 %collective-permute-start.48 = (bf16[96,2048]{1,0:T(8,128)(2,1)S(1)}, bf16[96,2048]{1,0:T(8,128)(2,1)S(1)}, u32[]{:S(2)}, u32[]{:S(2)}) collective-permute-start(bf16[96,2048]{1,0:T(8,128)(2,1)S(1)} %add_convert_fusion.4), channel_id=1, source_target_pairs={{0,2},{1,3},{2,0},{3,1},{4,6},{5,7},{6,4},{7,5},{8,10},{9,11},{10,... | collective-permute-start | bytes 1179656 | tf_op jit(solution)/shard_map/ppermute | solution.py:23
  154.1 13.4 %collective-permute-start.45 = (bf16[96,2048]{1,0:T(8,128)(2,1)S(1)}, bf16[96,2048]{1,0:T(8,128)(2,1)S(1)}, u32[]{:S(2)}, u32[]{:S(2)}) collective-permute-start(bf16[96,2048]{1,0:T(8,128)(2,1)S(1)} %get-tuple-element.199), channel_id=1, source_target_pairs={{0,1},{1,0},{2,3},{3,2},{4,5},{5,4},{6,7},{7,6},{8,9},{9,8},{10,11... | collective-permute-start | bytes 1179656 | tf_op jit(solution)/shard_map/ppermute | solution.py:23
  154.2 18.3 %collective-permute-start.46 = (bf16[96,2048]{1,0:T(8,128)(2,1)S(1)}, bf16[96,2048]{1,0:T(8,128)(2,1)S(1)}, u32[]{:S(2)}, u32[]{:S(2)}) collective-permute-start(bf16[96,2048]{1,0:T(8,128)(2,1)S(1)} %add_convert_fusion.2), channel_id=1, source_target_pairs={{0,2},{1,3},{2,0},{3,1},{4,6},{5,7},{6,4},{7,5},{8,10},{9,11},{10,... | collective-permute-start | bytes 1179656 | tf_op jit(solution)/shard_map/ppermute | solution.py:23
  155.3 19.4 %collective-permute-start.42 = (bf16[96,2048]{1,0:T(8,128)(2,1)S(1)}, bf16[96,2048]{1,0:T(8,128)(2,1)S(1)}, u32[]{:S(2)}, u32[]{:S(2)}) collective-permute-start(bf16[96,2048]{1,0:T(8,128)(2,1)S(1)} %get-tuple-element.195), channel_id=1, source_target_pairs={{0,1},{1,0},{2,3},{3,2},{4,5},{5,4},{6,7},{7,6},{8,9},{9,8},{10,11... | collective-permute-start | bytes 1179656 | tf_op jit(solution)/shard_map/ppermute | solution.py:23
  164.6 20.6 %collective-permute-start.52 = (bf16[96,2048]{1,0:T(8,128)(2,1)S(1)}, bf16[96,2048]{1,0:T(8,128)(2,1)S(1)}, u32[]{:S(2)}, u32[]{:S(2)}) collective-permute-start(bf16[96,2048]{1,0:T(8,128)(2,1)S(1)} %add_convert_fusion), channel_id=1, source_target_pairs={{0,8},{4,12},{8,0},{12,4},{1,9},{5,13},{9,1},{13,5},{2,10},{6,14},... | collective-permute-start | bytes 1179656 | tf_op jit(solution)/shard_map/ppermute | solution.py:23
  166.0 19.2 %collective-permute-start.44 = (bf16[96,2048]{1,0:T(8,128)(2,1)S(1)}, bf16[96,2048]{1,0:T(8,128)(2,1)S(1)}, u32[]{:S(2)}, u32[]{:S(2)}) collective-permute-start(bf16[96,2048]{1,0:T(8,128)(2,1)S(1)} %add_convert_fusion.1), channel_id=1, source_target_pairs={{0,2},{1,3},{2,0},{3,1},{4,6},{5,7},{6,4},{7,5},{8,10},{9,11},{10,... | collective-permute-start | bytes 1179656 | tf_op jit(solution)/shard_map/ppermute | solution.py:23
  172.6 12.5 %collective-permute-start.50 = (bf16[96,1024]{1,0:T(8,128)(2,1)S(1)}, bf16[96,1024]{1,0:T(8,128)(2,1)S(1)}, u32[]{:S(2)}, u32[]{:S(2)}) collective-permute-start(bf16[96,1024]{1,0:T(8,128)(2,1)S(1)} %get-tuple-element.205), channel_id=1, source_target_pairs={{0,16},{16,0},{1,17},{17,1},{2,18},{18,2},{3,19},{19,3},{4,20},{20... | collective-permute-start | bytes 589832 | tf_op jit(solution)/shard_map/ppermute | solution.py:23
  173.8 11.4 %collective-permute-start.51 = (bf16[96,1024]{1,0:T(8,128)(2,1)S(1)}, bf16[96,1024]{1,0:T(8,128)(2,1)S(1)}, u32[]{:S(2)}, u32[]{:S(2)}) collective-permute-start(bf16[96,1024]{1,0:T(8,128)(2,1)S(1)} %get-tuple-element.206), channel_id=1, source_target_pairs={{0,16},{16,0},{1,17},{17,1},{2,18},{18,2},{3,19},{19,3},{4,20},{20... | collective-permute-start | bytes 589832 | tf_op jit(solution)/shard_map/ppermute | solution.py:23
  (44 other events, 493.9 us)

commit v6 on v5

--- a/solution.py
+++ b/solution.py
@@ -354,9 +354,16 @@
     return [rows, swap(rows, "mp", 1), across, swap(across, "mp", 1)]
 
 
-def reduce_rows(own, across, far_own, far_across):
-    sent = (across + swap(far_across, "mp", 1).astype(jnp.float32)).astype(jnp.bfloat16)
-    return (own, swap(far_own, "mp", 1)), swap(sent, "mp", 2), sent
+def reduce_rows(own, across, far_own, far_across, edges=()):
+    came = swap(far_across, "mp", 1)
+    bounds = [0, *edges, own.shape[1]]
+    sent = [
+        (across[:, begin:end] + came[:, begin:end].astype(jnp.float32)).astype(jnp.bfloat16)
+        for begin, end in zip(bounds, bounds[1:])
+    ]
+    other = swap(far_own, "mp", 1)
+    kept = [(own[:, begin:end], other[:, begin:end]) for begin, end in zip(bounds, bounds[1:])]
+    return kept, [swap(part, "mp", 2) for part in sent], sent
 
 
 def total(kept, came):
@@ -488,7 +495,7 @@
     came, q = join(came, q)
     sums = attend(traded, q, k, v, blocks, came, facts[2], facts[3], output_weight)
     sums, wide = join(sums, wide)
-    kept, came, sent = reduce_rows(*sums)
+    (kept,), (came,), (sent,) = reduce_rows(*sums)
     down_cut = cut(info, after(down_weight, sent))
     kept, came, down_cut = join(kept, came, down_cut)
     wide.update(far_side({pair: wide[pair]}))
@@ -501,8 +508,9 @@
     rows_z, wide, over_chip = join(rows_z, wide, over_chip)
     parts = gather_rows(normed_own, over_chip[0]) + gather_rows(rows_x, over_chip[1])
     rows_both = swap(rows_z, "rep", 1)
-    back = {**across(after(down_cut[0], rows_z)), **near_side(after(down_cut[1], rows_z))}
-    parts += gather_rows(rows_z)
+    rows_z = gather_rows(rows_z)
+    back = {**across(after(down_cut[0], rows_z[0])), **near_side(after(down_cut[1], rows_z[1]))}
+    parts += rows_z
     masks = [0] + list(wide)
     in_order = lambda held: [held[mask] for mask in masks[1:]]
     acts = gate_up(masks, info, parts, gate_weight, up_weight, in_order(wide))
@@ -518,20 +526,24 @@
     def crossed(value, axis, mask):
         return swap(value.astype(jnp.bfloat16), axis, mask).astype(jnp.float32)
 
+    edges = (tokens.shape[1] * 5 // 8,)
     found_both, found_z = sums_of(acts[3], acts[2])
-    kept, came, sent = reduce_rows(*found_both)
-    kept_z, came_z, sent_z = reduce_rows(*found_z)
-    found_x, found = sums_of(after(acts[1], sent, sent_z), acts[0], gate=True)
-    came, found_x, found = join(came, found_x, found)
-    of_both, of_z = total(kept, came), total(kept_z, came_z)
-    of_both = of_both.astype(jnp.bfloat16)
-    sent = (of_z + crossed(of_both, "rep", 1)).astype(jnp.bfloat16)
-    of_z = swap(sent, "dp", pair).astype(jnp.float32)
-    found_x, found = after((found_x, found), of_both)
-    kept, came, sent_x = reduce_rows(*found_x)
+    kept, came, sent = reduce_rows(*found_both, edges)
+    kept_z, came_z, sent_z = reduce_rows(*found_z, edges)
+    found_x, found = sums_of(after(acts[1], *sent, *sent_z), acts[0], gate=True)
+    came[0], found_x, found = join(came[0], found_x, found)
+    of_both = [total(*terms).astype(jnp.bfloat16) for terms in zip(kept, came)]
+    of_z = [total(*terms) for terms in zip(kept_z, came_z)]
+    sent = [
+        (part + crossed(more, "rep", 1)).astype(jnp.bfloat16) for part, more in zip(of_z, of_both)
+    ]
+    of_z = jnp.concatenate([swap(part, "dp", pair) for part in sent], axis=1).astype(jnp.float32)
+    found_x, found = after((found_x, found), *of_both)
+    (kept,), (came,), sent_x = reduce_rows(*found_x)
     of_x = total(kept, came)
-    of_own = total(*reduce_rows(*after(found, sent_x))[:2])
-    of_x = after(of_x, sent)
+    (kept,), (came,), _ = reduce_rows(*after(found, *sent_x))
+    of_own = total(kept, came)
+    of_x = after(of_x, *sent)
     columns = of_x.shape[1]
     of_x = [crossed(of_x[:, at : at + columns // 2], "rep", 1) for at in (0, columns // 2)]
     of_own = of_own + jnp.concatenate(of_x, axis=1)

time: 187 us -> 185 us (0.989)
  waiting for transfers between devices: 98.3 us -> 89.8 us
  starting transfers between devices: 47.6 us -> 54.9 us
    ppermute x53 -> x57, waiting for transfers between devices: 98.3 us -> 89.8 us  [swap(): return lax.ppermute(value, axis, pairs)]
    ppermute x53 -> x57, starting transfers between devices: 47.6 us -> 54.9 us  [swap(): return lax.ppermute(value, axis, pairs)]
  transfers between devices with their start and end apart: 53 -> 57, of which waited for: 24 -> 26; matrix products, arithmetic and copies ran while one was open for 1% -> 1% of each run, Pallas kernels for 13% -> 13%
where the time goes in v6:
time: 185 us
  waiting for transfers between devices  89.8 us (49%)
  starting transfers between devices  54.9 us (30%)
  Pallas kernels  30.8 us (17%)
  local copies, waits for them, and re-layouts  5.77 us (3%)
  other arithmetic  2.74 us (1%)
    ppermute x57, waiting for transfers between devices, swap(): return lax.ppermute(value, axis, pairs)  89.8 us
    ppermute x57, starting transfers between devices, swap(): return lax.ppermute(value, axis, pairs)  54.9 us
    pallas_call x2, Pallas kernels, gate_up(): pl.pallas_call(body, in_specs=[smem()] + [vmem()] * blocks + [anywhere()]...  9.43 us
    pallas_call x2, Pallas kernels, down_rows(): pl.pallas_call(body, in_specs=[smem()] + [vmem()] * groups + [anywhere()]...  5.46 us
    unnamed x30, local copies, waits for them, and re-layouts  5.08 us
    pallas_call x1, Pallas kernels, prepare(): pl.pallas_call(body, in_specs=[smem(), vmem(), vmem()] + [anywhere()] * s...  4.87 us
    pallas_call x1, Pallas kernels, attend(): pl.pallas_call(attend_body, in_specs=[smem()] + [vmem()] * 3 + [anywhere(...  4.74 us
  transfers between devices with their start and end apart: 57, of which 26 were waited for; matrix products, arithmetic and copies ran while one was open for 1% of the time, Pallas kernels for 13%

profile of v6, /device:TPU:0, one launch (start us, length us, event | category | flops | bytes accessed | tf_op | source)
XLA Modules:
  0.0 185.1 jit_solution(18009496462400322719)
XLA Ops:
  1.3 4.9 %shard_map.127 = (bf16[96,1024]{1,0:T(8,128)(2,1)}, bf16[96,1024]{1,0:T(8,128)(2,1)}, bf16[128,1024]{1,0:T(8,128)(2,1)}, bf16[128,1024]{1,0:T(8,128)(2,1)}, bf16...) custom-call(s32[5]{0:T(128)} %stack.23.info_ref.info, ...), custom_call_target="tpu_custom_call" | custom-call | tf_op jit(solution)/shard_map/pallas_call | solution.py:71
  6.7 3.7 %collective-permute-start.14 = (bf16[1024,512]{1,0:T(8,128)(2,1)}, bf16[1024,512]{1,0:T(8,128)(2,1)S(1)}, u32[]{:S(2)}, u32[]{:S(2)}) collective-permute-start(bf16[1024,512]{1,0:T(8,128)(2,1)} %get-tuple-element.132), channel_id=1, source_target_pairs={{0,8},{4,12},{8,0},{12,4},{1,9},{5,13},{9,1},{13,5},{2,10},{6,14},... | collective-permute-start | bytes 3145736 | tf_op jit(solution)/shard_map/ppermute | solution.py:23
  14.0 6.0 %collective-permute-done.refs_4_ = bf16[96,1024]{1,0:T(8,128)(2,1)S(1)} collective-permute-done((bf16[96,1024]{1,0:T(8,128)(2,1)}, bf16[96,1024]{1,0:T(8,128)(2,1)S(1)}, u32[]{:S(2)}, u32[]{:S(2)}) %collective-permute-start) | collective-permute-done | bytes 196640 | tf_op jit(solution)/shard_map/ppermute | solution.py:23
  24.6 3.8 %collective-permute-done.2.refs_4_ = bf16[128,1024]{1,0:T(8,128)(2,1)S(1)} collective-permute-done((bf16[128,1024]{1,0:T(8,128)(2,1)}, bf16[128,1024]{1,0:T(8,128)(2,1)S(1)}, u32[]{:S(2)}, u32[]{:S(2)}) %collective-permute-start.2) | collective-permute-done | bytes 262176 | tf_op jit(solution)/shard_map/ppermute | solution.py:23
  36.5 4.4 %collective-permute-done.7.refs_3_ = bf16[128,1024]{1,0:T(8,128)(2,1)S(1)} collective-permute-done((bf16[128,1024]{1,0:T(8,128)(2,1)}, bf16[128,1024]{1,0:T(8,128)(2,1)S(1)}, u32[]{:S(2)}, u32[]{:S(2)}) %collective-permute-start.7) | collective-permute-done | bytes 262176 | tf_op jit(solution)/shard_map/ppermute | solution.py:23
  49.3 3.6 %shard_map.129 = (bf16[384,512]{1,0:T(8,128)(2,1)S(1)}, bf16[384,512]{1,0:T(8,128)(2,1)S(1)}, bf16[384,512]{1,0:T(8,128)(2,1)S(1)}) custom-call(bf16[96,1024]{1,0:T(8,128)(2,1)S(1)} %copy-done.8, bf16[96,1024]{1,0:T(8,128)(2,1)S(1)} %copy-done.9, bf16[96,1024]{1,0:T(8,128)(2,1)S(1)} %collective-permute-done.9.refs_2_, ...), custom_call_target="tpu_custom_call" | custom-call | tf_op jit(solution)/shard_map/pallas_call | solution.py:151
  53.0 4.7 %shard_map.130 = (f32[96,2048]{1,0:T(8,128)S(1)}, f32[96,2048]{1,0:T(8,128)S(1)}, bf16[96,2048]{1,0:T(8,128)(2,1)S(1)}, bf16[96,2048]{1,0:T(8,128)(2,1)S(1)}) custom-call(s32[1]{0:T(128)S(6)} %copy.14.traded, bf16[384,512]{1,0:T(8,128)(2,1)S(1)} %get-tuple-element.117.q, bf16[384,512]{1,0:T(8,128)(2,1)S(1)} %get-tuple-element.118.k, ...), custom_call_target="tpu_custom_call" | custom-call | tf_op jit(solution)/shard_map/pallas_call | solution.py:247
  63.0 8.2 %collective-permute-done.17 = bf16[96,2048]{1,0:T(8,128)(2,1)S(1)} collective-permute-done((bf16[96,2048]{1,0:T(8,128)(2,1)S(1)}, bf16[96,2048]{1,0:T(8,128)(2,1)S(1)}, u32[]{:S(2)}, u32[]{:S(2)}) %collective-permute-start.17) | collective-permute-done | bytes 393248 | tf_op jit(solution)/shard_map/ppermute | solution.py:23
  76.1 6.6 %collective-permute-done.21.refs_4_ = bf16[96,2048]{1,0:T(8,128)(2,1)S(1)} collective-permute-done((bf16[96,2048]{1,0:T(8,128)(2,1)S(1)}, bf16[96,2048]{1,0:T(8,128)(2,1)S(1)}, u32[]{:S(2)}, u32[]{:S(2)}) %collective-permute-start.21) | collective-permute-done | bytes 393248 | tf_op jit(solution)/shard_map/ppermute | solution.py:23
  83.9 10.7 %collective-permute-done.19.refs_16_.refs_8_ = bf16[1024,512]{1,0:T(8,128)(2,1)S(1)} collective-permute-done((bf16[1024,512]{1,0:T(8,128)(2,1)S(1)}, bf16[1024,512]{1,0:T(8,128)(2,1)S(1)}, u32[]{:S(2)}, u32[]{:S(2)}) %collective-permute-start.19) | collective-permute-done | bytes 1048608 | tf_op jit(solution)/shard_map/ppermute | solution.py:23
  101.5 5.2 %collective-permute-done.29.refs_10_ = bf16[96,2048]{1,0:T(8,128)(2,1)S(1)} collective-permute-done((bf16[96,2048]{1,0:T(8,128)(2,1)S(1)}, bf16[96,2048]{1,0:T(8,128)(2,1)S(1)}, u32[]{:S(2)}, u32[]{:S(2)}) %collective-permute-start.29) | collective-permute-done | bytes 393248 | tf_op jit(solution)/shard_map/ppermute | solution.py:23
  109.0 6.5 %shard_map.132 = (bf16[384,512]{1,0:T(8,128)(2,1)S(1)}, bf16[384,512]{1,0:T(8,128)(2,1)S(1)}, bf16[384,512]{1,0:T(8,128)(2,1)S(1)}) custom-call(s32[5]{0:T(128)S(1)} %copy-done.10, bf16[96,2048]{1,0:T(8,128)(2,1)S(1)} %fusion.3.refs_0_, bf16[96,2048]{1,0:T(8,128)(2,1)S(1)} %collective-permute-done.24.refs_1_, ...), custom_call_target="tpu_custom_call" | custom-call | tf_op jit(solution)/shard_map/pallas_call | solution.py:301
  115.6 7.5 %collective-permute-done.35.refs_4_ = bf16[512,512]{1,0:T(8,128)(2,1)S(1)} collective-permute-done((bf16[512,512]{1,0:T(8,128)(2,1)S(1)}, bf16[512,512]{1,0:T(8,128)(2,1)S(1)}, u32[]{:S(2)}, u32[]{:S(2)}) %collective-permute-start.35) | collective-permute-done | bytes 524320 | tf_op jit(solution)/shard_map/ppermute | solution.py:23
  126.8 2.9 %shard_map.133.refs_0_ = bf16[384,512]{1,0:T(8,128)(2,1)S(1)} custom-call(s32[5]{0:T(128)S(1)} %copy-done.10, bf16[96,2048]{1,0:T(8,128)(2,1)S(1)} %collective-permute-done.23.refs_0_, bf16[96,2048]{1,0:T(8,128)(2,1)S(1)} %collective-permute-done.31.refs_1_, bf16[96,2048]{1,0:T(8,128)(2,1)S(1)} %collective-permute-done.32.refs_2_, ...), custom_call_target="tpu_custom_call" | custom-call | tf_op jit(solution)/shard_map/pallas_call | solution.py:301
  129.7 6.2 %collective-permute-done.36.refs_5_ = bf16[512,512]{1,0:T(8,128)(2,1)S(1)} collective-permute-done((bf16[512,512]{1,0:T(8,128)(2,1)S(1)}, bf16[512,512]{1,0:T(8,128)(2,1)S(1)}, u32[]{:S(2)}, u32[]{:S(2)}) %collective-permute-start.36) | collective-permute-done | bytes 524320 | tf_op jit(solution)/shard_map/ppermute | solution.py:23
  135.9 2.6 %shard_map.134 = (f32[96,2048]{1,0:T(8,128)S(1)}, f32[96,2048]{1,0:T(8,128)S(1)}, bf16[96,2048]{1,0:T(8,128)(2,1)S(1)}, bf16[96,2048]{1,0:T(8,128)(2,1)S(1)}, f3...) custom-call(s32[5]{0:T(128)S(1)} %copy-done.10, ...), custom_call_target="tpu_custom_call" | custom-call | tf_op jit(solution)/shard_map/pallas_call | solution.py:336
  144.2 2.8 %shard_map.135 = (f32[96,2048]{1,0:T(8,128)S(1)}, f32[96,2048]{1,0:T(8,128)S(1)}, bf16[96,2048]{1,0:T(8,128)(2,1)S(1)}, bf16[96,2048]{1,0:T(8,128)(2,1)S(1)}, f3...) custom-call(s32[5]{0:T(128)S(1)} %copy-done.10, ...), custom_call_target="tpu_custom_call" | custom-call | flops 99999997952 | tf_op jit(solution)/shard_map/pallas_call | solution.py:336
  148.5 6.2 %collective-permute-done.38 = bf16[96,1280]{1,0:T(8,128)(2,1)S(1)} collective-permute-done((bf16[96,1280]{1,0:T(8,128)(2,1)S(1)}, bf16[96,1280]{1,0:T(8,128)(2,1)S(1)}, u32[]{:S(2)}, u32[]{:S(2)}) %collective-permute-start.38) | collective-permute-done | bytes 245792 | tf_op jit(solution)/shard_map/ppermute | solution.py:23
  161.2 2.3 %collective-permute-done.49 = bf16[96,1280]{1,0:T(8,128)(2,1)S(1)} collective-permute-done((bf16[96,1280]{1,0:T(8,128)(2,1)S(1)}, bf16[96,1280]{1,0:T(8,128)(2,1)S(1)}, u32[]{:S(2)}, u32[]{:S(2)}) %collective-permute-start.49) | collective-permute-done | bytes 245792 | tf_op jit(solution)/shard_map/ppermute | solution.py:23
  164.6 2.9 %collective-permute-start.55 = (bf16[96,1280]{1,0:T(8,128)(2,1)S(1)}, bf16[96,1280]{1,0:T(8,128)(2,1)S(1)}, u32[]{:S(2)}, u32[]{:S(2)}) collective-permute-start(bf16[96,1280]{1,0:T(8,128)(2,1)S(1)} %add_convert_fusion.4), channel_id=1, source_target_pairs={{0,8},{4,12},{8,0},{12,4},{1,9},{5,13},{9,1},{13,5},{2,10},{6,14},... | collective-permute-start | bytes 737288 | tf_op jit(solution)/shard_map/ppermute | solution.py:23
  168.0 3.7 %collective-permute-done.47 = bf16[96,2048]{1,0:T(8,128)(2,1)S(1)} collective-permute-done((bf16[96,2048]{1,0:T(8,128)(2,1)S(1)}, bf16[96,2048]{1,0:T(8,128)(2,1)S(1)}, u32[]{:S(2)}, u32[]{:S(2)}) %collective-permute-start.47) | collective-permute-done | bytes 393248 | tf_op jit(solution)/shard_map/ppermute | solution.py:23
  175.6 3.0 %collective-permute-done.55 = bf16[96,1280]{1,0:T(8,128)(2,1)S(1)} collective-permute-done((bf16[96,1280]{1,0:T(8,128)(2,1)S(1)}, bf16[96,1280]{1,0:T(8,128)(2,1)S(1)}, u32[]{:S(2)}, u32[]{:S(2)}) %collective-permute-start.55) | collective-permute-done | bytes 245792 | tf_op jit(solution)/shard_map/ppermute | solution.py:23
  178.7 2.8 %collective-permute-done.53 = bf16[96,1024]{1,0:T(8,128)(2,1)S(1)} collective-permute-done((bf16[96,1024]{1,0:T(8,128)(2,1)S(1)}, bf16[96,1024]{1,0:T(8,128)(2,1)S(1)}, u32[]{:S(2)}, u32[]{:S(2)}) %collective-permute-start.53) | collective-permute-done | bytes 196640 | tf_op jit(solution)/shard_map/ppermute | solution.py:23
  181.4 2.6 %collective-permute-done.54 = bf16[96,1024]{1,0:T(8,128)(2,1)S(1)} collective-permute-done((bf16[96,1024]{1,0:T(8,128)(2,1)S(1)}, bf16[96,1024]{1,0:T(8,128)(2,1)S(1)}, u32[]{:S(2)}, u32[]{:S(2)}) %collective-permute-start.54) | collective-permute-done | bytes 196640 | tf_op jit(solution)/shard_map/ppermute | solution.py:23
  (149 shorter events, 70.2 us)
Async XLA Ops:
  6.7 51.0 %collective-permute-start.14 = (bf16[1024,512]{1,0:T(8,128)(2,1)}, bf16[1024,512]{1,0:T(8,128)(2,1)S(1)}, u32[]{:S(2)}, u32[]{:S(2)}) collective-permute-start(bf16[1024,512]{1,0:T(8,128)(2,1)} %get-tuple-element.132), channel_id=1, source_target_pairs={{0,8},{4,12},{8,0},{12,4},{1,9},{5,13},{9,1},{13,5},{2,10},{6,14},... | collective-permute-start | bytes 3145736 | tf_op jit(solution)/shard_map/ppermute | solution.py:23
  10.4 47.3 %collective-permute-start.13 = (bf16[1024,512]{1,0:T(8,128)(2,1)}, bf16[1024,512]{1,0:T(8,128)(2,1)S(1)}, u32[]{:S(2)}, u32[]{:S(2)}) collective-permute-start(bf16[1024,512]{1,0:T(8,128)(2,1)} %get-tuple-element.131), channel_id=1, source_target_pairs={{0,4},{4,0},{8,12},{12,8},{1,5},{5,1},{9,13},{13,9},{2,6},{6,2},{1... | collective-permute-start | bytes 3145736 | tf_op jit(solution)/shard_map/ppermute | solution.py:23
  35.0 17.9 %collective-permute-start.6 = (bf16[128,1024]{1,0:T(8,128)(2,1)S(1)}, bf16[128,1024]{1,0:T(8,128)(2,1)S(1)}, u32[]{:S(2)}, u32[]{:S(2)}) collective-permute-start(bf16[128,1024]{1,0:T(8,128)(2,1)S(1)} %collective-permute-done.5.refs_2_), channel_id=1, source_target_pairs={{0,16},{16,0},{1,17},{17,1},{2,18},{18,2},{3,19},{19,3},{4,20},{20... | collective-permute-start | bytes 786440 | tf_op jit(solution)/shard_map/ppermute | solution.py:23
  40.9 12.0 %collective-permute-start.8 = (bf16[128,1024]{1,0:T(8,128)(2,1)S(1)}, bf16[128,1024]{1,0:T(8,128)(2,1)S(1)}, u32[]{:S(2)}, u32[]{:S(2)}) collective-permute-start(bf16[128,1024]{1,0:T(8,128)(2,1)S(1)} %collective-permute-done.7.refs_3_), channel_id=1, source_target_pairs={{0,16},{16,0},{1,17},{17,1},{2,18},{18,2},{3,19},{19,3},{4,20},{20... | collective-permute-start | bytes 786440 | tf_op jit(solution)/shard_map/ppermute | solution.py:23
  59.7 11.5 %collective-permute-start.17 = (bf16[96,2048]{1,0:T(8,128)(2,1)S(1)}, bf16[96,2048]{1,0:T(8,128)(2,1)S(1)}, u32[]{:S(2)}, u32[]{:S(2)}) collective-permute-start(bf16[96,2048]{1,0:T(8,128)(2,1)S(1)} %add_convert_fusion.3), channel_id=1, source_target_pairs={{0,2},{1,3},{2,0},{3,1},{4,6},{5,7},{6,4},{7,5},{8,10},{9,11},{10,... | collective-permute-start | bytes 1179656 | tf_op jit(solution)/shard_map/ppermute | solution.py:23
  61.0 33.6 %collective-permute-start.19 = (bf16[1024,512]{1,0:T(8,128)(2,1)S(1)}, bf16[1024,512]{1,0:T(8,128)(2,1)S(1)}, u32[]{:S(2)}, u32[]{:S(2)}) collective-permute-start(bf16[1024,512]{1,0:T(8,128)(2,1)S(1)} %collective-permute-done.14.refs_15_.refs_7_), channel_id=1, source_target_pairs={{0,4},{4,0},{8,12},{12,8},{1,5},{5,1},{9,13},{13,9},{2,6},{6,2},{1... | collective-permute-start | bytes 3145736 | tf_op jit(solution)/shard_map/ppermute | solution.py:23
  72.7 22.0 %collective-permute-start.18 = (bf16[96,2048]{1,0:T(8,128)(2,1)S(1)}, bf16[96,2048]{1,0:T(8,128)(2,1)S(1)}, u32[]{:S(2)}, u32[]{:S(2)}) collective-permute-start(bf16[96,2048]{1,0:T(8,128)(2,1)S(1)} %fusion.3.refs_0_), channel_id=1, source_target_pairs={{0,8},{4,12},{8,0},{12,4},{1,9},{5,13},{9,1},{13,5},{2,10},{6,14},... | collective-permute-start | bytes 1179656 | tf_op jit(solution)/shard_map/ppermute | solution.py:23
  74.6 20.0 %collective-permute-start.20 = (bf16[96,2048]{1,0:T(8,128)(2,1)S(1)}, bf16[96,2048]{1,0:T(8,128)(2,1)S(1)}, u32[]{:S(2)}, u32[]{:S(2)}) collective-permute-start(bf16[96,2048]{1,0:T(8,128)(2,1)S(1)} %fusion.3.refs_0_), channel_id=1, source_target_pairs={{0,2},{1,3},{2,0},{3,1},{4,6},{5,7},{6,4},{7,5},{8,10},{9,11},{10,... | collective-permute-start | bytes 1179656 | tf_op jit(solution)/shard_map/ppermute | solution.py:23
  82.7 11.9 %collective-permute-start.22 = (bf16[96,2048]{1,0:T(8,128)(2,1)S(1)}, bf16[96,2048]{1,0:T(8,128)(2,1)S(1)}, u32[]{:S(2)}, u32[]{:S(2)}) collective-permute-start(bf16[96,2048]{1,0:T(8,128)(2,1)S(1)} %collective-permute-done.21.refs_4_), channel_id=1, source_target_pairs={{0,2},{1,3},{2,0},{3,1},{4,6},{5,7},{6,4},{7,5},{8,10},{9,11},{10,... | collective-permute-start | bytes 1179656 | tf_op jit(solution)/shard_map/ppermute | solution.py:23
  95.3 11.5 %collective-permute-start.29 = (bf16[96,2048]{1,0:T(8,128)(2,1)S(1)}, bf16[96,2048]{1,0:T(8,128)(2,1)S(1)}, u32[]{:S(2)}, u32[]{:S(2)}) collective-permute-start(bf16[96,2048]{1,0:T(8,128)(2,1)S(1)} %collective-permute-done.18.refs_8_), channel_id=1, source_target_pairs={{0,2},{1,3},{2,0},{3,1},{4,6},{5,7},{6,4},{7,5},{8,10},{9,11},{10,... | collective-permute-start | bytes 1179656 | tf_op jit(solution)/shard_map/ppermute | solution.py:23
  96.1 10.7 %collective-permute-start.25 = (bf16[96,2048]{1,0:T(8,128)(2,1)S(1)}, bf16[96,2048]{1,0:T(8,128)(2,1)S(1)}, u32[]{:S(2)}, u32[]{:S(2)}) collective-permute-start(bf16[96,2048]{1,0:T(8,128)(2,1)S(1)} %collective-permute-done.20.refs_2_), channel_id=1, source_target_pairs={{0,1},{1,0},{2,3},{3,2},{4,5},{5,4},{6,7},{7,6},{8,9},{9,8},{10,11... | collective-permute-start | bytes 1179656 | tf_op jit(solution)/shard_map/ppermute | solution.py:23
  96.4 11.2 %collective-permute-start.23 = (bf16[96,2048]{1,0:T(8,128)(2,1)S(1)}, bf16[96,2048]{1,0:T(8,128)(2,1)S(1)}, u32[]{:S(2)}, u32[]{:S(2)}) collective-permute-start(bf16[96,2048]{1,0:T(8,128)(2,1)S(1)} %collective-permute-done.18.refs_8_), channel_id=1, source_target_pairs={{0,16},{16,0},{1,17},{17,1},{2,18},{18,2},{3,19},{19,3},{4,20},{20... | collective-permute-start | bytes 1179656 | tf_op jit(solution)/shard_map/ppermute | solution.py:23
  97.3 25.8 %collective-permute-start.35 = (bf16[512,512]{1,0:T(8,128)(2,1)S(1)}, bf16[512,512]{1,0:T(8,128)(2,1)S(1)}, u32[]{:S(2)}, u32[]{:S(2)}) collective-permute-start(bf16[512,512]{1,0:T(8,128)(2,1)S(1)} %get-tuple-element.158), channel_id=1, source_target_pairs={{0,8},{4,12},{8,0},{12,4},{1,9},{5,13},{9,1},{13,5},{2,10},{6,14},... | collective-permute-start | bytes 1572872 | tf_op jit(solution)/shard_map/ppermute | solution.py:23
  99.5 23.6 %collective-permute-start.34 = (bf16[512,512]{1,0:T(8,128)(2,1)S(1)}, bf16[512,512]{1,0:T(8,128)(2,1)S(1)}, u32[]{:S(2)}, u32[]{:S(2)}) collective-permute-start(bf16[512,512]{1,0:T(8,128)(2,1)S(1)} %get-tuple-element.156), channel_id=1, source_target_pairs={{0,4},{4,0},{8,12},{12,8},{1,5},{5,1},{9,13},{13,9},{2,6},{6,2},{1... | collective-permute-start | bytes 1572872 | tf_op jit(solution)/shard_map/ppermute | solution.py:23
  107.6 16.9 %collective-permute-start.32 = (bf16[96,2048]{1,0:T(8,128)(2,1)S(1)}, bf16[96,2048]{1,0:T(8,128)(2,1)S(1)}, u32[]{:S(2)}, u32[]{:S(2)}) collective-permute-start(bf16[96,2048]{1,0:T(8,128)(2,1)S(1)} %collective-permute-done.23.refs_0_), channel_id=1, source_target_pairs={{0,2},{1,3},{2,0},{3,1},{4,6},{5,7},{6,4},{7,5},{8,10},{9,11},{10,... | collective-permute-start | bytes 1179656 | tf_op jit(solution)/shard_map/ppermute | solution.py:23
  123.1 12.8 %collective-permute-start.36 = (bf16[512,512]{1,0:T(8,128)(2,1)S(1)}, bf16[512,512]{1,0:T(8,128)(2,1)S(1)}, u32[]{:S(2)}, u32[]{:S(2)}) collective-permute-start(bf16[512,512]{1,0:T(8,128)(2,1)S(1)} %collective-permute-done.35.refs_4_), channel_id=1, source_target_pairs={{0,4},{4,0},{8,12},{12,8},{1,5},{5,1},{9,13},{13,9},{2,6},{6,2},{1... | collective-permute-start | bytes 1572872 | tf_op jit(solution)/shard_map/ppermute | solution.py:23
  139.2 17.3 %collective-permute-start.48 = (bf16[96,2048]{1,0:T(8,128)(2,1)S(1)}, bf16[96,2048]{1,0:T(8,128)(2,1)S(1)}, u32[]{:S(2)}, u32[]{:S(2)}) collective-permute-start(bf16[96,2048]{1,0:T(8,128)(2,1)S(1)} %get-tuple-element.201), channel_id=1, source_target_pairs={{0,1},{1,0},{2,3},{3,2},{4,5},{5,4},{6,7},{7,6},{8,9},{9,8},{10,11... | collective-permute-start | bytes 1179656 | tf_op jit(solution)/shard_map/ppermute | solution.py:23
  142.0 15.7 %collective-permute-start.51 = (bf16[96,768]{1,0:T(8,128)(2,1)S(1)}, bf16[96,768]{1,0:T(8,128)(2,1)S(1)}, u32[]{:S(2)}, u32[]{:S(2)}) collective-permute-start(bf16[96,768]{1,0:T(8,128)(2,1)S(1)} %add_convert_fusion.10), channel_id=1, source_target_pairs={{0,2},{1,3},{2,0},{3,1},{4,6},{5,7},{6,4},{7,5},{8,10},{9,11},{10,... | collective-permute-start | bytes 442376 | tf_op jit(solution)/shard_map/ppermute | solution.py:23
  142.6 12.1 %collective-permute-start.38 = (bf16[96,1280]{1,0:T(8,128)(2,1)S(1)}, bf16[96,1280]{1,0:T(8,128)(2,1)S(1)}, u32[]{:S(2)}, u32[]{:S(2)}) collective-permute-start(bf16[96,1280]{1,0:T(8,128)(2,1)S(1)} %add_convert_fusion.7), channel_id=1, source_target_pairs={{0,2},{1,3},{2,0},{3,1},{4,6},{5,7},{6,4},{7,5},{8,10},{9,11},{10,... | collective-permute-start | bytes 737288 | tf_op jit(solution)/shard_map/ppermute | solution.py:23
  157.8 17.0 %collective-permute-start.56 = (bf16[96,768]{1,0:T(8,128)(2,1)S(1)}, bf16[96,768]{1,0:T(8,128)(2,1)S(1)}, u32[]{:S(2)}, u32[]{:S(2)}) collective-permute-start(bf16[96,768]{1,0:T(8,128)(2,1)S(1)} %add_convert_fusion.8), channel_id=1, source_target_pairs={{0,8},{4,12},{8,0},{12,4},{1,9},{5,13},{9,1},{13,5},{2,10},{6,14},... | collective-permute-start | bytes 442376 | tf_op jit(solution)/shard_map/ppermute | solution.py:23
  160.1 11.6 %collective-permute-start.47 = (bf16[96,2048]{1,0:T(8,128)(2,1)S(1)}, bf16[96,2048]{1,0:T(8,128)(2,1)S(1)}, u32[]{:S(2)}, u32[]{:S(2)}) collective-permute-start(bf16[96,2048]{1,0:T(8,128)(2,1)S(1)} %add_convert_fusion.1), channel_id=1, source_target_pairs={{0,2},{1,3},{2,0},{3,1},{4,6},{5,7},{6,4},{7,5},{8,10},{9,11},{10,... | collective-permute-start | bytes 1179656 | tf_op jit(solution)/shard_map/ppermute | solution.py:23
  164.6 14.1 %collective-permute-start.55 = (bf16[96,1280]{1,0:T(8,128)(2,1)S(1)}, bf16[96,1280]{1,0:T(8,128)(2,1)S(1)}, u32[]{:S(2)}, u32[]{:S(2)}) collective-permute-start(bf16[96,1280]{1,0:T(8,128)(2,1)S(1)} %add_convert_fusion.4), channel_id=1, source_target_pairs={{0,8},{4,12},{8,0},{12,4},{1,9},{5,13},{9,1},{13,5},{2,10},{6,14},... | collective-permute-start | bytes 737288 | tf_op jit(solution)/shard_map/ppermute | solution.py:23
  167.5 11.1 %collective-permute-start.43 = (bf16[96,2048]{1,0:T(8,128)(2,1)S(1)}, bf16[96,2048]{1,0:T(8,128)(2,1)S(1)}, u32[]{:S(2)}, u32[]{:S(2)}) collective-permute-start(bf16[96,2048]{1,0:T(8,128)(2,1)S(1)} %get-tuple-element.195), channel_id=1, source_target_pairs={{0,1},{1,0},{2,3},{3,2},{4,5},{5,4},{6,7},{7,6},{8,9},{9,8},{10,11... | collective-permute-start | bytes 1179656 | tf_op jit(solution)/shard_map/ppermute | solution.py:23
  171.9 12.1 %collective-permute-start.45 = (bf16[96,2048]{1,0:T(8,128)(2,1)S(1)}, bf16[96,2048]{1,0:T(8,128)(2,1)S(1)}, u32[]{:S(2)}, u32[]{:S(2)}) collective-permute-start(bf16[96,2048]{1,0:T(8,128)(2,1)S(1)} %add_convert_fusion), channel_id=1, source_target_pairs={{0,2},{1,3},{2,0},{3,1},{4,6},{5,7},{6,4},{7,5},{8,10},{9,11},{10,... | collective-permute-start | bytes 1179656 | tf_op jit(solution)/shard_map/ppermute | solution.py:23
  (48 other events, 537.8 us)

commit v7 on v6

--- a/solution.py
+++ b/solution.py
@@ -509,7 +509,7 @@
     parts = gather_rows(normed_own, over_chip[0]) + gather_rows(rows_x, over_chip[1])
     rows_both = swap(rows_z, "rep", 1)
     rows_z = gather_rows(rows_z)
-    back = {**across(after(down_cut[0], rows_z[0])), **near_side(after(down_cut[1], rows_z[1]))}
+    back = {**across(after(down_cut[0], rows_x)), **near_side(after(down_cut[1], rows_z[1]))}
     parts += rows_z
     masks = [0] + list(wide)
     in_order = lambda held: [held[mask] for mask in masks[1:]]
@@ -531,7 +531,7 @@
     kept, came, sent = reduce_rows(*found_both, edges)
     kept_z, came_z, sent_z = reduce_rows(*found_z, edges)
     found_x, found = sums_of(after(acts[1], *sent, *sent_z), acts[0], gate=True)
-    came[0], found_x, found = join(came[0], found_x, found)
+    came[0], came_z[0], found_x, found = join(came[0], came_z[0], found_x, found)
     of_both = [total(*terms).astype(jnp.bfloat16) for terms in zip(kept, came)]
     of_z = [total(*terms) for terms in zip(kept_z, came_z)]
     sent = [

time: 185 us -> 185 us (level)
  transfers between devices with their start and end apart: 57 -> 57, of which waited for: 26 -> 27; matrix products, arithmetic and copies ran while one was open for 1% -> 1% of each run, Pallas kernels for 13% -> 13%
where the time goes in v7:
time: 185 us
  waiting for transfers between devices  89.3 us (48%)
  starting transfers between devices  55.4 us (30%)
  Pallas kernels  30.8 us (17%)
  local copies, waits for them, and re-layouts  5.77 us (3%)
  other arithmetic  2.74 us (1%)
    ppermute x57, waiting for transfers between devices, swap(): return lax.ppermute(value, axis, pairs)  89.3 us
    ppermute x57, starting transfers between devices, swap(): return lax.ppermute(value, axis, pairs)  55.4 us
    pallas_call x2, Pallas kernels, gate_up(): pl.pallas_call(body, in_specs=[smem()] + [vmem()] * blocks + [anywhere()]...  9.43 us
    pallas_call x2, Pallas kernels, down_rows(): pl.pallas_call(body, in_specs=[smem()] + [vmem()] * groups + [anywhere()]...  5.46 us
    unnamed x30, local copies, waits for them, and re-layouts  5.08 us
    pallas_call x1, Pallas kernels, prepare(): pl.pallas_call(body, in_specs=[smem(), vmem(), vmem()] + [anywhere()] * s...  4.87 us
    pallas_call x1, Pallas kernels, attend(): pl.pallas_call(attend_body, in_specs=[smem()] + [vmem()] * 3 + [anywhere(...  4.75 us
  transfers between devices with their start and end apart: 57, of which 27 were waited for; matrix products, arithmetic and copies ran while one was open for 1% of the time, Pallas kernels for 13%

profile of v7, /device:TPU:0, one launch (start us, length us, event | category | flops | bytes accessed | tf_op | source)
XLA Modules:
  0.0 185.0 jit_solution(12643067495584664377)
XLA Ops:
  1.3 4.9 %shard_map.127 = (bf16[96,1024]{1,0:T(8,128)(2,1)}, bf16[96,1024]{1,0:T(8,128)(2,1)}, bf16[128,1024]{1,0:T(8,128)(2,1)}, bf16[128,1024]{1,0:T(8,128)(2,1)}, bf16...) custom-call(s32[5]{0:T(128)} %stack.23.info_ref.info, ...), custom_call_target="tpu_custom_call" | custom-call | tf_op jit(solution)/shard_map/pallas_call | solution.py:71
  6.7 3.7 %collective-permute-start.14 = (bf16[1024,512]{1,0:T(8,128)(2,1)}, bf16[1024,512]{1,0:T(8,128)(2,1)S(1)}, u32[]{:S(2)}, u32[]{:S(2)}) collective-permute-start(bf16[1024,512]{1,0:T(8,128)(2,1)} %get-tuple-element.133), channel_id=1, source_target_pairs={{0,8},{4,12},{8,0},{12,4},{1,9},{5,13},{9,1},{13,5},{2,10},{6,14},... | collective-permute-start | bytes 3145736 | tf_op jit(solution)/shard_map/ppermute | solution.py:23
  14.0 6.0 %collective-permute-done.refs_4_ = bf16[96,1024]{1,0:T(8,128)(2,1)S(1)} collective-permute-done((bf16[96,1024]{1,0:T(8,128)(2,1)}, bf16[96,1024]{1,0:T(8,128)(2,1)S(1)}, u32[]{:S(2)}, u32[]{:S(2)}) %collective-permute-start) | collective-permute-done | bytes 196640 | tf_op jit(solution)/shard_map/ppermute | solution.py:23
  24.6 3.8 %collective-permute-done.2.refs_4_ = bf16[128,1024]{1,0:T(8,128)(2,1)S(1)} collective-permute-done((bf16[128,1024]{1,0:T(8,128)(2,1)}, bf16[128,1024]{1,0:T(8,128)(2,1)S(1)}, u32[]{:S(2)}, u32[]{:S(2)}) %collective-permute-start.2) | collective-permute-done | bytes 262176 | tf_op jit(solution)/shard_map/ppermute | solution.py:23
  36.5 4.4 %collective-permute-done.7.refs_3_ = bf16[128,1024]{1,0:T(8,128)(2,1)S(1)} collective-permute-done((bf16[128,1024]{1,0:T(8,128)(2,1)}, bf16[128,1024]{1,0:T(8,128)(2,1)S(1)}, u32[]{:S(2)}, u32[]{:S(2)}) %collective-permute-start.7) | collective-permute-done | bytes 262176 | tf_op jit(solution)/shard_map/ppermute | solution.py:23
  49.3 3.6 %shard_map.129 = (bf16[384,512]{1,0:T(8,128)(2,1)S(1)}, bf16[384,512]{1,0:T(8,128)(2,1)S(1)}, bf16[384,512]{1,0:T(8,128)(2,1)S(1)}) custom-call(bf16[96,1024]{1,0:T(8,128)(2,1)S(1)} %copy-done.8, bf16[96,1024]{1,0:T(8,128)(2,1)S(1)} %copy-done.9, bf16[96,1024]{1,0:T(8,128)(2,1)S(1)} %collective-permute-done.9.refs_2_, ...), custom_call_target="tpu_custom_call" | custom-call | tf_op jit(solution)/shard_map/pallas_call | solution.py:151
  53.0 4.7 %shard_map.130 = (f32[96,2048]{1,0:T(8,128)S(1)}, f32[96,2048]{1,0:T(8,128)S(1)}, bf16[96,2048]{1,0:T(8,128)(2,1)S(1)}, bf16[96,2048]{1,0:T(8,128)(2,1)S(1)}) custom-call(s32[1]{0:T(128)S(6)} %copy.14.traded, bf16[384,512]{1,0:T(8,128)(2,1)S(1)} %get-tuple-element.118.q, bf16[384,512]{1,0:T(8,128)(2,1)S(1)} %get-tuple-element.119.k, ...), custom_call_target="tpu_custom_call" | custom-call | tf_op jit(solution)/shard_map/pallas_call | solution.py:247
  63.0 8.2 %collective-permute-done.17 = bf16[96,2048]{1,0:T(8,128)(2,1)S(1)} collective-permute-done((bf16[96,2048]{1,0:T(8,128)(2,1)S(1)}, bf16[96,2048]{1,0:T(8,128)(2,1)S(1)}, u32[]{:S(2)}, u32[]{:S(2)}) %collective-permute-start.17) | collective-permute-done | bytes 393248 | tf_op jit(solution)/shard_map/ppermute | solution.py:23
  76.1 6.6 %collective-permute-done.21.refs_4_ = bf16[96,2048]{1,0:T(8,128)(2,1)S(1)} collective-permute-done((bf16[96,2048]{1,0:T(8,128)(2,1)S(1)}, bf16[96,2048]{1,0:T(8,128)(2,1)S(1)}, u32[]{:S(2)}, u32[]{:S(2)}) %collective-permute-start.21) | collective-permute-done | bytes 393248 | tf_op jit(solution)/shard_map/ppermute | solution.py:23
  83.9 10.7 %collective-permute-done.19.refs_16_.refs_8_ = bf16[1024,512]{1,0:T(8,128)(2,1)S(1)} collective-permute-done((bf16[1024,512]{1,0:T(8,128)(2,1)S(1)}, bf16[1024,512]{1,0:T(8,128)(2,1)S(1)}, u32[]{:S(2)}, u32[]{:S(2)}) %collective-permute-start.19) | collective-permute-done | bytes 1048608 | tf_op jit(solution)/shard_map/ppermute | solution.py:23
  97.3 2.3 %collective-permute-start.35 = (bf16[512,512]{1,0:T(8,128)(2,1)S(1)}, bf16[512,512]{1,0:T(8,128)(2,1)S(1)}, u32[]{:S(2)}, u32[]{:S(2)}) collective-permute-start(bf16[512,512]{1,0:T(8,128)(2,1)S(1)} %get-tuple-element.159), channel_id=1, source_target_pairs={{0,8},{4,12},{8,0},{12,4},{1,9},{5,13},{9,1},{13,5},{2,10},{6,14},... | collective-permute-start | bytes 1572872 | tf_op jit(solution)/shard_map/ppermute | solution.py:23
  101.5 5.2 %collective-permute-done.29.refs_10_ = bf16[96,2048]{1,0:T(8,128)(2,1)S(1)} collective-permute-done((bf16[96,2048]{1,0:T(8,128)(2,1)S(1)}, bf16[96,2048]{1,0:T(8,128)(2,1)S(1)}, u32[]{:S(2)}, u32[]{:S(2)}) %collective-permute-start.29) | collective-permute-done | bytes 393248 | tf_op jit(solution)/shard_map/ppermute | solution.py:23
  109.0 6.5 %shard_map.132 = (bf16[384,512]{1,0:T(8,128)(2,1)S(1)}, bf16[384,512]{1,0:T(8,128)(2,1)S(1)}, bf16[384,512]{1,0:T(8,128)(2,1)S(1)}) custom-call(s32[5]{0:T(128)S(1)} %copy-done.10, bf16[96,2048]{1,0:T(8,128)(2,1)S(1)} %fusion.3.refs_0_, bf16[96,2048]{1,0:T(8,128)(2,1)S(1)} %collective-permute-done.24.refs_1_, ...), custom_call_target="tpu_custom_call" | custom-call | tf_op jit(solution)/shard_map/pallas_call | solution.py:301
  115.6 7.5 %collective-permute-done.35.refs_4_ = bf16[512,512]{1,0:T(8,128)(2,1)S(1)} collective-permute-done((bf16[512,512]{1,0:T(8,128)(2,1)S(1)}, bf16[512,512]{1,0:T(8,128)(2,1)S(1)}, u32[]{:S(2)}, u32[]{:S(2)}) %collective-permute-start.35) | collective-permute-done | bytes 524320 | tf_op jit(solution)/shard_map/ppermute | solution.py:23
  126.8 2.9 %shard_map.133.refs_0_ = bf16[384,512]{1,0:T(8,128)(2,1)S(1)} custom-call(s32[5]{0:T(128)S(1)} %copy-done.10, bf16[96,2048]{1,0:T(8,128)(2,1)S(1)} %collective-permute-done.23.refs_0_, bf16[96,2048]{1,0:T(8,128)(2,1)S(1)} %collective-permute-done.31.refs_1_, bf16[96,2048]{1,0:T(8,128)(2,1)S(1)} %collective-permute-done.32.refs_2_, ...), custom_call_target="tpu_custom_call" | custom-call | tf_op jit(solution)/shard_map/pallas_call | solution.py:301
  129.7 6.2 %collective-permute-done.36.refs_5_ = bf16[512,512]{1,0:T(8,128)(2,1)S(1)} collective-permute-done((bf16[512,512]{1,0:T(8,128)(2,1)S(1)}, bf16[512,512]{1,0:T(8,128)(2,1)S(1)}, u32[]{:S(2)}, u32[]{:S(2)}) %collective-permute-start.36) | collective-permute-done | bytes 524320 | tf_op jit(solution)/shard_map/ppermute | solution.py:23
  135.9 2.6 %shard_map.134 = (f32[96,2048]{1,0:T(8,128)S(1)}, f32[96,2048]{1,0:T(8,128)S(1)}, bf16[96,2048]{1,0:T(8,128)(2,1)S(1)}, bf16[96,2048]{1,0:T(8,128)(2,1)S(1)}, f3...) custom-call(s32[5]{0:T(128)S(1)} %copy-done.10, ...), custom_call_target="tpu_custom_call" | custom-call | tf_op jit(solution)/shard_map/pallas_call | solution.py:336
  144.2 2.8 %shard_map.135 = (f32[96,2048]{1,0:T(8,128)S(1)}, f32[96,2048]{1,0:T(8,128)S(1)}, bf16[96,2048]{1,0:T(8,128)(2,1)S(1)}, bf16[96,2048]{1,0:T(8,128)(2,1)S(1)}, f3...) custom-call(s32[5]{0:T(128)S(1)} %copy-done.10, ...), custom_call_target="tpu_custom_call" | custom-call | flops 99999997952 | tf_op jit(solution)/shard_map/pallas_call | solution.py:336
  149.1 3.3 %collective-permute-done.40 = bf16[96,1280]{1,0:T(8,128)(2,1)S(1)} collective-permute-done((bf16[96,1280]{1,0:T(8,128)(2,1)S(1)}, bf16[96,1280]{1,0:T(8,128)(2,1)S(1)}, u32[]{:S(2)}, u32[]{:S(2)}) %collective-permute-start.40) | collective-permute-done | bytes 245792 | tf_op jit(solution)/shard_map/ppermute | solution.py:23
  152.4 5.3 %collective-permute-done.38 = bf16[96,1280]{1,0:T(8,128)(2,1)S(1)} collective-permute-done((bf16[96,1280]{1,0:T(8,128)(2,1)S(1)}, bf16[96,1280]{1,0:T(8,128)(2,1)S(1)}, u32[]{:S(2)}, u32[]{:S(2)}) %collective-permute-start.38) | collective-permute-done | bytes 245792 | tf_op jit(solution)/shard_map/ppermute | solution.py:23
  160.1 3.1 %collective-permute-start.56 = (bf16[96,768]{1,0:T(8,128)(2,1)S(1)}, bf16[96,768]{1,0:T(8,128)(2,1)S(1)}, u32[]{:S(2)}, u32[]{:S(2)}) collective-permute-start(bf16[96,768]{1,0:T(8,128)(2,1)S(1)} %add_convert_fusion.8), channel_id=1, source_target_pairs={{0,8},{4,12},{8,0},{12,4},{1,9},{5,13},{9,1},{13,5},{2,10},{6,14},... | collective-permute-start | bytes 442376 | tf_op jit(solution)/shard_map/ppermute | solution.py:23
  166.3 3.1 %collective-permute-start.55 = (bf16[96,1280]{1,0:T(8,128)(2,1)S(1)}, bf16[96,1280]{1,0:T(8,128)(2,1)S(1)}, u32[]{:S(2)}, u32[]{:S(2)}) collective-permute-start(bf16[96,1280]{1,0:T(8,128)(2,1)S(1)} %add_convert_fusion.4), channel_id=1, source_target_pairs={{0,8},{4,12},{8,0},{12,4},{1,9},{5,13},{9,1},{13,5},{2,10},{6,14},... | collective-permute-start | bytes 737288 | tf_op jit(solution)/shard_map/ppermute | solution.py:23
  169.9 3.5 %collective-permute-done.48 = bf16[96,2048]{1,0:T(8,128)(2,1)S(1)} collective-permute-done((bf16[96,2048]{1,0:T(8,128)(2,1)S(1)}, bf16[96,2048]{1,0:T(8,128)(2,1)S(1)}, u32[]{:S(2)}, u32[]{:S(2)}) %collective-permute-start.48) | collective-permute-done | bytes 393248 | tf_op jit(solution)/shard_map/ppermute | solution.py:23
  177.1 3.4 %collective-permute-done.55 = bf16[96,1280]{1,0:T(8,128)(2,1)S(1)} collective-permute-done((bf16[96,1280]{1,0:T(8,128)(2,1)S(1)}, bf16[96,1280]{1,0:T(8,128)(2,1)S(1)}, u32[]{:S(2)}, u32[]{:S(2)}) %collective-permute-start.55) | collective-permute-done | bytes 245792 | tf_op jit(solution)/shard_map/ppermute | solution.py:23
  (149 shorter events, 69.7 us)
Async XLA Ops:
  6.7 51.0 %collective-permute-start.14 = (bf16[1024,512]{1,0:T(8,128)(2,1)}, bf16[1024,512]{1,0:T(8,128)(2,1)S(1)}, u32[]{:S(2)}, u32[]{:S(2)}) collective-permute-start(bf16[1024,512]{1,0:T(8,128)(2,1)} %get-tuple-element.133), channel_id=1, source_target_pairs={{0,8},{4,12},{8,0},{12,4},{1,9},{5,13},{9,1},{13,5},{2,10},{6,14},... | collective-permute-start | bytes 3145736 | tf_op jit(solution)/shard_map/ppermute | solution.py:23
  10.4 47.3 %collective-permute-start.13 = (bf16[1024,512]{1,0:T(8,128)(2,1)}, bf16[1024,512]{1,0:T(8,128)(2,1)S(1)}, u32[]{:S(2)}, u32[]{:S(2)}) collective-permute-start(bf16[1024,512]{1,0:T(8,128)(2,1)} %get-tuple-element.132), channel_id=1, source_target_pairs={{0,4},{4,0},{8,12},{12,8},{1,5},{5,1},{9,13},{13,9},{2,6},{6,2},{1... | collective-permute-start | bytes 3145736 | tf_op jit(solution)/shard_map/ppermute | solution.py:23
  35.0 17.9 %collective-permute-start.6 = (bf16[128,1024]{1,0:T(8,128)(2,1)S(1)}, bf16[128,1024]{1,0:T(8,128)(2,1)S(1)}, u32[]{:S(2)}, u32[]{:S(2)}) collective-permute-start(bf16[128,1024]{1,0:T(8,128)(2,1)S(1)} %collective-permute-done.5.refs_2_), channel_id=1, source_target_pairs={{0,16},{16,0},{1,17},{17,1},{2,18},{18,2},{3,19},{19,3},{4,20},{20... | collective-permute-start | bytes 786440 | tf_op jit(solution)/shard_map/ppermute | solution.py:23
  40.9 12.0 %collective-permute-start.8 = (bf16[128,1024]{1,0:T(8,128)(2,1)S(1)}, bf16[128,1024]{1,0:T(8,128)(2,1)S(1)}, u32[]{:S(2)}, u32[]{:S(2)}) collective-permute-start(bf16[128,1024]{1,0:T(8,128)(2,1)S(1)} %collective-permute-done.7.refs_3_), channel_id=1, source_target_pairs={{0,16},{16,0},{1,17},{17,1},{2,18},{18,2},{3,19},{19,3},{4,20},{20... | collective-permute-start | bytes 786440 | tf_op jit(solution)/shard_map/ppermute | solution.py:23
  59.8 11.5 %collective-permute-start.17 = (bf16[96,2048]{1,0:T(8,128)(2,1)S(1)}, bf16[96,2048]{1,0:T(8,128)(2,1)S(1)}, u32[]{:S(2)}, u32[]{:S(2)}) collective-permute-start(bf16[96,2048]{1,0:T(8,128)(2,1)S(1)} %add_convert_fusion.3), channel_id=1, source_target_pairs={{0,2},{1,3},{2,0},{3,1},{4,6},{5,7},{6,4},{7,5},{8,10},{9,11},{10,... | collective-permute-start | bytes 1179656 | tf_op jit(solution)/shard_map/ppermute | solution.py:23
  61.0 33.6 %collective-permute-start.19 = (bf16[1024,512]{1,0:T(8,128)(2,1)S(1)}, bf16[1024,512]{1,0:T(8,128)(2,1)S(1)}, u32[]{:S(2)}, u32[]{:S(2)}) collective-permute-start(bf16[1024,512]{1,0:T(8,128)(2,1)S(1)} %collective-permute-done.14.refs_15_.refs_7_), channel_id=1, source_target_pairs={{0,4},{4,0},{8,12},{12,8},{1,5},{5,1},{9,13},{13,9},{2,6},{6,2},{1... | collective-permute-start | bytes 3145736 | tf_op jit(solution)/shard_map/ppermute | solution.py:23
  72.1 10.6 %collective-permute-start.21 = (bf16[96,2048]{1,0:T(8,128)(2,1)S(1)}, bf16[96,2048]{1,0:T(8,128)(2,1)S(1)}, u32[]{:S(2)}, u32[]{:S(2)}) collective-permute-start(bf16[96,2048]{1,0:T(8,128)(2,1)S(1)} %fusion.3.refs_0_), channel_id=1, source_target_pairs={{0,16},{16,0},{1,17},{17,1},{2,18},{18,2},{3,19},{19,3},{4,20},{20... | collective-permute-start | bytes 1179656 | tf_op jit(solution)/shard_map/ppermute | solution.py:23
  72.7 22.0 %collective-permute-start.18 = (bf16[96,2048]{1,0:T(8,128)(2,1)S(1)}, bf16[96,2048]{1,0:T(8,128)(2,1)S(1)}, u32[]{:S(2)}, u32[]{:S(2)}) collective-permute-start(bf16[96,2048]{1,0:T(8,128)(2,1)S(1)} %fusion.3.refs_0_), channel_id=1, source_target_pairs={{0,8},{4,12},{8,0},{12,4},{1,9},{5,13},{9,1},{13,5},{2,10},{6,14},... | collective-permute-start | bytes 1179656 | tf_op jit(solution)/shard_map/ppermute | solution.py:23
  74.6 20.0 %collective-permute-start.20 = (bf16[96,2048]{1,0:T(8,128)(2,1)S(1)}, bf16[96,2048]{1,0:T(8,128)(2,1)S(1)}, u32[]{:S(2)}, u32[]{:S(2)}) collective-permute-start(bf16[96,2048]{1,0:T(8,128)(2,1)S(1)} %fusion.3.refs_0_), channel_id=1, source_target_pairs={{0,2},{1,3},{2,0},{3,1},{4,6},{5,7},{6,4},{7,5},{8,10},{9,11},{10,... | collective-permute-start | bytes 1179656 | tf_op jit(solution)/shard_map/ppermute | solution.py:23
  82.7 11.9 %collective-permute-start.22 = (bf16[96,2048]{1,0:T(8,128)(2,1)S(1)}, bf16[96,2048]{1,0:T(8,128)(2,1)S(1)}, u32[]{:S(2)}, u32[]{:S(2)}) collective-permute-start(bf16[96,2048]{1,0:T(8,128)(2,1)S(1)} %collective-permute-done.21.refs_4_), channel_id=1, source_target_pairs={{0,2},{1,3},{2,0},{3,1},{4,6},{5,7},{6,4},{7,5},{8,10},{9,11},{10,... | collective-permute-start | bytes 1179656 | tf_op jit(solution)/shard_map/ppermute | solution.py:23
  95.3 11.5 %collective-permute-start.29 = (bf16[96,2048]{1,0:T(8,128)(2,1)S(1)}, bf16[96,2048]{1,0:T(8,128)(2,1)S(1)}, u32[]{:S(2)}, u32[]{:S(2)}) collective-permute-start(bf16[96,2048]{1,0:T(8,128)(2,1)S(1)} %collective-permute-done.18.refs_8_), channel_id=1, source_target_pairs={{0,2},{1,3},{2,0},{3,1},{4,6},{5,7},{6,4},{7,5},{8,10},{9,11},{10,... | collective-permute-start | bytes 1179656 | tf_op jit(solution)/shard_map/ppermute | solution.py:23
  96.1 10.7 %collective-permute-start.25 = (bf16[96,2048]{1,0:T(8,128)(2,1)S(1)}, bf16[96,2048]{1,0:T(8,128)(2,1)S(1)}, u32[]{:S(2)}, u32[]{:S(2)}) collective-permute-start(bf16[96,2048]{1,0:T(8,128)(2,1)S(1)} %collective-permute-done.20.refs_2_), channel_id=1, source_target_pairs={{0,1},{1,0},{2,3},{3,2},{4,5},{5,4},{6,7},{7,6},{8,9},{9,8},{10,11... | collective-permute-start | bytes 1179656 | tf_op jit(solution)/shard_map/ppermute | solution.py:23
  96.4 11.2 %collective-permute-start.23 = (bf16[96,2048]{1,0:T(8,128)(2,1)S(1)}, bf16[96,2048]{1,0:T(8,128)(2,1)S(1)}, u32[]{:S(2)}, u32[]{:S(2)}) collective-permute-start(bf16[96,2048]{1,0:T(8,128)(2,1)S(1)} %collective-permute-done.18.refs_8_), channel_id=1, source_target_pairs={{0,16},{16,0},{1,17},{17,1},{2,18},{18,2},{3,19},{19,3},{4,20},{20... | collective-permute-start | bytes 1179656 | tf_op jit(solution)/shard_map/ppermute | solution.py:23
  97.3 25.8 %collective-permute-start.35 = (bf16[512,512]{1,0:T(8,128)(2,1)S(1)}, bf16[512,512]{1,0:T(8,128)(2,1)S(1)}, u32[]{:S(2)}, u32[]{:S(2)}) collective-permute-start(bf16[512,512]{1,0:T(8,128)(2,1)S(1)} %get-tuple-element.159), channel_id=1, source_target_pairs={{0,8},{4,12},{8,0},{12,4},{1,9},{5,13},{9,1},{13,5},{2,10},{6,14},... | collective-permute-start | bytes 1572872 | tf_op jit(solution)/shard_map/ppermute | solution.py:23
  99.5 23.6 %collective-permute-start.34 = (bf16[512,512]{1,0:T(8,128)(2,1)S(1)}, bf16[512,512]{1,0:T(8,128)(2,1)S(1)}, u32[]{:S(2)}, u32[]{:S(2)}) collective-permute-start(bf16[512,512]{1,0:T(8,128)(2,1)S(1)} %get-tuple-element.157), channel_id=1, source_target_pairs={{0,4},{4,0},{8,12},{12,8},{1,5},{5,1},{9,13},{13,9},{2,6},{6,2},{1... | collective-permute-start | bytes 1572872 | tf_op jit(solution)/shard_map/ppermute | solution.py:23
  107.6 16.9 %collective-permute-start.32 = (bf16[96,2048]{1,0:T(8,128)(2,1)S(1)}, bf16[96,2048]{1,0:T(8,128)(2,1)S(1)}, u32[]{:S(2)}, u32[]{:S(2)}) collective-permute-start(bf16[96,2048]{1,0:T(8,128)(2,1)S(1)} %collective-permute-done.23.refs_0_), channel_id=1, source_target_pairs={{0,2},{1,3},{2,0},{3,1},{4,6},{5,7},{6,4},{7,5},{8,10},{9,11},{10,... | collective-permute-start | bytes 1179656 | tf_op jit(solution)/shard_map/ppermute | solution.py:23
  123.1 12.8 %collective-permute-start.36 = (bf16[512,512]{1,0:T(8,128)(2,1)S(1)}, bf16[512,512]{1,0:T(8,128)(2,1)S(1)}, u32[]{:S(2)}, u32[]{:S(2)}) collective-permute-start(bf16[512,512]{1,0:T(8,128)(2,1)S(1)} %collective-permute-done.35.refs_4_), channel_id=1, source_target_pairs={{0,4},{4,0},{8,12},{12,8},{1,5},{5,1},{9,13},{13,9},{2,6},{6,2},{1... | collective-permute-start | bytes 1572872 | tf_op jit(solution)/shard_map/ppermute | solution.py:23
  139.2 20.0 %collective-permute-start.49 = (bf16[96,2048]{1,0:T(8,128)(2,1)S(1)}, bf16[96,2048]{1,0:T(8,128)(2,1)S(1)}, u32[]{:S(2)}, u32[]{:S(2)}) collective-permute-start(bf16[96,2048]{1,0:T(8,128)(2,1)S(1)} %get-tuple-element.202), channel_id=1, source_target_pairs={{0,1},{1,0},{2,3},{3,2},{4,5},{5,4},{6,7},{7,6},{8,9},{9,8},{10,11... | collective-permute-start | bytes 1179656 | tf_op jit(solution)/shard_map/ppermute | solution.py:23
  142.6 15.0 %collective-permute-start.38 = (bf16[96,1280]{1,0:T(8,128)(2,1)S(1)}, bf16[96,1280]{1,0:T(8,128)(2,1)S(1)}, u32[]{:S(2)}, u32[]{:S(2)}) collective-permute-start(bf16[96,1280]{1,0:T(8,128)(2,1)S(1)} %add_convert_fusion.7), channel_id=1, source_target_pairs={{0,2},{1,3},{2,0},{3,1},{4,6},{5,7},{6,4},{7,5},{8,10},{9,11},{10,... | collective-permute-start | bytes 737288 | tf_op jit(solution)/shard_map/ppermute | solution.py:23
  147.1 12.9 %collective-permute-start.51 = (bf16[96,768]{1,0:T(8,128)(2,1)S(1)}, bf16[96,768]{1,0:T(8,128)(2,1)S(1)}, u32[]{:S(2)}, u32[]{:S(2)}) collective-permute-start(bf16[96,768]{1,0:T(8,128)(2,1)S(1)} %add_convert_fusion.10), channel_id=1, source_target_pairs={{0,2},{1,3},{2,0},{3,1},{4,6},{5,7},{6,4},{7,5},{8,10},{9,11},{10,... | collective-permute-start | bytes 442376 | tf_op jit(solution)/shard_map/ppermute | solution.py:23
  147.7 12.3 %collective-permute-start.52 = (bf16[96,768]{1,0:T(8,128)(2,1)S(1)}, bf16[96,768]{1,0:T(8,128)(2,1)S(1)}, u32[]{:S(2)}, u32[]{:S(2)}) collective-permute-start(bf16[96,768]{1,0:T(8,128)(2,1)S(1)} %add_convert_fusion.9), channel_id=1, source_target_pairs={{0,16},{16,0},{1,17},{17,1},{2,18},{18,2},{3,19},{19,3},{4,20},{20... | collective-permute-start | bytes 442376 | tf_op jit(solution)/shard_map/ppermute | solution.py:23
  160.1 16.1 %collective-permute-start.56 = (bf16[96,768]{1,0:T(8,128)(2,1)S(1)}, bf16[96,768]{1,0:T(8,128)(2,1)S(1)}, u32[]{:S(2)}, u32[]{:S(2)}) collective-permute-start(bf16[96,768]{1,0:T(8,128)(2,1)S(1)} %add_convert_fusion.8), channel_id=1, source_target_pairs={{0,8},{4,12},{8,0},{12,4},{1,9},{5,13},{9,1},{13,5},{2,10},{6,14},... | collective-permute-start | bytes 442376 | tf_op jit(solution)/shard_map/ppermute | solution.py:23
  166.3 14.2 %collective-permute-start.55 = (bf16[96,1280]{1,0:T(8,128)(2,1)S(1)}, bf16[96,1280]{1,0:T(8,128)(2,1)S(1)}, u32[]{:S(2)}, u32[]{:S(2)}) collective-permute-start(bf16[96,1280]{1,0:T(8,128)(2,1)S(1)} %add_convert_fusion.4), channel_id=1, source_target_pairs={{0,8},{4,12},{8,0},{12,4},{1,9},{5,13},{9,1},{13,5},{2,10},{6,14},... | collective-permute-start | bytes 737288 | tf_op jit(solution)/shard_map/ppermute | solution.py:23
  169.4 11.0 %collective-permute-start.44 = (bf16[96,2048]{1,0:T(8,128)(2,1)S(1)}, bf16[96,2048]{1,0:T(8,128)(2,1)S(1)}, u32[]{:S(2)}, u32[]{:S(2)}) collective-permute-start(bf16[96,2048]{1,0:T(8,128)(2,1)S(1)} %get-tuple-element.196), channel_id=1, source_target_pairs={{0,1},{1,0},{2,3},{3,2},{4,5},{5,4},{6,7},{7,6},{8,9},{9,8},{10,11... | collective-permute-start | bytes 1179656 | tf_op jit(solution)/shard_map/ppermute | solution.py:23
  (48 other events, 537.7 us)
